TPU v7x, 32 devices: a whole 2x2x4 slice. The times are simulated.
32 devices in a mesh: row: 8 (over y, x, core), col: 4 (over z).
Axes of the slice: x: 2, y: 2, z: 4, core: 2. Of those that a mesh axis runs over, the one named last changes fastest.
Arguments:
- matrix: float32 [1536, 1536], P('row', 'col'), as said below
- left_panel: float32 [1536, 1024], P('row', 'col'), may hold values from -2.5 to 2.5
- right_panel: float32 [1536, 1024], P('row', 'col'), may hold values from -2.5 to 2.5
- reflectors: float32 [1536, 256], P('row', 'col'), may hold values from -0.3125 to 0.3125
Outputs:
- updated: float32 [1536, 1536], P('row', 'col')
Inputs may be any that keep to these rules, and one draw needn't show every extreme that they name: matrix is exactly skew-symmetric.
All inputs are finite; a program needn't handle non-finite values.
Results may differ from a plain program's by a relative error of at most 0.00011.
Values sent between devices are 32-bit elements; how exact they have to be, the bound alone decides.
No kernel may reach another device: no remote copies, remote signals or barrier semaphores. Data moves between devices by JAX's collectives and lax.ppermute only.
A program may use at most 128 MiB of HBM per device.

v0:
```python
import jax
import jax.numpy as jnp
from jax import lax
from jax.sharding import PartitionSpec as P


def spread(value, axis, source):
    kept = jnp.where(lax.axis_index(axis) == source, value, 0).astype(value.dtype)
    return lax.psum(kept, axis)


def product(first, second):
    return jnp.dot(
        first, second, precision=lax.Precision.HIGHEST, preferred_element_type=jnp.float32
    )


def outer_rows(first, second):
    return lax.dot_general(
        first,
        second,
        (((1,), (1,)), ((), ())),
        precision=lax.Precision.HIGHEST,
        preferred_element_type=jnp.float32,
    )


def split_parts(joined, k_share, nb_share, groups):
    rows = joined.shape[0]
    shaped = joined.reshape(rows, groups, 2 * k_share + nb_share)
    left_part = shaped[:, :, :k_share].reshape(rows, groups * k_share)
    right_part = shaped[:, :, k_share : 2 * k_share].reshape(rows, groups * k_share)
    refl_part = shaped[:, :, 2 * k_share :].reshape(rows, groups * nb_share)
    return (left_part, right_part, refl_part)


def column_rows(full_rows, col_index):
    per_column = lax.axis_size("row") // lax.axis_size("col")
    received = []
    for offset in range(per_column):
        received.append(spread(full_rows, "row", col_index * per_column + offset))
    return jnp.concatenate(received, axis=0)


def local(matrix, left_panel, right_panel, reflectors):
    col_index = lax.axis_index("col")
    groups = lax.axis_size("col")
    k_share = left_panel.shape[1]
    nb_share = reflectors.shape[1]
    joined = jnp.concatenate([left_panel, right_panel, reflectors], axis=1)
    row_joined = lax.all_gather(joined, "col", axis=1, tiled=True)
    row_left, row_right, row_refl = split_parts(row_joined, k_share, nb_share, groups)
    col_joined = column_rows(row_joined, col_index)
    col_left, col_right, col_refl = split_parts(col_joined, k_share, nb_share, groups)
    reduced = matrix - outer_rows(row_left, col_right) + outer_rows(row_right, col_left)
    image_rows = lax.psum(product(reduced, col_refl), "col")
    image_cols = column_rows(image_rows, col_index)
    return reduced + outer_rows(row_refl, image_cols) - outer_rows(image_rows, col_refl)


def solution(mesh):
    in_specs = (P("row", "col"), P("row", "col"), P("row", "col"), P("row", "col"))
    out_specs = P("row", "col")
    return jax.shard_map(local, mesh=mesh, in_specs=in_specs, out_specs=out_specs, check_vma=False)
```

profile of v0, /device:TPU:0, one launch (start us, length us, event | category | flops | bytes accessed | tf_op | source)
XLA Modules:
  0.0 253.0 jit_solution(16978762701984601350)
XLA Ops:
  6.5 0.0 all-gather.3.cloned.1.call-start
  6.5 0.9 copy.14
  7.5 1.9 maximum_bitcast_fusion
  9.3 0.0 all-gather.3.cloned.1.call-update
  9.4 0.0 all-reduce.10.cloned.1.call-start
  9.4 46.4 %all-gather.3.cloned.1.call-done = f32[4,576,192]{1,2,0:T(8,128)} async-done(((f32[1,576,192]{1,2,0:T(8,128)}), f32[4,576,192]{1,2,0:T(8,128)}) %all-gather.3.cloned.1.call-update) | async-done | bytes 1769488 | tf_op jit(solution)/shard_map/all_gather | solution.py:51
  55.8 4.1 %copy.15 = f32[4,576,192]{1,0,2:T(4,128)} copy(f32[4,576,192]{1,2,0:T(8,128)} %all-gather.3.cloned.1.call-done) | data formatting | bytes 3538944 | tf_op jit(solution)/shard_map/all_gather | solution.py:51
  59.9 2.4 reshape.21
  62.2 2.0 broadcast_select_fusion.1
  64.2 0.0 all-reduce.10.cloned.1.call-update
  64.2 0.0 all-reduce.6.cloned.1.call-start
  64.3 2.7 %reshape.16 = f32[192,4,576]{2,1,0:T(4,128)} reshape(f32[192,2304]{1,0:T(8,128)S(1)} %bitcast.25) | data formatting | bytes 3538944 | tf_op jit(solution)/shard_map/reshape | solution.py:30
  67.0 2.8 %fusion.22 = (f32[192,4,256]{2,1,0:T(4,128)}, f32[192,4,256]{2,1,0:T(4,128)}) fusion(f32[192,4,576]{2,1,0:T(4,128)} %reshape.16), kind=kLoop, calls=%fused_computation.22 | loop fusion | bytes 3145728 | tf_op jit(solution)/shard_map/slice | solution.py:32
  69.9 67.3 %all-reduce.10.cloned.1.call-done = (f32[192,2304]{1,0:T(8,128)}, f32[192,2304]{1,0:T(8,128)}) async-done(((f32[192,2304]{1,0:T(8,128)}, f32[192,2304]{1,0:T(8,128)}), (f32[192,2304]{1,0:T(8,128)}, f32[192,2304]{1,0:T(8,128)})) %all-reduce.10.cloned.1.call-update) | async-done | bytes 3538960 | tf_op jit(solution)/shard_map/psum | solution.py:9
  137.2 4.0 %pad_maximum_fusion = f32[384,2304]{1,0:T(8,128)} fusion(f32[192,2304]{1,0:T(8,128)} %get-tuple-element.7, f32[192,2304]{1,0:T(8,128)} %get-tuple-element.8), kind=kLoop, calls=%fused_computation | loop fusion | flops 884736 | bytes 7077888 | tf_op jit(solution)/shard_map/concatenate | solution.py:42
  141.2 3.3 %copy.17 = f32[384,2304]{0,1:T(8,128)S(1)} copy(f32[384,2304]{1,0:T(8,128)} %pad_maximum_fusion) | data formatting | bytes 7077888 | tf_op jit(solution)/shard_map/concatenate | solution.py:42
  144.5 0.0 copy-start.2
  144.5 0.0 copy-start
  144.6 2.9 %fusion.13 = f32[192,384]{1,0:T(8,128)S(1)} fusion(f32[192,384]{1,0:T(8,128)} %param.4, f32[384,4,576]{0,2,1:T(8,128)S(1)} %bitcast.27, f32[192,4,256]{2,1,0:T(4,128)} %get-tuple-element.10), kind=kOutput, calls=%fused_computation.10 | convolution fusion | flops 906043392 | bytes 2949120 | tf_op jit(solution)/shard_map/dot_general | solution.py:19
  147.4 0.0 copy-done.2
  147.4 1.5 fusion.10
  149.0 0.0 copy-start.3
  149.0 0.0 slice-start
  149.0 0.0 copy-done
  149.0 0.7 copy-done.3
  149.7 1.3 fusion.23
  150.9 0.0 copy-start.4
  150.9 0.0 all-reduce.6.cloned.1.call-update
  151.0 0.0 copy-start.1
  151.0 0.0 all-reduce.8.cloned.1.call-start
  151.0 35.0 %all-reduce.6.cloned.1.call-done = f32[192,256]{1,0:T(8,128)} async-done(((f32[192,256]{1,0:T(8,128)}), f32[192,256]{1,0:T(8,128)}) %all-reduce.6.cloned.1.call-update) | async-done | bytes 196624 | tf_op jit(solution)/shard_map/psum | solution.py:56
  186.0 0.0 copy-start.5
  186.0 1.8 broadcast_select_fusion.3
  187.8 0.0 all-reduce.8.cloned.1.call-update
  187.8 0.0 slice-done
  187.8 0.2 copy.21
  188.0 55.2 %all-reduce.8.cloned.1.call-done = (f32[192,256]{1,0:T(8,128)}, f32[192,256]{1,0:T(8,128)}) async-done(((f32[192,256]{1,0:T(8,128)}, f32[192,256]{1,0:T(8,128)}), (f32[192,256]{1,0:T(8,128)}, f32[192,256]{1,0:T(8,128)})) %all-reduce.8.cloned.1.call-update) | async-done | bytes 393232 | tf_op jit(solution)/shard_map/psum | solution.py:9
  243.2 0.0 copy-done.4
  243.2 2.0 convolution_add_fusion
  245.2 0.0 copy-done.1
  245.2 0.0 copy-done.5
  245.2 1.2 convolution_subtract_fusion
  (1 shorter events, 0.0 us)
Async XLA Ops:
  6.5 49.2 %all-gather.3.cloned.1.call-start = ((), (), s32[]{:S(2)}) async-start(), calls=%async_computation.1 | async-start | bytes 2457600 | tf_op jit(solution)/shard_map/all_gather | solution.py:51
  9.4 127.8 %all-reduce.10.cloned.1.call-start = ((), (), s32[]{:S(2)}) async-start(), calls=%async_computation.3 | async-start | bytes 7077888 | tf_op jit(solution)/shard_map/psum | solution.py:9
  64.2 121.7 %all-reduce.6.cloned.1.call-start = ((), (), s32[]{:S(2)}) async-start(), calls=%async_computation | async-start | bytes 393216 | tf_op jit(solution)/shard_map/psum | solution.py:56
  144.5 2.9 %copy-start.2 = (f32[192,4,256]{2,1,0:T(4,128)S(1)}, f32[192,4,256]{2,1,0:T(4,128)}, u32[]{:S(2)}) copy-start(f32[192,4,256]{2,1,0:T(4,128)} %get-tuple-element.9) | copy-start | bytes 2359300
  144.5 4.5 %copy-start = (f32[384,4,64]{0,2,1:T(8,128)}, f32[384,4,64]{0,2,1:T(8,128)S(1)}, u32[]{:S(2)}) copy-start(f32[384,4,64]{0,2,1:T(8,128)S(1)} %slice.29) | copy-start | bytes 1179652
  149.0 0.7 copy-start.3
  149.0 38.8 %slice-start = ((f32[192,4,576]{2,1,0:T(4,128)}), f32[192,4,64]{2,1,0:T(4,128)S(1)}, s32[]{:S(2)}) async-start(f32[192,4,576]{2,1,0:T(4,128)} %reshape.16), calls=%async_computation.4 | async-start | bytes 786432 | tf_op jit(solution)/shard_map/slice | solution.py:33
  150.9 92.3 %copy-start.4 = (f32[192,384]{1,0:T(8,128)S(1)}, f32[192,384]{1,0:T(8,128)}, u32[]{:S(2)}) copy-start(f32[192,384]{1,0:T(8,128)} %copy-done.3) | copy-start | bytes 884740
  151.0 94.3 %copy-start.1 = (f32[384,4,64]{0,2,1:T(8,128)S(1)}, f32[384,4,64]{0,2,1:T(8,128)}, u32[]{:S(2)}) copy-start(f32[384,4,64]{0,2,1:T(8,128)} %copy-done) | copy-start | bytes 1179652
  151.0 92.2 %all-reduce.8.cloned.1.call-start = ((), (), s32[]{:S(2)}) async-start(), calls=%async_computation.2 | async-start | bytes 786432 | tf_op jit(solution)/shard_map/psum | solution.py:9
  186.0 59.3 %copy-start.5 = (f32[192,256]{1,0:T(8,128)S(1)}, f32[192,256]{1,0:T(8,128)}, u32[]{:S(2)}) copy-start(f32[192,256]{1,0:T(8,128)} %all-reduce.6.cloned.1.call-done) | copy-start | bytes 589828
Sparse Core Ops, SparseCore 0:
  9.5 46.2 all-gather.2
  64.4 72.7 all-reduce.9
  151.1 34.8 all-reduce.5
  189.2 53.9 all-reduce.7
where the time goes:
time: 253 us
  waiting for transfers between devices  204 us (81%)
  local copies, waits for them, and re-layouts  17.2 us (7%)
  between operations  13.3 us (5%)
  other arithmetic  9.65 us (4%)
  matrix products  8.88 us (4%)
    psum x2, waiting for transfers between devices, spread(): return lax.psum(kept, axis)  123 us
    all_gather x1, waiting for transfers between devices, local(): row_joined = lax.all_gather(joined, 'col', axis=1, tiled=True)  46.4 us
    psum x1, waiting for transfers between devices, local(): image_rows = lax.psum(product(reduced, col_refl), 'col')  35 us
    dot_general x4, matrix products, outer_rows(): lax.dot_general(first, second, (((1,), (1,)), ((), ())), precision=lax.Pr...  7.63 us
  transfers between devices with their start and end apart: 4, of which 4 were waited for; matrix products, arithmetic and copies ran while one was open for 2% of the time, Pallas kernels for 0%

commit v1 on v0

v1 whole, which is shorter than its diff:
```python
import jax
import jax.numpy as jnp
from jax import lax
from jax.sharding import PartitionSpec as P


def dot(first, second, dims):
    return lax.dot_general(
        first,
        second,
        (dims, ((), ())),
        precision=lax.Precision.HIGH,
        preferred_element_type=jnp.float32,
    )


def swap(value, axis, offset):
    size = lax.axis_size(axis)
    return lax.ppermute(value, axis, [(i, i ^ offset) for i in range(size)])


def gather_rows(value, rows):
    own = {0: value}
    for chip in range(2, rows, 2):
        own[chip] = swap(value, "row", chip)
    blocks = []
    for chip in range(0, rows, 2):
        blocks += [own[chip], swap(own[chip], "row", 1)]
    return jnp.concatenate(blocks, axis=0)


def sum_rows(value, rows):
    core = lax.axis_index("row") % 2
    half = value.shape[0] // 2
    kept = lax.dynamic_slice_in_dim(value, core * half, half, 0)
    given = lax.dynamic_slice_in_dim(value, (1 - core) * half, half, 0)
    total = kept + swap(given, "row", 1)
    bit = 2
    while bit < rows:
        total = total + swap(total, "row", bit)
        bit *= 2
    other = swap(total, "row", 1)
    first = jnp.where(core == 0, total, other)
    second = jnp.where(core == 0, other, total)
    return jnp.concatenate([first, second], axis=0)


def order_blocks(value, per, first):
    width = value.shape[1] // per
    bit = 1
    while bit < per:
        parts = [value[:, t * width : (t + 1) * width] for t in range(per)]
        moved = jnp.concatenate([parts[t ^ bit] for t in range(per)], axis=1)
        value = jnp.where((first // bit) % 2 == 1, moved, value)
        bit *= 2
    return value


def local(matrix, left_panel, right_panel, reflectors):
    rows, cols = lax.axis_size("row"), lax.axis_size("col")
    per = rows // cols
    row, col = lax.axis_index("row"), lax.axis_index("col")
    height, share = left_panel.shape
    wide = per * height

    own_refl = jnp.concatenate(
        [reflectors] + [swap(reflectors, "col", k) for k in range(1, cols)], axis=1
    )
    panels = jnp.concatenate([left_panel, right_panel], axis=1)
    all_panels = gather_rows(panels, rows)
    all_refl = gather_rows(own_refl, rows)

    def start(offset):
        return ((row // per) ^ col ^ offset) * wide

    along = ((1,), (1,))
    over = ((1,), (0,))
    mixed = dot(all_panels, all_refl, ((0,), (0,)))
    mixed_left, mixed_right = mixed[:share], mixed[share:]
    mine = order_blocks(matrix, per, row % per)
    col_refl = lax.dynamic_slice_in_dim(all_refl, start(0), wide, 0)
    image = (
        dot(right_panel, mixed_left, over)
        - dot(left_panel, mixed_right, over)
        + dot(mine, col_refl, over)
    )
    factors = jnp.concatenate(
        [
            right_panel - dot(own_refl, mixed_right, along),
            dot(own_refl, mixed_left, along) - left_panel,
            -image,
        ],
        axis=1,
    )
    whole = jnp.concatenate([all_panels, all_refl], axis=1)

    def block(offset):
        return dot(factors, lax.dynamic_slice_in_dim(whole, start(offset), wide, 0), along)

    total = block(0)
    for k in range(1, cols):
        total = total + swap(block(k), "col", k)
    sides = sum_rows(dot(own_refl, matrix, ((0,), (0,))), rows)
    return order_blocks(total, per, row % per) + (matrix - dot(own_refl, sides, over))


def solution(mesh):
    spec = P("row", "col")
    return jax.shard_map(
        local, mesh=mesh, in_specs=(spec,) * 4, out_specs=spec, check_vma=False
    )
```

time: 253 us -> 110 us (0.43)
  waiting for transfers between devices: 204 us -> 52.1 us
  starting transfers between devices: 0.13 us -> 21 us
  between operations: 13.3 us -> 0.33 us
  other arithmetic: 9.65 us -> 4.67 us
  local copies, waits for them, and re-layouts: 17.2 us -> 21.4 us
    psum x3 -> x0, waiting for transfers between devices: 157 us -> none  [the longest x2 123 us: spread(): return lax.psum(kept, axis)]
    ppermute x0 -> x24, waiting for transfers between devices: none -> 52.1 us  [swap(): return lax.ppermute(value, axis, [(i, i ^ offset) for i in range(size)])]
    all_gather x1 -> x0, waiting for transfers between devices: 46.4 us -> none  [local(): row_joined = lax.all_gather(joined, 'col', axis=1, tiled=True)]
    ppermute x0 -> x24, starting transfers between devices: none -> 21 us  [swap(): return lax.ppermute(value, axis, [(i, i ^ offset) for i in range(size)])]
    unnamed x14 -> x38, local copies, waits for them, and re-layouts: 4 us -> 10.3 us
    concatenate x1 -> x5, local copies, waits for them, and re-layouts: 3.3 us -> 8.43 us  [the longest x3 6.76 us: gather_rows(): return jnp.concatenate(blocks, axis=0)]
    add x0 -> x4, other arithmetic: none -> 4.64 us  [the longest x2 2.88 us: sum_rows(): total = total + swap(total, 'row', bit)]
    all_gather x1 -> x0, local copies, waits for them, and re-layouts: 4.08 us -> none  [local(): row_joined = lax.all_gather(joined, 'col', axis=1, tiled=True)]
  transfers between devices with their start and end apart: 4 -> 24, of which waited for: 4 -> 8; matrix products, arithmetic and copies ran while one was open for 2% -> 28% of each run, Pallas kernels for 0% -> 0%
where the time goes in v1:
time: 110 us; the launch traced here: 109 us
  waiting for transfers between devices  52.1 us (47%)
  local copies, waits for them, and re-layouts  21.4 us (19%)
  starting transfers between devices  21 us (19%)
  matrix products  9.64 us (9%)
  other arithmetic  4.67 us (4%)
    ppermute x24, waiting for transfers between devices, swap(): return lax.ppermute(value, axis, [(i, i ^ offset) for i in range(size)])  52.1 us
    ppermute x24, starting transfers between devices, swap(): return lax.ppermute(value, axis, [(i, i ^ offset) for i in range(size)])  21 us
    unnamed x38, local copies, waits for them, and re-layouts  10.3 us
    dot_general x12, matrix products, dot(): lax.dot_general(first, second, (dims, ((), ())), precision=lax.Precision....  9.64 us
    concatenate x3, local copies, waits for them, and re-layouts, gather_rows(): return jnp.concatenate(blocks, axis=0)  6.76 us
    add x2, other arithmetic, sum_rows(): total = total + swap(total, 'row', bit)  2.88 us
  transfers between devices with their start and end apart: 24, of which 8 were waited for; matrix products, arithmetic and copies ran while one was open for 28% of the time, Pallas kernels for 0%

profile of v1, /device:TPU:0, one launch (start us, length us, event | category | flops | bytes accessed | tf_op | source)
XLA Modules:
  0.0 109.1 jit_solution(2578371346214048225)
XLA Ops:
  0.0 3.0 %collective-permute-start = (f32[192,64]{0,1:T(8,128)}, f32[192,64]{0,1:T(8,128)S(1)}, u32[]{:S(2)}, u32[]{:S(2)}) collective-permute-start(f32[192,64]{0,1:T(8,128)} %param.7), channel_id=1, source_target_pairs={{0,1},{1,0},{2,3},{3,2},{4,5},{5,4},{6,7},{7,6},{8,9},{9,8},{10,11... | collective-permute-start | bytes 147464 | tf_op jit(solution)/shard_map/ppermute | solution.py:19
  3.0 2.6 %collective-permute-start.1 = (f32[192,64]{0,1:T(8,128)}, f32[192,64]{0,1:T(8,128)S(1)}, u32[]{:S(2)}, u32[]{:S(2)}) collective-permute-start(f32[192,64]{0,1:T(8,128)} %param.7), channel_id=1, source_target_pairs={{0,2},{1,3},{2,0},{3,1},{4,6},{5,7},{6,4},{7,5},{8,10},{9,11},{10,... | collective-permute-start | bytes 147464 | tf_op jit(solution)/shard_map/ppermute | solution.py:19
  5.6 0.9 constant_dynamic-update-slice_fusion.3
  6.5 4.0 %collective-permute-done.1 = f32[192,64]{0,1:T(8,128)S(1)} collective-permute-done((f32[192,64]{0,1:T(8,128)}, f32[192,64]{0,1:T(8,128)S(1)}, u32[]{:S(2)}, u32[]{:S(2)}) %collective-permute-start.1) | collective-permute-done | bytes 49184 | tf_op jit(solution)/shard_map/ppermute | solution.py:19
  10.5 1.4 %collective-permute-done.2 = f32[192,64]{0,1:T(8,128)S(1)} collective-permute-done((f32[192,64]{0,1:T(8,128)}, f32[192,64]{0,1:T(8,128)S(1)}, u32[]{:S(2)}, u32[]{:S(2)}) %collective-permute-start.2) | collective-permute-done | bytes 49184 | tf_op jit(solution)/shard_map/ppermute | solution.py:19
  11.9 1.3 %fusion.46 = f32[256,384]{1,0:T(8,128)S(1)} fusion(f32[192,256]{0,1:T(8,128)S(1)} %constant_dynamic-update-slice_fusion, f32[192,384]{1,0:T(8,128)} %param.4), kind=kOutput, calls=%fused_computation.74 | convolution fusion | flops 113246208 | bytes 884736 | tf_op jit(solution)/shard_map/dot_general | solution.py:8
  13.3 0.8 constant_dynamic-slice_fusion
  14.1 1.7 %constant_dynamic-update-slice_fusion.5 = (f32[192,512]{1,0:T(8,128)}, f32[1536,512]{1,0:T(8,128)S(1)}) fusion(f32[192,256]{1,0:T(8,128)} %param.5), kind=kLoop, calls=%fused_computation.49 | loop fusion | bytes 589824
  15.8 1.7 %constant_dynamic-update-slice_fusion.4 = (f32[192,512]{1,0:T(8,128)}, f32[1536,512]{1,0:T(8,128)S(1)}) fusion(f32[192,512]{1,0:T(8,128)} %get-tuple-element.13, f32[192,256]{1,0:T(8,128)} %param.6, f32[1536,512]{1,0:T(8,128)S(1)} %get-tuple-element.14), kind=kLoop, calls=%fused_computation.48 | loop fusion | bytes 589824 | tf_op jit(solution)/shard_map/concatenate | solution.py:69
  17.5 1.5 %collective-permute-start.4 = (f32[192,512]{1,0:T(8,128)}, f32[192,512]{1,0:T(8,128)}, u32[]{:S(2)}, u32[]{:S(2)}) collective-permute-start(f32[192,512]{1,0:T(8,128)} %get-tuple-element.11), channel_id=1, source_target_pairs={{0,8},{4,12},{8,0},{12,4},{16,24},{20,28},{24,16},{28,20},{1,9},{5... | collective-permute-start | bytes 1179656 | tf_op jit(solution)/shard_map/ppermute | solution.py:19
  19.2 0.5 collective-permute-start.11
  19.7 1.5 %collective-permute-start.13 = (f32[192,256]{0,1:T(8,128)S(1)}, f32[192,256]{0,1:T(8,128)S(1)}, u32[]{:S(2)}, u32[]{:S(2)}) collective-permute-start(f32[192,256]{0,1:T(8,128)S(1)} %constant_dynamic-update-slice_fusion), channel_id=1, source_target_pairs={{0,16},{4,20},{8,24},{12,28},{16,0},{20,4},{24,8},{28,12},{1,17},{... | collective-permute-start | bytes 589832 | tf_op jit(solution)/shard_map/ppermute | solution.py:19
  21.2 1.4 %collective-permute-start.15 = (f32[192,256]{0,1:T(8,128)S(1)}, f32[192,256]{0,1:T(8,128)S(1)}, u32[]{:S(2)}, u32[]{:S(2)}) collective-permute-start(f32[192,256]{0,1:T(8,128)S(1)} %constant_dynamic-update-slice_fusion), channel_id=1, source_target_pairs={{0,24},{4,28},{8,16},{12,20},{16,8},{20,12},{24,0},{28,4},{1,25},{... | collective-permute-start | bytes 589832 | tf_op jit(solution)/shard_map/ppermute | solution.py:19
  22.7 1.7 %dynamic-slice_add_fusion = f32[128,384]{1,0:T(8,128)} fusion(f32[128,384]{1,0:T(8,128)} %collective-permute-done.20, f32[256,384]{1,0:T(8,128)} %copy-done.5, s32[]{:T(128)S(6)} %select_n.81), kind=kLoop, calls=%fused_computation.40 | loop fusion | flops 49152 | bytes 589828 | tf_op jit(solution)/shard_map/add | solution.py:37
  24.4 0.5 collective-permute-start.21
  24.9 10.3 %collective-permute-done.11 = f32[192,256]{0,1:T(8,128)S(1)} collective-permute-done((f32[192,256]{0,1:T(8,128)S(1)}, f32[192,256]{0,1:T(8,128)S(1)}, u32[]{:S(2)}, u32[]{:S(2)}) %collective-permute-start.11) | collective-permute-done | bytes 196640 | tf_op jit(solution)/shard_map/ppermute | solution.py:19
  35.2 1.6 %collective-permute-start.6 = (f32[192,512]{1,0:T(8,128)}, f32[192,512]{1,0:T(8,128)}, u32[]{:S(2)}, u32[]{:S(2)}) collective-permute-start(f32[192,512]{1,0:T(8,128)} %get-tuple-element.11), channel_id=1, source_target_pairs={{0,16},{4,20},{8,24},{12,28},{16,0},{20,4},{24,8},{28,12},{1,17},{... | collective-permute-start | bytes 1179656 | tf_op jit(solution)/shard_map/ppermute | solution.py:19
  36.8 5.0 %collective-permute-done.15 = f32[192,256]{0,1:T(8,128)S(1)} collective-permute-done((f32[192,256]{0,1:T(8,128)S(1)}, f32[192,256]{0,1:T(8,128)S(1)}, u32[]{:S(2)}, u32[]{:S(2)}) %collective-permute-start.15) | collective-permute-done | bytes 196640 | tf_op jit(solution)/shard_map/ppermute | solution.py:19
  41.8 0.7 copy-done.11
  42.5 1.4 %collective-permute-start.8 = (f32[192,512]{1,0:T(8,128)}, f32[192,512]{1,0:T(8,128)}, u32[]{:S(2)}, u32[]{:S(2)}) collective-permute-start(f32[192,512]{1,0:T(8,128)} %get-tuple-element.11), channel_id=1, source_target_pairs={{0,24},{4,28},{8,16},{12,20},{16,8},{20,12},{24,0},{28,4},{1,25},{... | collective-permute-start | bytes 1179656 | tf_op jit(solution)/shard_map/ppermute | solution.py:19
  43.9 0.8 collective-permute-done.21
  44.8 1.8 %fusion.44 = (f32[192,192]{1,0:T(8,128)}, f32[192,192]{1,0:T(8,128)}) fusion(f32[192,384]{1,0:T(8,128)} %param.4), kind=kLoop, calls=%fused_computation.72 | loop fusion | bytes 589824 | tf_op jit(solution)/shard_map/slice | solution.py:52
  46.6 1.7 %add.68 = f32[128,384]{1,0:T(8,128)} add(f32[128,384]{1,0:T(8,128)} %dynamic-slice_add_fusion, f32[128,384]{1,0:T(8,128)} %collective-permute-done.21) | non-fusion elementwise | flops 49152 | bytes 589824 | tf_op jit(solution)/shard_map/add | solution.py:40
  48.3 0.5 collective-permute-start.14
  48.8 9.5 %collective-permute-done.6 = f32[192,512]{1,0:T(8,128)} collective-permute-done((f32[192,512]{1,0:T(8,128)}, f32[192,512]{1,0:T(8,128)}, u32[]{:S(2)}, u32[]{:S(2)}) %collective-permute-start.6) | collective-permute-done | bytes 393248 | tf_op jit(solution)/shard_map/ppermute | solution.py:19
  58.9 0.5 collective-permute-start.22
  59.4 1.0 constant_dynamic-update-slice_fusion.12
  60.4 1.0 constant_dynamic-update-slice_fusion.11
  61.5 0.7 copy-done.13
  62.2 2.6 %concatenate.30 = f32[1536,256]{0,1:T(8,128)} concatenate(f32[192,256]{0,1:T(8,128)S(1)} %constant_dynamic-update-slice_fusion, f32[192,256]{0,1:T(8,128)} %copy-done.8, f32[192,256]{0,1:T(8,128)} %copy-done.9, f32[192,256]{0,1:T(8,128)} %copy-done.12, f32[192,256]{0,1:T(8,128)} %copy-done.10, f32[192,256]{0,1:T(8,128)} %copy-done.13, f32[192,256]{0,1:T(8,128)} %copy-done.11, ...), dimensions={0} | concatenate | bytes 3145728 | tf_op jit(solution)/shard_map/concatenate | solution.py:29
  64.8 3.0 %copy.5 = f32[1536,256]{1,0:T(8,128)} copy(f32[1536,256]{0,1:T(8,128)} %concatenate.30) | data formatting | bytes 3145728 | tf_op jit(solution)/shard_map/concatenate | solution.py:29
  67.9 1.2 %add.69 = f32[128,384]{1,0:T(8,128)S(1)} add(f32[128,384]{1,0:T(8,128)} %add.68, f32[128,384]{1,0:T(8,128)} %collective-permute-done.22) | non-fusion elementwise | flops 49152 | bytes 589824 | tf_op jit(solution)/shard_map/add | solution.py:40
  69.0 0.6 collective-permute-start.23
  69.6 1.0 constant_dynamic-update-slice_fusion.10
  70.6 1.0 constant_dynamic-update-slice_fusion.9
  71.7 1.0 constant_dynamic-update-slice_fusion.8
  72.7 1.0 constant_dynamic-update-slice_fusion.7
  73.7 1.1 constant_dynamic-update-slice_fusion.6
  74.9 2.7 %fusion.45 = f32[512,256]{1,0:T(8,128)S(1)} fusion(f32[1536,512]{1,0:T(8,128)S(1)} %constant_dynamic-update-slice_fusion.6, f32[1536,256]{0,1:T(8,128)S(1)} %copy-done.1), kind=kOutput, calls=%fused_computation.73 | convolution fusion | flops 1207959552 | bytes 5242880 | tf_op jit(solution)/shard_map/dot_general | solution.py:8
  79.3 0.7 fusion.1
  80.0 1.9 %collective-permute-start.19 = (f32[192,384]{1,0:T(8,128)S(1)}, f32[192,384]{1,0:T(8,128)S(1)}, u32[]{:S(2)}, u32[]{:S(2)}) collective-permute-start(f32[192,384]{1,0:T(8,128)S(1)} %fusion.1), channel_id=1, source_target_pairs={{0,3},{1,2},{2,1},{3,0},{4,7},{5,6},{6,5},{7,4},{8,11},{9,10},{10,... | collective-permute-start | bytes 884744 | tf_op jit(solution)/shard_map/ppermute | solution.py:19
  81.9 0.7 fusion.7
  83.0 0.7 fusion.10
  83.7 2.3 %collective-permute-start.18 = (f32[192,384]{1,0:T(8,128)S(1)}, f32[192,384]{1,0:T(8,128)S(1)}, u32[]{:S(2)}, u32[]{:S(2)}) collective-permute-start(f32[192,384]{1,0:T(8,128)S(1)} %fusion.10), channel_id=1, source_target_pairs={{0,2},{1,3},{2,0},{3,1},{4,6},{5,7},{6,4},{7,5},{8,10},{9,11},{10,... | collective-permute-start | bytes 884744 | tf_op jit(solution)/shard_map/ppermute | solution.py:19
  86.1 13.3 %collective-permute-done.17 = f32[192,384]{1,0:T(8,128)S(1)} collective-permute-done((f32[192,384]{1,0:T(8,128)S(1)}, f32[192,384]{1,0:T(8,128)S(1)}, u32[]{:S(2)}, u32[]{:S(2)}) %collective-permute-start.17) | collective-permute-done | bytes 294944 | tf_op jit(solution)/shard_map/ppermute | solution.py:19
  99.4 0.7 fusion.12
  100.1 7.7 %collective-permute-done.18 = f32[192,384]{1,0:T(8,128)S(1)} collective-permute-done((f32[192,384]{1,0:T(8,128)S(1)}, f32[192,384]{1,0:T(8,128)S(1)}, u32[]{:S(2)}, u32[]{:S(2)}) %collective-permute-start.18) | collective-permute-done | bytes 294944 | tf_op jit(solution)/shard_map/ppermute | solution.py:19
  108.0 1.2 %fusion.23 = f32[192,384]{1,0:T(8,128)} fusion(f32[192,384]{1,0:T(8,128)S(1)} %add_add_fusion, f32[192,192]{1,0:T(8,128)S(1)} %get-tuple-element.8, f32[192,192]{1,0:T(8,128)S(1)} %get-tuple-element.7, pred[]{:T(512)S(6)} %eq.14, f32[192,384]{1,0:T(8,128)S(1)} %copy-done.2, f32[192,256]{0,1:T(8,128)S(1)} %constant_dynamic-update-slice_fusion, ...), kind=kOutput, calls=%fused_computation.33 | convolution fusion | flops 113639424 | bytes 1769473 | tf_op jit(solution)/shard_map/dot_general | solution.py:8
  (63 shorter events, 3.2 us)
Async XLA Ops:
  0.0 6.5 %collective-permute-start = (f32[192,64]{0,1:T(8,128)}, f32[192,64]{0,1:T(8,128)S(1)}, u32[]{:S(2)}, u32[]{:S(2)}) collective-permute-start(f32[192,64]{0,1:T(8,128)} %param.7), channel_id=1, source_target_pairs={{0,1},{1,0},{2,3},{3,2},{4,5},{5,4},{6,7},{7,6},{8,9},{9,8},{10,11... | collective-permute-start | bytes 147464 | tf_op jit(solution)/shard_map/ppermute | solution.py:19
  3.0 7.5 %collective-permute-start.1 = (f32[192,64]{0,1:T(8,128)}, f32[192,64]{0,1:T(8,128)S(1)}, u32[]{:S(2)}, u32[]{:S(2)}) collective-permute-start(f32[192,64]{0,1:T(8,128)} %param.7), channel_id=1, source_target_pairs={{0,2},{1,3},{2,0},{3,1},{4,6},{5,7},{6,4},{7,5},{8,10},{9,11},{10,... | collective-permute-start | bytes 147464 | tf_op jit(solution)/shard_map/ppermute | solution.py:19
  5.6 6.3 %collective-permute-start.2 = (f32[192,64]{0,1:T(8,128)}, f32[192,64]{0,1:T(8,128)S(1)}, u32[]{:S(2)}, u32[]{:S(2)}) collective-permute-start(f32[192,64]{0,1:T(8,128)} %param.7), channel_id=1, source_target_pairs={{0,3},{1,2},{2,1},{3,0},{4,7},{5,6},{6,5},{7,4},{8,11},{9,10},{10,... | collective-permute-start | bytes 147464 | tf_op jit(solution)/shard_map/ppermute | solution.py:19
  13.3 0.8 copy-start.5
  14.1 7.1 %collective-permute-start.20 = (f32[128,384]{1,0:T(8,128)}, f32[128,384]{1,0:T(8,128)}, u32[]{:S(2)}, u32[]{:S(2)}) collective-permute-start(f32[128,384]{1,0:T(8,128)} %constant_dynamic-slice_fusion), channel_id=1, source_target_pairs={{0,4},{4,0},{8,12},{12,8},{16,20},{20,16},{24,28},{28,24},{1,5},{5... | collective-permute-start | bytes 589832 | tf_op jit(solution)/shard_map/ppermute | solution.py:19
  17.5 26.5 %collective-permute-start.4 = (f32[192,512]{1,0:T(8,128)}, f32[192,512]{1,0:T(8,128)}, u32[]{:S(2)}, u32[]{:S(2)}) collective-permute-start(f32[192,512]{1,0:T(8,128)} %get-tuple-element.11), channel_id=1, source_target_pairs={{0,8},{4,12},{8,0},{12,4},{16,24},{20,28},{24,16},{28,20},{1,9},{5... | collective-permute-start | bytes 1179656 | tf_op jit(solution)/shard_map/ppermute | solution.py:19
  18.9 5.4 %collective-permute-start.10 = (f32[192,256]{0,1:T(8,128)S(1)}, f32[192,256]{0,1:T(8,128)S(1)}, u32[]{:S(2)}, u32[]{:S(2)}) collective-permute-start(f32[192,256]{0,1:T(8,128)S(1)} %constant_dynamic-update-slice_fusion), channel_id=1, source_target_pairs={{0,4},{4,0},{8,12},{12,8},{16,20},{20,16},{24,28},{28,24},{1,5},{5... | collective-permute-start | bytes 589832 | tf_op jit(solution)/shard_map/ppermute | solution.py:19
  19.2 16.0 %collective-permute-start.11 = (f32[192,256]{0,1:T(8,128)S(1)}, f32[192,256]{0,1:T(8,128)S(1)}, u32[]{:S(2)}, u32[]{:S(2)}) collective-permute-start(f32[192,256]{0,1:T(8,128)S(1)} %constant_dynamic-update-slice_fusion), channel_id=1, source_target_pairs={{0,8},{4,12},{8,0},{12,4},{16,24},{20,28},{24,16},{28,20},{1,9},{5... | collective-permute-start | bytes 589832 | tf_op jit(solution)/shard_map/ppermute | solution.py:19
  19.7 15.5 %collective-permute-start.13 = (f32[192,256]{0,1:T(8,128)S(1)}, f32[192,256]{0,1:T(8,128)S(1)}, u32[]{:S(2)}, u32[]{:S(2)}) collective-permute-start(f32[192,256]{0,1:T(8,128)S(1)} %constant_dynamic-update-slice_fusion), channel_id=1, source_target_pairs={{0,16},{4,20},{8,24},{12,28},{16,0},{20,4},{24,8},{28,12},{1,17},{... | collective-permute-start | bytes 589832 | tf_op jit(solution)/shard_map/ppermute | solution.py:19
  21.2 20.6 %collective-permute-start.15 = (f32[192,256]{0,1:T(8,128)S(1)}, f32[192,256]{0,1:T(8,128)S(1)}, u32[]{:S(2)}, u32[]{:S(2)}) collective-permute-start(f32[192,256]{0,1:T(8,128)S(1)} %constant_dynamic-update-slice_fusion), channel_id=1, source_target_pairs={{0,24},{4,28},{8,16},{12,20},{16,8},{20,12},{24,0},{28,4},{1,25},{... | collective-permute-start | bytes 589832 | tf_op jit(solution)/shard_map/ppermute | solution.py:19
  24.4 17.4 %copy-start.8 = (f32[192,256]{0,1:T(8,128)}, f32[192,256]{0,1:T(8,128)S(1)}, u32[]{:S(2)}) copy-start(f32[192,256]{0,1:T(8,128)S(1)} %collective-permute-done.10) | copy-start | bytes 589828
  24.4 20.4 %collective-permute-start.21 = (f32[128,384]{1,0:T(8,128)}, f32[128,384]{1,0:T(8,128)}, u32[]{:S(2)}, u32[]{:S(2)}) collective-permute-start(f32[128,384]{1,0:T(8,128)} %dynamic-slice_add_fusion), channel_id=1, source_target_pairs={{0,8},{4,12},{8,0},{12,4},{16,24},{20,28},{24,16},{28,20},{1,9},{5... | collective-permute-start | bytes 589832 | tf_op jit(solution)/shard_map/ppermute | solution.py:19
  35.2 6.6 %copy-start.9 = (f32[192,256]{0,1:T(8,128)}, f32[192,256]{0,1:T(8,128)S(1)}, u32[]{:S(2)}) copy-start(f32[192,256]{0,1:T(8,128)S(1)} %collective-permute-done.11) | copy-start | bytes 589828
  35.2 13.1 %collective-permute-start.3 = (f32[192,512]{1,0:T(8,128)}, f32[192,512]{1,0:T(8,128)}, u32[]{:S(2)}, u32[]{:S(2)}) collective-permute-start(f32[192,512]{1,0:T(8,128)} %get-tuple-element.11), channel_id=1, source_target_pairs={{0,4},{4,0},{8,12},{12,8},{16,20},{20,16},{24,28},{28,24},{1,5},{5... | collective-permute-start | bytes 1179656 | tf_op jit(solution)/shard_map/ppermute | solution.py:19
  35.2 6.6 %copy-start.10 = (f32[192,256]{0,1:T(8,128)}, f32[192,256]{0,1:T(8,128)S(1)}, u32[]{:S(2)}) copy-start(f32[192,256]{0,1:T(8,128)S(1)} %collective-permute-done.13) | copy-start | bytes 589828
  35.2 23.1 %collective-permute-start.6 = (f32[192,512]{1,0:T(8,128)}, f32[192,512]{1,0:T(8,128)}, u32[]{:S(2)}, u32[]{:S(2)}) collective-permute-start(f32[192,512]{1,0:T(8,128)} %get-tuple-element.11), channel_id=1, source_target_pairs={{0,16},{4,20},{8,24},{12,28},{16,0},{20,4},{24,8},{28,12},{1,17},{... | collective-permute-start | bytes 1179656 | tf_op jit(solution)/shard_map/ppermute | solution.py:19
  41.8 0.7 copy-start.11
  42.5 15.9 %collective-permute-start.8 = (f32[192,512]{1,0:T(8,128)}, f32[192,512]{1,0:T(8,128)}, u32[]{:S(2)}, u32[]{:S(2)}) collective-permute-start(f32[192,512]{1,0:T(8,128)} %get-tuple-element.11), channel_id=1, source_target_pairs={{0,24},{4,28},{8,16},{12,20},{16,8},{20,12},{24,0},{28,4},{1,25},{... | collective-permute-start | bytes 1179656 | tf_op jit(solution)/shard_map/ppermute | solution.py:19
  43.9 14.9 %collective-permute-start.12 = (f32[192,256]{0,1:T(8,128)}, f32[192,256]{0,1:T(8,128)S(1)}, u32[]{:S(2)}, u32[]{:S(2)}) collective-permute-start(f32[192,256]{0,1:T(8,128)} %copy-done.9), channel_id=1, source_target_pairs={{0,4},{4,0},{8,12},{12,8},{16,20},{20,16},{24,28},{28,24},{1,5},{5... | collective-permute-start | bytes 589832 | tf_op jit(solution)/shard_map/ppermute | solution.py:19
  44.8 24.8 %collective-permute-start.5 = (f32[192,512]{1,0:T(8,128)}, f32[192,512]{1,0:T(8,128)}, u32[]{:S(2)}, u32[]{:S(2)}) collective-permute-start(f32[192,512]{1,0:T(8,128)} %collective-permute-done.4), channel_id=1, source_target_pairs={{0,4},{4,0},{8,12},{12,8},{16,20},{20,16},{24,28},{28,24},{1,5},{5... | collective-permute-start | bytes 1179656 | tf_op jit(solution)/shard_map/ppermute | solution.py:19
  48.3 13.1 %collective-permute-start.14 = (f32[192,256]{0,1:T(8,128)}, f32[192,256]{0,1:T(8,128)S(1)}, u32[]{:S(2)}, u32[]{:S(2)}) collective-permute-start(f32[192,256]{0,1:T(8,128)} %copy-done.10), channel_id=1, source_target_pairs={{0,4},{4,0},{8,12},{12,8},{16,20},{20,16},{24,28},{28,24},{1,5},{5... | collective-permute-start | bytes 589832 | tf_op jit(solution)/shard_map/ppermute | solution.py:19
  58.3 3.8 %collective-permute-start.16 = (f32[192,256]{0,1:T(8,128)}, f32[192,256]{0,1:T(8,128)}, u32[]{:S(2)}, u32[]{:S(2)}) collective-permute-start(f32[192,256]{0,1:T(8,128)} %copy-done.11), channel_id=1, source_target_pairs={{0,4},{4,0},{8,12},{12,8},{16,20},{20,16},{24,28},{28,24},{1,5},{5... | collective-permute-start | bytes 589832 | tf_op jit(solution)/shard_map/ppermute | solution.py:19
  58.4 13.2 %collective-permute-start.7 = (f32[192,512]{1,0:T(8,128)}, f32[192,512]{1,0:T(8,128)}, u32[]{:S(2)}, u32[]{:S(2)}) collective-permute-start(f32[192,512]{1,0:T(8,128)} %collective-permute-done.6), channel_id=1, source_target_pairs={{0,4},{4,0},{8,12},{12,8},{16,20},{20,16},{24,28},{28,24},{1,5},{5... | collective-permute-start | bytes 1179656 | tf_op jit(solution)/shard_map/ppermute | solution.py:19
  58.9 2.6 %copy-start.12 = (f32[192,256]{0,1:T(8,128)}, f32[192,256]{0,1:T(8,128)S(1)}, u32[]{:S(2)}) copy-start(f32[192,256]{0,1:T(8,128)S(1)} %collective-permute-done.12) | copy-start | bytes 589828
  58.9 9.0 %collective-permute-start.22 = (f32[128,384]{1,0:T(8,128)}, f32[128,384]{1,0:T(8,128)}, u32[]{:S(2)}, u32[]{:S(2)}) collective-permute-start(f32[128,384]{1,0:T(8,128)} %add.68), channel_id=1, source_target_pairs={{0,16},{4,20},{8,24},{12,28},{16,0},{20,4},{24,8},{28,12},{1,17},{... | collective-permute-start | bytes 589832 | tf_op jit(solution)/shard_map/ppermute | solution.py:19
  61.4 0.7 copy-start.13
  62.1 11.6 %collective-permute-start.9 = (f32[192,512]{1,0:T(8,128)}, f32[192,512]{1,0:T(8,128)}, u32[]{:S(2)}, u32[]{:S(2)}) collective-permute-start(f32[192,512]{1,0:T(8,128)} %collective-permute-done.8), channel_id=1, source_target_pairs={{0,4},{4,0},{8,12},{12,8},{16,20},{20,16},{24,28},{28,24},{1,5},{5... | collective-permute-start | bytes 1179656 | tf_op jit(solution)/shard_map/ppermute | solution.py:19
  67.8 7.0 %copy-start.1 = (f32[1536,256]{0,1:T(8,128)S(1)}, f32[1536,256]{0,1:T(8,128)}, u32[]{:S(2)}) copy-start(f32[1536,256]{0,1:T(8,128)} %concatenate.30) | copy-start | bytes 4718596
  69.0 17.0 %collective-permute-start.23 = (f32[128,384]{1,0:T(8,128)S(1)}, f32[128,384]{1,0:T(8,128)S(1)}, u32[]{:S(2)}, u32[]{:S(2)}) collective-permute-start(f32[128,384]{1,0:T(8,128)S(1)} %add.69), channel_id=1, source_target_pairs={{0,4},{4,0},{8,12},{12,8},{16,20},{20,16},{24,28},{28,24},{1,5},{5... | collective-permute-start | bytes 589832 | tf_op jit(solution)/shard_map/ppermute | solution.py:19
  73.7 3.8 %copy-start.3 = (f32[192,256]{1,0:T(8,128)S(1)}, f32[192,256]{1,0:T(8,128)}, u32[]{:S(2)}) copy-start(f32[192,256]{1,0:T(8,128)} %param.6) | copy-start | bytes 589828
  73.7 4.1 %copy-start.4 = (f32[192,256]{1,0:T(8,128)S(1)}, f32[192,256]{1,0:T(8,128)}, u32[]{:S(2)}) copy-start(f32[192,256]{1,0:T(8,128)} %param.5) | copy-start | bytes 589828
  74.8 4.0 %copy-start.2 = (f32[192,384]{1,0:T(8,128)S(1)}, f32[192,384]{1,0:T(8,128)}, u32[]{:S(2)}) copy-start(f32[192,384]{1,0:T(8,128)} %param.4) | copy-start | bytes 884740
  74.8 4.0 %copy-start.6 = (f32[192,192]{1,0:T(8,128)S(1)}, f32[192,192]{1,0:T(8,128)}, u32[]{:S(2)}) copy-start(f32[192,192]{1,0:T(8,128)} %get-tuple-element.9) | copy-start | bytes 442372
  74.9 4.0 %copy-start.7 = (f32[192,192]{1,0:T(8,128)S(1)}, f32[192,192]{1,0:T(8,128)}, u32[]{:S(2)}) copy-start(f32[192,192]{1,0:T(8,128)} %get-tuple-element.10) | copy-start | bytes 442372
  77.5 1.7 %copy-start = (f32[1536,256]{1,0:T(8,128)S(1)}, f32[1536,256]{1,0:T(8,128)}, u32[]{:S(2)}) copy-start(f32[1536,256]{1,0:T(8,128)} %copy.5) | copy-start | bytes 4718596
  80.0 20.1 %collective-permute-start.19 = (f32[192,384]{1,0:T(8,128)S(1)}, f32[192,384]{1,0:T(8,128)S(1)}, u32[]{:S(2)}, u32[]{:S(2)}) collective-permute-start(f32[192,384]{1,0:T(8,128)S(1)} %fusion.1), channel_id=1, source_target_pairs={{0,3},{1,2},{2,1},{3,0},{4,7},{5,6},{6,5},{7,4},{8,11},{9,10},{10,... | collective-permute-start | bytes 884744 | tf_op jit(solution)/shard_map/ppermute | solution.py:19
  82.6 16.8 %collective-permute-start.17 = (f32[192,384]{1,0:T(8,128)S(1)}, f32[192,384]{1,0:T(8,128)S(1)}, u32[]{:S(2)}, u32[]{:S(2)}) collective-permute-start(f32[192,384]{1,0:T(8,128)S(1)} %fusion.7), channel_id=1, source_target_pairs={{0,1},{1,0},{2,3},{3,2},{4,5},{5,4},{6,7},{7,6},{8,9},{9,8},{10,11... | collective-permute-start | bytes 884744 | tf_op jit(solution)/shard_map/ppermute | solution.py:19
  83.7 24.1 %collective-permute-start.18 = (f32[192,384]{1,0:T(8,128)S(1)}, f32[192,384]{1,0:T(8,128)S(1)}, u32[]{:S(2)}, u32[]{:S(2)}) collective-permute-start(f32[192,384]{1,0:T(8,128)S(1)} %fusion.10), channel_id=1, source_target_pairs={{0,2},{1,3},{2,0},{3,1},{4,6},{5,7},{6,4},{7,5},{8,10},{9,11},{10,... | collective-permute-start | bytes 884744 | tf_op jit(solution)/shard_map/ppermute | solution.py:19

commit v2 on v1

v2 whole, which is shorter than its diff:
```python
import functools

import jax
import jax.numpy as jnp
from jax import lax
from jax.experimental import pallas as pl
from jax.experimental.pallas import tpu as pltpu
from jax.sharding import PartitionSpec as P

ALONG = ((1,), (1,))
OVER = ((1,), (0,))
DOWN = ((0,), (0,))
VMEM_BYTES = 24 * 2**20


def dot(first, second, dims):
    return lax.dot_general(
        first,
        second,
        (dims, ((), ())),
        precision=lax.Precision.HIGH,
        preferred_element_type=jnp.float32,
    )


def halves(value):
    high = value.astype(jnp.bfloat16)
    return high, (value - high.astype(jnp.float32)).astype(jnp.bfloat16)


def pair_dot(first, second, dims):
    def one(a, b):
        return lax.dot_general(a, b, (dims, ((), ())), preferred_element_type=jnp.float32)

    return one(first[0], second[0]) + (one(first[0], second[1]) + one(first[1], second[0]))


def swap(value, axis, offset):
    size = lax.axis_size(axis)
    return lax.ppermute(value, axis, [(i, i ^ offset) for i in range(size)])


def gather_row(value, rows):
    blocks = []
    for chip in range(0, rows, 2):
        here = swap(value, "row", chip) if chip else value
        blocks += [here, swap(here, "row", 1)]
    return blocks


def stack(*parts):
    return jnp.concatenate(parts, axis=0)


def gather_square(panels, own_refl, height):
    near_x, near_y = swap(panels, "row", 2), swap(panels, "row", 4)
    by_x = swap(stack(near_y[:height], own_refl), "row", 2)
    by_y = swap(stack(near_x[height:], own_refl), "row", 4)
    far = swap(own_refl, "row", 6)
    found = []
    for value, places in (
        (panels, ((0, 0), (0, 1))),
        (near_x, ((2, 0), (2, 1))),
        (near_y, ((4, 0), (4, 1))),
        (own_refl, ((0, 2),)),
        (by_x, ((6, 0), (2, 2))),
        (by_y, ((6, 1), (4, 2))),
        (far, ((6, 2),)),
    ):
        found.append((value, places))
        found.append((swap(value, "row", 1), tuple((i + 1, kind) for i, kind in places)))
    return found


def core_sum(value):
    core = lax.axis_index("row") % 2
    half = value.shape[0] // 2
    kept = lax.dynamic_slice_in_dim(value, core * half, half, 0)
    given = lax.dynamic_slice_in_dim(value, (1 - core) * half, half, 0)
    return kept + swap(given, "row", 1)


def chips_sum(total, rows):
    bit = 2
    while bit < rows:
        total = total + swap(total, "row", bit)
        bit *= 2
    core = lax.axis_index("row") % 2
    other = swap(total, "row", 1)
    first = jnp.where(core == 0, total, other)
    second = jnp.where(core == 0, other, total)
    return jnp.concatenate([first, second], axis=0)


def order_blocks(value, per, first):
    width = value.shape[1] // per
    bit = 1
    while bit < per:
        parts = [value[:, t * width : (t + 1) * width] for t in range(per)]
        moved = jnp.concatenate([parts[t ^ bit] for t in range(per)], axis=1)
        value = jnp.where((first // bit) % 2 == 1, moved, value)
        bit *= 2
    return value


def block_kernel(pieces, cols, per, share, place, *refs):
    in_refs, matrix = refs[: len(pieces)], refs[len(pieces)]
    outs = refs[len(pieces) + 1 : len(pieces) + 1 + cols]
    high, low, made = refs[len(pieces) + 1 + cols :]
    height = matrix.shape[0]
    wide = per * height
    base, first = place[0], place[1]
    for ref, places in zip(in_refs, pieces):
        for n, (index, kind) in enumerate(places):
            upper, lower = halves(ref[n * height : (n + 1) * height, :])
            rows = slice(index * height, (index + 1) * height)
            columns = slice(kind * share, kind * share + ref.shape[1])
            high[rows, columns] = upper
            low[rows, columns] = lower
    panels = (high[:, : 2 * share], low[:, : 2 * share])
    refl = (high[:, 2 * share :], low[:, 2 * share :])
    mixed = pair_dot(refl, panels, DOWN)
    own = in_refs[0][...]
    left_panel, right_panel = own[:height], own[height:]
    mixed_pair = halves(mixed)
    own_refl = (high[:height, 2 * share :], low[:height, 2 * share :])
    spread = pair_dot(own_refl, mixed_pair, OVER)
    turned = halves(jnp.concatenate([right_panel, -left_panel], axis=1))
    image = pair_dot(turned, mixed_pair, ALONG)
    for t in range(per):
        begin = pl.multiple_of((base * per + (t ^ first)) * height, 16)
        rows = pl.ds(begin, height)
        image = image + pair_dot(
            halves(matrix[:, t * height : (t + 1) * height]),
            (high[rows, 2 * share :], low[rows, 2 * share :]),
            OVER,
        )
    factors = halves(
        jnp.concatenate(
            [right_panel - spread[:, share:], spread[:, :share] - left_panel, -image], axis=1
        )
    )
    for block in range(cols):
        rows = slice(block * wide, (block + 1) * wide)
        made[block] = pair_dot(factors, (high[rows, :], low[rows, :]), ALONG)
    for k in range(cols):
        outs[k][...] = made[base ^ k]


def blocks_in_kernel(found, matrix, place, rows, cols, share, width):
    per = rows // cols
    arrays = [value for value, _ in found]
    pieces = tuple(places for _, places in found)
    height = matrix.shape[0]
    total, depth = rows * height, 2 * share + width
    out = jax.ShapeDtypeStruct((height, per * height), jnp.float32)
    flops = 6 * total * (2 * share * width + height * depth)
    vmem = pl.BlockSpec(memory_space=pltpu.VMEM)
    return pl.pallas_call(
        functools.partial(block_kernel, pieces, cols, per, share),
        out_shape=[out] * cols,
        in_specs=[pl.BlockSpec(memory_space=pltpu.SMEM)] + [vmem] * (len(arrays) + 1),
        out_specs=[vmem] * cols,
        scratch_shapes=[
            pltpu.VMEM((total, depth), jnp.bfloat16),
            pltpu.VMEM((total, depth), jnp.bfloat16),
            pltpu.VMEM((cols, height, per * height), jnp.float32),
        ],
        compiler_params=pltpu.CompilerParams(vmem_limit_bytes=VMEM_BYTES),
        cost_estimate=pl.CostEstimate(
            flops=flops, bytes_accessed=4 * total * depth, transcendentals=0
        ),
    )(place, *arrays, matrix)


def blocks_plain(panels, refls, matrix, base, first, cols, per):
    all_panels, all_refl = jnp.concatenate(panels, axis=0), jnp.concatenate(refls, axis=0)
    own, own_refl = panels[0], refls[0]
    height, share = own.shape[0], own.shape[1] // 2
    wide = per * height
    left_panel, right_panel = own[:, :share], own[:, share:]
    mixed = dot(all_panels, all_refl, DOWN)
    mixed_left, mixed_right = mixed[:share], mixed[share:]
    mine = order_blocks(matrix, per, first)
    col_refl = lax.dynamic_slice_in_dim(all_refl, base * wide, wide, 0)
    image = (
        dot(right_panel, mixed_left, OVER)
        - dot(left_panel, mixed_right, OVER)
        + dot(mine, col_refl, OVER)
    )
    factors = jnp.concatenate(
        [
            right_panel - dot(own_refl, mixed_right, ALONG),
            dot(own_refl, mixed_left, ALONG) - left_panel,
            -image,
        ],
        axis=1,
    )
    whole = jnp.concatenate([all_panels, all_refl], axis=1)
    return [
        dot(factors, lax.dynamic_slice_in_dim(whole, (base ^ k) * wide, wide, 0), ALONG)
        for k in range(cols)
    ]


def local(matrix, left_panel, right_panel, reflectors):
    rows, cols = lax.axis_size("row"), lax.axis_size("col")
    per = rows // cols
    row, col = lax.axis_index("row"), lax.axis_index("col")
    height, share = left_panel.shape
    base, first = (row // per) ^ col, row % per

    own_refl = reflectors
    bit = 1
    while bit < cols:
        own_refl = jnp.concatenate([own_refl, swap(own_refl, "col", bit)], axis=1)
        bit *= 2
    width = own_refl.shape[1]
    halved = core_sum(dot(own_refl, matrix, DOWN))

    need = rows * height * (2 * share + width) * 8 + rows * height * height * 8
    if rows == 8 and share == width and need <= VMEM_BYTES:
        found = gather_square(stack(left_panel, right_panel), own_refl, height)
        place = jnp.stack([base, first]).astype(jnp.int32)
        made = blocks_in_kernel(found, matrix, place, rows, cols, share, width)
    else:
        panels = gather_row(jnp.concatenate([left_panel, right_panel], axis=1), rows)
        refls = gather_row(own_refl, rows)
        made = blocks_plain(panels, refls, matrix, base, first, cols, per)

    halved, own_refl, _ = lax.optimization_barrier((halved, own_refl, made[0]))
    received = [swap(made[k], "col", k) for k in range(1, cols)]
    rest = lax.optimization_barrier(matrix - dot(own_refl, chips_sum(halved, rows), OVER))
    total = made[0]
    for block in received:
        total = total + block
    return order_blocks(total, per, first) + rest


def solution(mesh):
    spec = P("row", "col")
    return jax.shard_map(
        local, mesh=mesh, in_specs=(spec,) * 4, out_specs=spec, check_vma=False
    )
```

time: 110 us -> 75.6 us (0.69)
  the two profiles are of different devices: /device:TPU:0 before, /device:TPU:9 now
where the time goes in v2:
time: 75.6 us; the launch traced here: 75.4 us
  waiting for transfers between devices  38.1 us (50%)
  starting transfers between devices  22.7 us (30%)
  Pallas kernels  7.22 us (10%)
  local copies, waits for them, and re-layouts  4.24 us (6%)
  other arithmetic  2.31 us (3%)
    ppermute x21, waiting for transfers between devices, swap(): return lax.ppermute(value, axis, [(i, i ^ offset) for i in range(size)])  38.1 us
    ppermute x21, starting transfers between devices, swap(): return lax.ppermute(value, axis, [(i, i ^ offset) for i in range(size)])  22.7 us
    pallas_call x1, Pallas kernels, blocks_in_kernel(): pl.pallas_call(functools.partial(block_kernel, pieces, cols, per, share),...  7.22 us
    unnamed x16, local copies, waits for them, and re-layouts  3.6 us
  transfers between devices with their start and end apart: 21, of which 11 were waited for; matrix products, arithmetic and copies ran while one was open for 1% of the time, Pallas kernels for 10%

profile of v2, /device:TPU:9, one launch (start us, length us, event | category | flops | bytes accessed | tf_op | source)
XLA Modules:
  0.0 75.4 jit_solution(8506320004649240947)
XLA Ops:
  0.0 1.0 %constant_dynamic-update-slice_fusion.1 = f32[384,256]{1,0:T(8,128)S(1)} fusion(f32[192,256]{1,0:T(8,128)} %param.5), kind=kLoop, calls=%fused_computation.16 | loop fusion | bytes 393216
  1.0 1.3 %collective-permute-start.3 = (f32[384,256]{1,0:T(8,128)S(1)}, f32[384,256]{1,0:T(8,128)S(1)}, u32[]{:S(2)}, u32[]{:S(2)}) collective-permute-start(f32[384,256]{1,0:T(8,128)S(1)} %constant_dynamic-update-slice_fusion.refs_0_), channel_id=1, source_target_pairs={{0,16},{4,20},{8,24},{12,28},{16,0},{20,4},{24,8},{28,12},{1,17},{... | collective-permute-start | bytes 1179656 | tf_op jit(solution)/shard_map/ppermute | solution.py:40
  2.3 1.2 %collective-permute-start.1 = (f32[384,256]{1,0:T(8,128)S(1)}, f32[384,256]{1,0:T(8,128)S(1)}, u32[]{:S(2)}, u32[]{:S(2)}) collective-permute-start(f32[384,256]{1,0:T(8,128)S(1)} %constant_dynamic-update-slice_fusion.refs_0_), channel_id=1, source_target_pairs={{0,8},{4,12},{8,0},{12,4},{16,24},{20,28},{24,16},{28,20},{1,9},{5... | collective-permute-start | bytes 1179656 | tf_op jit(solution)/shard_map/ppermute | solution.py:40
  3.6 0.1 copy.7
  3.7 0.2 collective-permute-start.5
  3.9 3.6 %collective-permute-done.5 = f32[192,64]{1,0:T(8,128)S(1)} collective-permute-done((f32[192,64]{1,0:T(8,128)S(1)}, f32[192,64]{1,0:T(8,128)S(1)}, u32[]{:S(2)}, u32[]{:S(2)}) %collective-permute-start.5) | collective-permute-done | bytes 49184 | tf_op jit(solution)/shard_map/ppermute | solution.py:40
  7.5 0.1 pad_maximum_fusion.4
  7.6 2.4 %collective-permute-start.6 = (f32[192,128]{1,0:T(8,128)S(1)}, f32[192,128]{1,0:T(8,128)S(1)}, u32[]{:S(2)}, u32[]{:S(2)}) collective-permute-start(f32[192,128]{1,0:T(8,128)S(1)} %pad_maximum_fusion.4), channel_id=1, source_target_pairs={{0,2},{1,3},{2,0},{3,1},{4,6},{5,7},{6,4},{7,5},{8,10},{9,11},{10,... | collective-permute-start | bytes 294920 | tf_op jit(solution)/shard_map/ppermute | solution.py:40
  10.0 1.1 %collective-permute-done.3.refs_4_ = f32[384,256]{1,0:T(8,128)S(1)} collective-permute-done((f32[384,256]{1,0:T(8,128)S(1)}, f32[384,256]{1,0:T(8,128)S(1)}, u32[]{:S(2)}, u32[]{:S(2)}) %collective-permute-start.3) | collective-permute-done | bytes 393248 | tf_op jit(solution)/shard_map/ppermute | solution.py:40
  11.1 0.7 copy-done.1
  11.8 0.2 collective-permute-done.1.refs_2_
  12.0 0.4 collective-permute-done.6
  12.5 0.5 slice-done
  12.9 1.0 %pad_maximum_fusion.2 = (f32[384,256]{1,0:T(8,128)}, f32[384,256]{1,0:T(8,128)}) fusion(f32[192,256]{1,0:T(8,128)S(1)} %slice.17, f32[192,128]{1,0:T(8,128)S(1)} %collective-permute-done.6, f32[192,64]{1,0:T(8,128)S(1)} %collective-permute-done.5, f32[192,64]{1,0:T(8,128)S(1)} %copy.7, f32[192,256]{1,0:T(8,128)S(1)} %slice-done), kind=kLoop, calls=%fused_computation.3 | loop fusion | flops 393216 | bytes 1376256 | tf_op jit(solution)/shard_map/concatenate | solution.py:52
  14.0 1.1 %collective-permute-start.10 = (f32[384,256]{1,0:T(8,128)}, f32[384,256]{1,0:T(8,128)S(1)}, u32[]{:S(2)}, u32[]{:S(2)}) collective-permute-start(f32[384,256]{1,0:T(8,128)} %get-tuple-element.21), channel_id=1, source_target_pairs={{0,16},{4,20},{8,24},{12,28},{16,0},{20,4},{24,8},{28,12},{1,17},{... | collective-permute-start | bytes 1179656 | tf_op jit(solution)/shard_map/ppermute | solution.py:40
  15.0 1.2 %collective-permute-start.8 = (f32[384,256]{1,0:T(8,128)}, f32[384,256]{1,0:T(8,128)S(1)}, u32[]{:S(2)}, u32[]{:S(2)}) collective-permute-start(f32[384,256]{1,0:T(8,128)} %get-tuple-element.22), channel_id=1, source_target_pairs={{0,8},{4,12},{8,0},{12,4},{16,24},{20,28},{24,16},{28,20},{1,9},{5... | collective-permute-start | bytes 1179656 | tf_op jit(solution)/shard_map/ppermute | solution.py:40
  16.3 2.1 %collective-permute-start = (f32[384,256]{1,0:T(8,128)S(1)}, f32[384,256]{1,0:T(8,128)S(1)}, u32[]{:S(2)}, u32[]{:S(2)}) collective-permute-start(f32[384,256]{1,0:T(8,128)S(1)} %constant_dynamic-update-slice_fusion.refs_0_), channel_id=1, source_target_pairs={{0,4},{4,0},{8,12},{12,8},{16,20},{20,16},{24,28},{28,24},{1,5},{5... | collective-permute-start | bytes 1179656 | tf_op jit(solution)/shard_map/ppermute | solution.py:40
  18.4 0.1 pad_maximum_fusion.3.refs_6_
  18.5 1.4 %collective-permute-start.12 = (f32[192,256]{1,0:T(8,128)S(1)}, f32[192,256]{1,0:T(8,128)S(1)}, u32[]{:S(2)}, u32[]{:S(2)}) collective-permute-start(f32[192,256]{1,0:T(8,128)S(1)} %pad_maximum_fusion.3.refs_6_), channel_id=1, source_target_pairs={{0,24},{4,28},{8,16},{12,20},{16,8},{20,12},{24,0},{28,4},{1,25},{... | collective-permute-start | bytes 589832 | tf_op jit(solution)/shard_map/ppermute | solution.py:40
  19.8 0.3 collective-permute-start.7
  20.1 7.1 %collective-permute-done.12.refs_12_ = f32[192,256]{1,0:T(8,128)S(1)} collective-permute-done((f32[192,256]{1,0:T(8,128)S(1)}, f32[192,256]{1,0:T(8,128)S(1)}, u32[]{:S(2)}, u32[]{:S(2)}) %collective-permute-start.12) | collective-permute-done | bytes 196640 | tf_op jit(solution)/shard_map/ppermute | solution.py:40
  27.3 3.9 %collective-permute-start.2 = (f32[384,256]{1,0:T(8,128)S(1)}, f32[384,256]{1,0:T(8,128)S(1)}, u32[]{:S(2)}, u32[]{:S(2)}) collective-permute-start(f32[384,256]{1,0:T(8,128)S(1)} %collective-permute-done.1.refs_2_), channel_id=1, source_target_pairs={{0,4},{4,0},{8,12},{12,8},{16,20},{20,16},{24,28},{28,24},{1,5},{5... | collective-permute-start | bytes 1179656 | tf_op jit(solution)/shard_map/ppermute | solution.py:40
  31.1 0.1 collective-permute-start.4
  31.2 0.4 collective-permute-start.11
  31.6 0.1 collective-permute-start.9
  31.7 0.1 pad_add_fusion.place
  31.8 0.4 collective-permute-start.13
  32.2 0.4 fusion.6
  32.7 1.3 %collective-permute-done.13.refs_13_ = f32[192,256]{1,0:T(8,128)S(1)} collective-permute-done((f32[192,256]{1,0:T(8,128)S(1)}, f32[192,256]{1,0:T(8,128)S(1)}, u32[]{:S(2)}, u32[]{:S(2)}) %collective-permute-start.13) | collective-permute-done | bytes 196640 | tf_op jit(solution)/shard_map/ppermute | solution.py:40
  34.0 0.1 collective-permute-start.17
  34.2 0.7 copy-done.3
  34.9 1.0 %copy-done.4 = f32[384,256]{1,0:T(8,128)S(1)} copy-done((f32[384,256]{1,0:T(8,128)S(1)}, f32[384,256]{1,0:T(8,128)}, u32[]{:S(2)}) %copy-start.4) | copy-done | bytes 393240
  35.9 7.2 %shard_map.46 = (f32[192,384]{1,0:T(8,128)S(1)}, f32[192,384]{1,0:T(8,128)}, f32[192,384]{1,0:T(8,128)}, f32[192,384]{1,0:T(8,128)}) custom-call(s32[2]{0:T(128)S(1)} %pad_add_fusion.place, f32[384,256]{1,0:T(8,128)S(1)} %constant_dynamic-update-slice_fusion.refs_0_, f32[384,256]{1,0:T(8,128)S(1)} %collective-permute-done.refs_1_, ...), custom_call_target="tpu_custom_call" | custom-call | flops 2566914048 | bytes 4718592 | tf_op jit(solution)/shard_map/pallas_call | solution.py:159
  43.1 0.2 collective-permute-start.14
  43.3 2.3 %collective-permute-start.15 = (f32[192,384]{1,0:T(8,128)}, f32[192,384]{1,0:T(8,128)S(1)}, u32[]{:S(2)}, u32[]{:S(2)}) collective-permute-start(f32[192,384]{1,0:T(8,128)} %get-tuple-element.13), channel_id=1, source_target_pairs={{0,2},{1,3},{2,0},{3,1},{4,6},{5,7},{6,4},{7,5},{8,10},{9,11},{10,... | collective-permute-start | bytes 884744 | tf_op jit(solution)/shard_map/ppermute | solution.py:40
  45.6 0.2 collective-permute-start.16
  45.8 1.3 %collective-permute-start.18 = (f32[128,384]{1,0:T(8,128)S(1)}, f32[128,384]{1,0:T(8,128)S(1)}, u32[]{:S(2)}, u32[]{:S(2)}) collective-permute-start(f32[128,384]{1,0:T(8,128)S(1)} %dynamic-slice_add_fusion), channel_id=1, source_target_pairs={{0,8},{4,12},{8,0},{12,4},{16,24},{20,28},{24,16},{28,20},{1,9},{5... | collective-permute-start | bytes 589832 | tf_op jit(solution)/shard_map/ppermute | solution.py:40
  47.1 4.0 %collective-permute-done.18 = f32[128,384]{1,0:T(8,128)S(1)} collective-permute-done((f32[128,384]{1,0:T(8,128)S(1)}, f32[128,384]{1,0:T(8,128)S(1)}, u32[]{:S(2)}, u32[]{:S(2)}) %collective-permute-start.18) | collective-permute-done | bytes 196640 | tf_op jit(solution)/shard_map/ppermute | solution.py:40
  51.1 1.1 %collective-permute-start.19 = (f32[128,384]{1,0:T(8,128)S(1)}, f32[128,384]{1,0:T(8,128)S(1)}, u32[]{:S(2)}, u32[]{:S(2)}) collective-permute-start(f32[128,384]{1,0:T(8,128)S(1)} %add.46), channel_id=1, source_target_pairs={{0,16},{4,20},{8,24},{12,28},{16,0},{20,4},{24,8},{28,12},{1,17},{... | collective-permute-start | bytes 589832 | tf_op jit(solution)/shard_map/ppermute | solution.py:40
  52.2 3.2 %collective-permute-done.14 = f32[192,384]{1,0:T(8,128)S(1)} collective-permute-done((f32[192,384]{1,0:T(8,128)}, f32[192,384]{1,0:T(8,128)S(1)}, u32[]{:S(2)}, u32[]{:S(2)}) %collective-permute-start.14) | collective-permute-done | bytes 294944 | tf_op jit(solution)/shard_map/ppermute | solution.py:40
  55.4 3.6 %collective-permute-done.15 = f32[192,384]{1,0:T(8,128)S(1)} collective-permute-done((f32[192,384]{1,0:T(8,128)}, f32[192,384]{1,0:T(8,128)S(1)}, u32[]{:S(2)}, u32[]{:S(2)}) %collective-permute-start.15) | collective-permute-done | bytes 294944 | tf_op jit(solution)/shard_map/ppermute | solution.py:40
  58.9 12.5 %collective-permute-done.16 = f32[192,384]{1,0:T(8,128)S(1)} collective-permute-done((f32[192,384]{1,0:T(8,128)}, f32[192,384]{1,0:T(8,128)S(1)}, u32[]{:S(2)}, u32[]{:S(2)}) %collective-permute-start.16) | collective-permute-done | bytes 294944 | tf_op jit(solution)/shard_map/ppermute | solution.py:40
  71.5 0.1 add_add_fusion
  71.6 1.5 %collective-permute-start.20 = (f32[128,384]{1,0:T(8,128)S(1)}, f32[128,384]{1,0:T(8,128)S(1)}, u32[]{:S(2)}, u32[]{:S(2)}) collective-permute-start(f32[128,384]{1,0:T(8,128)S(1)} %add.47), channel_id=1, source_target_pairs={{0,4},{4,0},{8,12},{12,8},{16,20},{20,16},{24,28},{28,24},{1,5},{5... | collective-permute-start | bytes 589832 | tf_op jit(solution)/shard_map/ppermute | solution.py:40
  73.1 0.1 fusion.5
  73.2 1.0 %collective-permute-done.20 = f32[128,384]{1,0:T(8,128)S(1)} collective-permute-done((f32[128,384]{1,0:T(8,128)S(1)}, f32[128,384]{1,0:T(8,128)S(1)}, u32[]{:S(2)}, u32[]{:S(2)}) %collective-permute-start.20) | collective-permute-done | bytes 196640 | tf_op jit(solution)/shard_map/ppermute | solution.py:40
  74.2 0.3 convolution_subtract_fusion
  74.6 0.8 %fusion.3 = f32[192,384]{1,0:T(8,128)} fusion(f32[192,384]{1,0:T(8,128)S(1)} %convolution_subtract_fusion, f32[192,384]{1,0:T(8,128)S(1)} %add_add_fusion, f32[192,192]{1,0:T(8,128)S(1)} %get-tuple-element.20, f32[192,192]{1,0:T(8,128)S(1)} %get-tuple-element.19, pred[]{:T(512)S(6)} %eq.12), kind=kLoop, calls=%fused_computation.8 | loop fusion | flops 221184 | bytes 1179649 | tf_op jit(solution)/shard_map/add | solution.py:237
  (29 shorter events, 0.2 us)
Async XLA Ops:
  0.0 1.0 %copy-start.5 = (f32[192,256]{1,0:T(8,128)S(1)}, f32[192,256]{1,0:T(8,128)}, u32[]{:S(2)}) copy-start(f32[192,256]{1,0:T(8,128)} %param.6) | copy-start | bytes 589828
  1.0 2.5 %copy-start.6 = (f32[192,64]{0,1:T(8,128)S(1)}, f32[192,64]{0,1:T(8,128)}, u32[]{:S(2)}) copy-start(f32[192,64]{0,1:T(8,128)} %param.7) | copy-start | bytes 147460
  1.0 10.0 %collective-permute-start.3 = (f32[384,256]{1,0:T(8,128)S(1)}, f32[384,256]{1,0:T(8,128)S(1)}, u32[]{:S(2)}, u32[]{:S(2)}) collective-permute-start(f32[384,256]{1,0:T(8,128)S(1)} %constant_dynamic-update-slice_fusion.refs_0_), channel_id=1, source_target_pairs={{0,16},{4,20},{8,24},{12,28},{16,0},{20,4},{24,8},{28,12},{1,17},{... | collective-permute-start | bytes 1179656 | tf_op jit(solution)/shard_map/ppermute | solution.py:40
  2.3 9.7 %collective-permute-start.1 = (f32[384,256]{1,0:T(8,128)S(1)}, f32[384,256]{1,0:T(8,128)S(1)}, u32[]{:S(2)}, u32[]{:S(2)}) collective-permute-start(f32[384,256]{1,0:T(8,128)S(1)} %constant_dynamic-update-slice_fusion.refs_0_), channel_id=1, source_target_pairs={{0,8},{4,12},{8,0},{12,4},{16,24},{20,28},{24,16},{28,20},{1,9},{5... | collective-permute-start | bytes 1179656 | tf_op jit(solution)/shard_map/ppermute | solution.py:40
  3.7 3.8 %collective-permute-start.5 = (f32[192,64]{1,0:T(8,128)S(1)}, f32[192,64]{1,0:T(8,128)S(1)}, u32[]{:S(2)}, u32[]{:S(2)}) collective-permute-start(f32[192,64]{1,0:T(8,128)S(1)} %copy.7), channel_id=1, source_target_pairs={{0,1},{1,0},{2,3},{3,2},{4,5},{5,4},{6,7},{7,6},{8,9},{9,8},{10,11... | collective-permute-start | bytes 147464 | tf_op jit(solution)/shard_map/ppermute | solution.py:40
  7.6 4.9 %collective-permute-start.6 = (f32[192,128]{1,0:T(8,128)S(1)}, f32[192,128]{1,0:T(8,128)S(1)}, u32[]{:S(2)}, u32[]{:S(2)}) collective-permute-start(f32[192,128]{1,0:T(8,128)S(1)} %pad_maximum_fusion.4), channel_id=1, source_target_pairs={{0,2},{1,3},{2,0},{3,1},{4,6},{5,7},{6,4},{7,5},{8,10},{9,11},{10,... | collective-permute-start | bytes 294920 | tf_op jit(solution)/shard_map/ppermute | solution.py:40
  11.1 0.7 copy-start.1
  12.0 0.9 %slice-start = ((f32[384,256]{1,0:T(8,128)}), f32[192,256]{1,0:T(8,128)S(1)}, s32[]{:S(2)}) async-start(f32[384,256]{1,0:T(8,128)} %copy-done.1), calls=%async_computation | async-start | bytes 393216 | tf_op jit(solution)/shard_map/slice | solution.py:57
  12.9 18.2 %copy-start.2 = (f32[384,256]{1,0:T(8,128)S(1)}, f32[384,256]{1,0:T(8,128)}, u32[]{:S(2)}) copy-start(f32[384,256]{1,0:T(8,128)} %copy-done.1) | copy-start | bytes 1179652
  14.0 18.3 %copy-start = (f32[192,384]{1,0:T(8,128)S(1)}, f32[192,384]{1,0:T(8,128)}, u32[]{:S(2)}) copy-start(f32[192,384]{1,0:T(8,128)} %refs_14_.1) | copy-start | bytes 884740
  14.0 17.2 %collective-permute-start.10 = (f32[384,256]{1,0:T(8,128)}, f32[384,256]{1,0:T(8,128)S(1)}, u32[]{:S(2)}, u32[]{:S(2)}) collective-permute-start(f32[384,256]{1,0:T(8,128)} %get-tuple-element.21), channel_id=1, source_target_pairs={{0,16},{4,20},{8,24},{12,28},{16,0},{20,4},{24,8},{28,12},{1,17},{... | collective-permute-start | bytes 1179656 | tf_op jit(solution)/shard_map/ppermute | solution.py:40
  15.0 16.6 %collective-permute-start.8 = (f32[384,256]{1,0:T(8,128)}, f32[384,256]{1,0:T(8,128)S(1)}, u32[]{:S(2)}, u32[]{:S(2)}) collective-permute-start(f32[384,256]{1,0:T(8,128)} %get-tuple-element.22), channel_id=1, source_target_pairs={{0,8},{4,12},{8,0},{12,4},{16,24},{20,28},{24,16},{28,20},{1,9},{5... | collective-permute-start | bytes 1179656 | tf_op jit(solution)/shard_map/ppermute | solution.py:40
  16.3 15.5 %collective-permute-start = (f32[384,256]{1,0:T(8,128)S(1)}, f32[384,256]{1,0:T(8,128)S(1)}, u32[]{:S(2)}, u32[]{:S(2)}) collective-permute-start(f32[384,256]{1,0:T(8,128)S(1)} %constant_dynamic-update-slice_fusion.refs_0_), channel_id=1, source_target_pairs={{0,4},{4,0},{8,12},{12,8},{16,20},{20,16},{24,28},{28,24},{1,5},{5... | collective-permute-start | bytes 1179656 | tf_op jit(solution)/shard_map/ppermute | solution.py:40
  18.5 8.8 %collective-permute-start.12 = (f32[192,256]{1,0:T(8,128)S(1)}, f32[192,256]{1,0:T(8,128)S(1)}, u32[]{:S(2)}, u32[]{:S(2)}) collective-permute-start(f32[192,256]{1,0:T(8,128)S(1)} %pad_maximum_fusion.3.refs_6_), channel_id=1, source_target_pairs={{0,24},{4,28},{8,16},{12,20},{16,8},{20,12},{24,0},{28,4},{1,25},{... | collective-permute-start | bytes 589832 | tf_op jit(solution)/shard_map/ppermute | solution.py:40
  19.8 11.3 %collective-permute-start.7 = (f32[192,256]{1,0:T(8,128)S(1)}, f32[192,256]{1,0:T(8,128)}, u32[]{:S(2)}, u32[]{:S(2)}) collective-permute-start(f32[192,256]{1,0:T(8,128)S(1)} %pad_maximum_fusion.3.refs_6_), channel_id=1, source_target_pairs={{0,4},{4,0},{8,12},{12,8},{16,20},{20,16},{24,28},{28,24},{1,5},{5... | collective-permute-start | bytes 589832 | tf_op jit(solution)/shard_map/ppermute | solution.py:40
  27.3 6.9 %collective-permute-start.2 = (f32[384,256]{1,0:T(8,128)S(1)}, f32[384,256]{1,0:T(8,128)S(1)}, u32[]{:S(2)}, u32[]{:S(2)}) collective-permute-start(f32[384,256]{1,0:T(8,128)S(1)} %collective-permute-done.1.refs_2_), channel_id=1, source_target_pairs={{0,4},{4,0},{8,12},{12,8},{16,20},{20,16},{24,28},{28,24},{1,5},{5... | collective-permute-start | bytes 1179656 | tf_op jit(solution)/shard_map/ppermute | solution.py:40
  31.1 3.8 %collective-permute-start.4 = (f32[384,256]{1,0:T(8,128)S(1)}, f32[384,256]{1,0:T(8,128)}, u32[]{:S(2)}, u32[]{:S(2)}) collective-permute-start(f32[384,256]{1,0:T(8,128)S(1)} %copy-done.2), channel_id=1, source_target_pairs={{0,4},{4,0},{8,12},{12,8},{16,20},{20,16},{24,28},{28,24},{1,5},{5... | collective-permute-start | bytes 1179656 | tf_op jit(solution)/shard_map/ppermute | solution.py:40
  31.2 3.7 %collective-permute-start.11 = (f32[384,256]{1,0:T(8,128)S(1)}, f32[384,256]{1,0:T(8,128)}, u32[]{:S(2)}, u32[]{:S(2)}) collective-permute-start(f32[384,256]{1,0:T(8,128)S(1)} %collective-permute-done.10.refs_10_), channel_id=1, source_target_pairs={{0,4},{4,0},{8,12},{12,8},{16,20},{20,16},{24,28},{28,24},{1,5},{5... | collective-permute-start | bytes 1179656 | tf_op jit(solution)/shard_map/ppermute | solution.py:40
  31.6 3.3 %collective-permute-start.9 = (f32[384,256]{1,0:T(8,128)S(1)}, f32[384,256]{1,0:T(8,128)}, u32[]{:S(2)}, u32[]{:S(2)}) collective-permute-start(f32[384,256]{1,0:T(8,128)S(1)} %collective-permute-done.8.refs_8_), channel_id=1, source_target_pairs={{0,4},{4,0},{8,12},{12,8},{16,20},{20,16},{24,28},{28,24},{1,5},{5... | collective-permute-start | bytes 1179656 | tf_op jit(solution)/shard_map/ppermute | solution.py:40
  31.8 2.2 %collective-permute-start.13 = (f32[192,256]{1,0:T(8,128)S(1)}, f32[192,256]{1,0:T(8,128)S(1)}, u32[]{:S(2)}, u32[]{:S(2)}) collective-permute-start(f32[192,256]{1,0:T(8,128)S(1)} %collective-permute-done.12.refs_12_), channel_id=1, source_target_pairs={{0,4},{4,0},{8,12},{12,8},{16,20},{20,16},{24,28},{28,24},{1,5},{5... | collective-permute-start | bytes 589832 | tf_op jit(solution)/shard_map/ppermute | solution.py:40
  34.0 11.8 %collective-permute-start.17 = (f32[128,384]{1,0:T(8,128)S(1)}, f32[128,384]{1,0:T(8,128)S(1)}, u32[]{:S(2)}, u32[]{:S(2)}) collective-permute-start(f32[128,384]{1,0:T(8,128)S(1)} %constant_dynamic-slice_fusion), channel_id=1, source_target_pairs={{0,4},{4,0},{8,12},{12,8},{16,20},{20,16},{24,28},{28,24},{1,5},{5... | collective-permute-start | bytes 589832 | tf_op jit(solution)/shard_map/ppermute | solution.py:40
  34.2 0.7 copy-start.3
  34.9 1.0 %copy-start.4 = (f32[384,256]{1,0:T(8,128)S(1)}, f32[384,256]{1,0:T(8,128)}, u32[]{:S(2)}) copy-start(f32[384,256]{1,0:T(8,128)} %copy-done.3) | copy-start | bytes 1179652
  43.1 12.2 %collective-permute-start.14 = (f32[192,384]{1,0:T(8,128)}, f32[192,384]{1,0:T(8,128)S(1)}, u32[]{:S(2)}, u32[]{:S(2)}) collective-permute-start(f32[192,384]{1,0:T(8,128)} %get-tuple-element.12), channel_id=1, source_target_pairs={{0,1},{1,0},{2,3},{3,2},{4,5},{5,4},{6,7},{7,6},{8,9},{9,8},{10,11... | collective-permute-start | bytes 884744 | tf_op jit(solution)/shard_map/ppermute | solution.py:40
  43.3 15.6 %collective-permute-start.15 = (f32[192,384]{1,0:T(8,128)}, f32[192,384]{1,0:T(8,128)S(1)}, u32[]{:S(2)}, u32[]{:S(2)}) collective-permute-start(f32[192,384]{1,0:T(8,128)} %get-tuple-element.13), channel_id=1, source_target_pairs={{0,2},{1,3},{2,0},{3,1},{4,6},{5,7},{6,4},{7,5},{8,10},{9,11},{10,... | collective-permute-start | bytes 884744 | tf_op jit(solution)/shard_map/ppermute | solution.py:40
  45.6 25.9 %collective-permute-start.16 = (f32[192,384]{1,0:T(8,128)}, f32[192,384]{1,0:T(8,128)S(1)}, u32[]{:S(2)}, u32[]{:S(2)}) collective-permute-start(f32[192,384]{1,0:T(8,128)} %get-tuple-element.14), channel_id=1, source_target_pairs={{0,3},{1,2},{2,1},{3,0},{4,7},{5,6},{6,5},{7,4},{8,11},{9,10},{10,... | collective-permute-start | bytes 884744 | tf_op jit(solution)/shard_map/ppermute | solution.py:40
  45.8 5.3 %collective-permute-start.18 = (f32[128,384]{1,0:T(8,128)S(1)}, f32[128,384]{1,0:T(8,128)S(1)}, u32[]{:S(2)}, u32[]{:S(2)}) collective-permute-start(f32[128,384]{1,0:T(8,128)S(1)} %dynamic-slice_add_fusion), channel_id=1, source_target_pairs={{0,8},{4,12},{8,0},{12,4},{16,24},{20,28},{24,16},{28,20},{1,9},{5... | collective-permute-start | bytes 589832 | tf_op jit(solution)/shard_map/ppermute | solution.py:40
  51.1 20.5 %collective-permute-start.19 = (f32[128,384]{1,0:T(8,128)S(1)}, f32[128,384]{1,0:T(8,128)S(1)}, u32[]{:S(2)}, u32[]{:S(2)}) collective-permute-start(f32[128,384]{1,0:T(8,128)S(1)} %add.46), channel_id=1, source_target_pairs={{0,16},{4,20},{8,24},{12,28},{16,0},{20,4},{24,8},{28,12},{1,17},{... | collective-permute-start | bytes 589832 | tf_op jit(solution)/shard_map/ppermute | solution.py:40
  71.6 2.6 %collective-permute-start.20 = (f32[128,384]{1,0:T(8,128)S(1)}, f32[128,384]{1,0:T(8,128)S(1)}, u32[]{:S(2)}, u32[]{:S(2)}) collective-permute-start(f32[128,384]{1,0:T(8,128)S(1)} %add.47), channel_id=1, source_target_pairs={{0,4},{4,0},{8,12},{12,8},{16,20},{20,16},{24,28},{28,24},{1,5},{5... | collective-permute-start | bytes 589832 | tf_op jit(solution)/shard_map/ppermute | solution.py:40

commit v3 on v2

v3 whole, which is shorter than its diff:
```python
import functools

import jax
import jax.numpy as jnp
from jax import lax
from jax.experimental import pallas as pl
from jax.experimental.pallas import tpu as pltpu
from jax.sharding import PartitionSpec as P

ALONG = ((1,), (1,))
OVER = ((1,), (0,))
DOWN = ((0,), (0,))
VMEM_BYTES = 24 * 2**20


def dot(first, second, dims):
    return lax.dot_general(
        first,
        second,
        (dims, ((), ())),
        precision=lax.Precision.HIGH,
        preferred_element_type=jnp.float32,
    )


def halves(value):
    high = value.astype(jnp.bfloat16)
    return high, (value - high.astype(jnp.float32)).astype(jnp.bfloat16)


def pair_dot(first, second, dims):
    def one(a, b):
        return lax.dot_general(a, b, (dims, ((), ())), preferred_element_type=jnp.float32)

    return one(first[0], second[0]) + (one(first[0], second[1]) + one(first[1], second[0]))


def swap(value, axis, offset):
    size = lax.axis_size(axis)
    return lax.ppermute(value, axis, [(i, i ^ offset) for i in range(size)])


def gather_row(value, rows):
    blocks = []
    for chip in range(0, rows, 2):
        here = swap(value, "row", chip) if chip else value
        blocks += [here, swap(here, "row", 1)]
    return blocks


def stack(*parts):
    return jnp.concatenate(parts, axis=0)


def pack_kernel(panels, near_x, near_y, *refs):
    *parts, by_x, by_y, near = refs
    height = panels.shape[0] // 2
    at = 0
    for part in parts:
        near[:height, at : at + part.shape[1]] = part[...]
        at += part.shape[1]
    for n, value in enumerate((panels, near_x, near_y)):
        near[(2 * n + 1) * height : (2 * n + 3) * height, :] = value[...]
    by_x[:height, :] = near_y[:height, :]
    by_x[height:, :] = near[:height, :]
    by_y[:height, :] = near_x[height:, :]
    by_y[height:, :] = near[:height, :]


def gather_square(panels, refl_parts, height):
    near_x, near_y = swap(panels, "row", 2), swap(panels, "row", 4)
    width = panels.shape[1]
    by_x, by_y, near = run_kernel(
        pack_kernel,
        [(2 * height, width)] * 2 + [(7 * height, width)],
        [panels, near_x, near_y, *refl_parts],
        (),
        0,
        72 * height * width,
    )
    far = swap(near[:height], "row", 6)
    by_x, by_y = swap(by_x, "row", 2), swap(by_y, "row", 4)
    last = stack(by_x, by_y, far)
    near_at = ((0, 2), (0, 0), (0, 1), (2, 0), (2, 1), (4, 0), (4, 1))
    last_at = ((6, 0), (2, 2), (6, 1), (4, 2), (6, 2))

    def across(places):
        return tuple((index + 1, kind) for index, kind in places)

    found = []
    for value, places in ((near, near_at), (last, last_at)):
        found += [(value, places), (swap(value, "row", 1), across(places))]
    return found, near, by_x


def core_sum(value):
    core = lax.axis_index("row") % 2
    half = value.shape[0] // 2
    kept = lax.dynamic_slice_in_dim(value, core * half, half, 0)
    given = lax.dynamic_slice_in_dim(value, (1 - core) * half, half, 0)
    return kept + swap(given, "row", 1)


def chips_sum(total, rows):
    bit = 2
    while bit < rows:
        total = total + swap(total, "row", bit)
        bit *= 2
    core = lax.axis_index("row") % 2
    other = swap(total, "row", 1)
    first = jnp.where(core == 0, total, other)
    second = jnp.where(core == 0, other, total)
    return jnp.concatenate([first, second], axis=0)


def order_blocks(value, per, first):
    width = value.shape[1] // per
    bit = 1
    while bit < per:
        parts = [value[:, t * width : (t + 1) * width] for t in range(per)]
        moved = jnp.concatenate([parts[t ^ bit] for t in range(per)], axis=1)
        value = jnp.where((first // bit) % 2 == 1, moved, value)
        bit *= 2
    return value


def place_in_kernel(per):
    row, col = lax.axis_index("row"), lax.axis_index("col")
    return (row // per) ^ col, row % per


def split_pieces(pieces, in_refs, high, low, height, share):
    for ref, places in zip(in_refs, pieces):
        for n, (index, kind) in enumerate(places):
            upper, lower = halves(ref[n * height : (n + 1) * height, :])
            rows = slice(index * height, (index + 1) * height)
            columns = slice(kind * share, (kind + 1) * share)
            high[rows, columns] = upper
            low[rows, columns] = lower


def block_of(factors, high, low, begin, wide):
    height = factors.shape[0] // 2
    rows = pl.ds(pl.multiple_of(begin, 16), wide)

    def one(a, b):
        return lax.dot_general(a, b, (ALONG, ((), ())), preferred_element_type=jnp.float32)

    both = one(factors, high[rows, :])
    return both[:height] + (both[height:] + one(factors[:height], low[rows, :]))


def send_kernel(pieces, per, share, offsets, *refs):
    count = len(pieces)
    in_refs, matrix, factors_ref = refs[:count], refs[count], refs[count + 1]
    outs = refs[count + 2 : count + 2 + len(offsets)]
    high, low = refs[count + 2 + len(offsets) :]
    height = matrix.shape[0]
    wide = per * height
    base, first = place_in_kernel(per)
    split_pieces(pieces, in_refs, high, low, height, share)
    panels = (high[:, : 2 * share], low[:, : 2 * share])
    refl = (high[:, 2 * share :], low[:, 2 * share :])
    mixed_pair = halves(pair_dot(refl, panels, DOWN))
    left_panel, right_panel = (in_refs[0][n * height : (n + 1) * height, :] for n in (1, 2))
    own_refl = (high[:height, 2 * share :], low[:height, 2 * share :])
    spread = pair_dot(own_refl, mixed_pair, OVER)
    turned = halves(jnp.concatenate([right_panel, -left_panel], axis=1))
    image = pair_dot(turned, mixed_pair, ALONG)
    for t in range(per):
        begin = pl.multiple_of((base * per + (t ^ first)) * height, 16)
        rows = pl.ds(begin, height)
        image = image + pair_dot(
            halves(matrix[:, t * height : (t + 1) * height]),
            (high[rows, 2 * share :], low[rows, 2 * share :]),
            OVER,
        )
    factors = jnp.concatenate(
        [right_panel - spread[:, share:], spread[:, :share] - left_panel, -image], axis=1
    )
    factors_ref[...] = factors
    stacked = jnp.concatenate(halves(factors), axis=0)
    for k, out in zip(offsets, outs):
        out[...] = block_of(stacked, high, low, (base ^ k) * wide, wide)


def keep_kernel(pieces, per, share, *refs):
    count = len(pieces)
    in_refs, (factors_ref, matrix, out, high, low, made) = refs[:count], refs[count:]
    height = matrix.shape[0]
    wide = per * height
    base, first = place_in_kernel(per)
    split_pieces(pieces, in_refs, high, low, height, share)
    stacked = jnp.concatenate(halves(factors_ref[...]), axis=0)
    made[...] = block_of(stacked, high, low, base * wide, wide)
    put_in_order(out, matrix, made, first, per)


def put_in_order(out, base, total, first, per):
    height = out.shape[0]
    for other in range(per):

        @pl.when(first == other)
        def _():
            for t in range(per):
                here = slice(t * height, (t + 1) * height)
                there = slice((t ^ other) * height, ((t ^ other) + 1) * height)
                out[:, here] = base[:, here] + total[:, there]


def sides_kernel(near, matrix, out):
    refl = near[: matrix.shape[0], :]
    out[...] = pair_dot(halves(refl), halves(matrix[...]), DOWN)


def sum_kernel(per, *refs):
    *blocks, base, out, made = refs
    _, first = place_in_kernel(per)
    total = blocks[0][...]
    for block in blocks[1:]:
        total = total + block[...]
    made[...] = total
    put_in_order(out, base, made, first, per)


def last_kernel(*refs):
    summed, sides, *parts, near, out = refs
    refl = near[: out.shape[0], :]
    whole = sides[...] + jnp.concatenate([part[...] for part in parts], axis=0)
    out[...] = summed[...] - pair_dot(halves(refl), halves(whole), OVER)


def run_kernel(body, outs, args, scratch=(), flops=0, moved=0):
    vmem = pl.BlockSpec(memory_space=pltpu.VMEM)
    return pl.pallas_call(
        body,
        out_shape=[jax.ShapeDtypeStruct(shape, jnp.float32) for shape in outs],
        in_specs=[vmem] * len(args),
        out_specs=[vmem] * len(outs),
        scratch_shapes=list(scratch),
        compiler_params=pltpu.CompilerParams(vmem_limit_bytes=VMEM_BYTES),
        cost_estimate=pl.CostEstimate(flops=flops, bytes_accessed=moved, transcendentals=0),
    )(*args)


def blocks_plain(panels, refls, matrix, base, first, cols, per):
    all_panels, all_refl = jnp.concatenate(panels, axis=0), jnp.concatenate(refls, axis=0)
    own, own_refl = panels[0], refls[0]
    height, share = own.shape[0], own.shape[1] // 2
    wide = per * height
    left_panel, right_panel = own[:, :share], own[:, share:]
    mixed = dot(all_panels, all_refl, DOWN)
    mixed_left, mixed_right = mixed[:share], mixed[share:]
    mine = order_blocks(matrix, per, first)
    col_refl = lax.dynamic_slice_in_dim(all_refl, base * wide, wide, 0)
    image = (
        dot(right_panel, mixed_left, OVER)
        - dot(left_panel, mixed_right, OVER)
        + dot(mine, col_refl, OVER)
    )
    factors = jnp.concatenate(
        [
            right_panel - dot(own_refl, mixed_right, ALONG),
            dot(own_refl, mixed_left, ALONG) - left_panel,
            -image,
        ],
        axis=1,
    )
    whole = jnp.concatenate([all_panels, all_refl], axis=1)
    return [
        dot(factors, lax.dynamic_slice_in_dim(whole, (base ^ k) * wide, wide, 0), ALONG)
        for k in range(cols)
    ]


def gather_columns(reflectors, cols):
    value, bit = reflectors, 1
    while bit < cols:
        value = jnp.concatenate([value, swap(value, "col", bit)], axis=1)
        bit *= 2
    return value


def local_square(matrix, left_panel, right_panel, reflectors):
    rows, cols = lax.axis_size("row"), lax.axis_size("col")
    per = rows // cols
    height, share = left_panel.shape
    wide = per * height
    refl_parts, bit = [reflectors], 1
    while bit < cols:
        known = jnp.concatenate(refl_parts, axis=1)
        refl_parts = [known, swap(known, "col", bit)]
        bit *= 2
    found, near, by_x = gather_square(stack(left_panel, right_panel), refl_parts, height)
    width = share
    (sides,) = run_kernel(
        sides_kernel,
        [(width, wide)],
        [near, matrix],
        (),
        6 * height * width * wide,
        4 * height * (width + wide),
    )
    sides = sides + swap(sides, "row", 1)
    sides, _ = lax.optimization_barrier((sides, by_x))
    beside = swap(sides, "row", 2)

    arrays = [value for value, _ in found]
    pieces = tuple(places for _, places in found)
    total, depth = rows * height, 2 * share + width
    halved = pltpu.VMEM((total, depth), jnp.bfloat16)
    block = pltpu.VMEM((height, wide), jnp.float32)
    offsets = sorted(range(1, cols), key=lambda k: (k == 1, k))
    factors, *blocks = run_kernel(
        functools.partial(send_kernel, pieces, per, share, offsets),
        [(height, depth)] + [(height, wide)] * len(offsets),
        arrays + [matrix],
        [halved, halved],
        12 * total * share * width + 6 * total * height * depth,
        4 * total * depth,
    )
    received = [swap(b, "col", k) for k, b in zip(offsets, blocks)]
    (base,) = run_kernel(
        functools.partial(keep_kernel, pieces, per, share),
        [(height, wide)],
        arrays + [factors, matrix],
        [halved, halved, block],
        6 * wide * height * depth,
        4 * total * depth,
    )
    sides, beside, _ = lax.optimization_barrier((sides, beside, factors))
    sides = sides + beside
    parts = [swap(sides[n : n + width // 2], "row", 4) for n in (0, width // 2)]
    (summed,) = run_kernel(
        functools.partial(sum_kernel, per),
        [(height, wide)],
        [*received, base],
        [block],
        height * wide * cols,
        4 * height * wide * (cols + 1),
    )
    summed, parts = lax.optimization_barrier((summed, parts))
    (updated,) = run_kernel(
        last_kernel,
        [(height, wide)],
        [summed, sides, *parts, near],
        (),
        6 * height * width * wide,
        4 * width * wide * 2,
    )
    return updated


def local_general(matrix, left_panel, right_panel, reflectors):
    rows, cols = lax.axis_size("row"), lax.axis_size("col")
    per = rows // cols
    row, col = lax.axis_index("row"), lax.axis_index("col")
    base, first = (row // per) ^ col, row % per
    own_refl = gather_columns(reflectors, cols)
    panels = gather_row(jnp.concatenate([left_panel, right_panel], axis=1), rows)
    refls = gather_row(own_refl, rows)
    made = blocks_plain(panels, refls, matrix, base, first, cols, per)
    total = made[0]
    for k in range(1, cols):
        total = total + swap(made[k], "col", k)
    sides = chips_sum(core_sum(dot(own_refl, matrix, DOWN)), rows)
    return order_blocks(total, per, first) + (matrix - dot(own_refl, sides, OVER))


def local(matrix, left_panel, right_panel, reflectors):
    rows, cols = lax.axis_size("row"), lax.axis_size("col")
    height, share = left_panel.shape
    width = reflectors.shape[1] * cols
    need = rows * height * (2 * share + width) * 8 + rows * height * height * 8
    if rows == 8 and share == width and need <= VMEM_BYTES:
        return local_square(matrix, left_panel, right_panel, reflectors)
    return local_general(matrix, left_panel, right_panel, reflectors)


def solution(mesh):
    spec = P("row", "col")
    return jax.shard_map(
        local, mesh=mesh, in_specs=(spec,) * 4, out_specs=spec, check_vma=False
    )
```

time: 75.6 us -> 69.1 us (0.914)
  the two profiles are of different devices: /device:TPU:9 before, /device:TPU:17 now
where the time goes in v3:
time: 69.1 us; the launch traced here: 68.9 us
  waiting for transfers between devices  36.4 us (53%)
  starting transfers between devices  21.2 us (31%)
  Pallas kernels  7.97 us (12%)
  local copies, waits for them, and re-layouts  2.93 us (4%)
    ppermute x16, waiting for transfers between devices, swap(): return lax.ppermute(value, axis, [(i, i ^ offset) for i in range(size)])  36.4 us
    ppermute x16, starting transfers between devices, swap(): return lax.ppermute(value, axis, [(i, i ^ offset) for i in range(size)])  21.2 us
    pallas_call x6, Pallas kernels, run_kernel(): pl.pallas_call(body, out_shape=[jax.ShapeDtypeStruct(shape, jnp.float32)...  7.97 us
    unnamed x6, local copies, waits for them, and re-layouts  1.93 us
  transfers between devices with their start and end apart: 16, of which 8 were waited for; matrix products, arithmetic and copies ran while one was open for 2% of the time, Pallas kernels for 10%

profile of v3, /device:TPU:17, one launch (start us, length us, event | category | flops | bytes accessed | tf_op | source)
XLA Modules:
  0.0 68.9 jit_solution(12332959391244462246)
XLA Ops:
  0.0 0.9 %constant_dynamic-update-slice_fusion.1 = f32[384,256]{1,0:T(8,128)S(1)} fusion(f32[192,256]{1,0:T(8,128)} %param.5), kind=kLoop, calls=%fused_computation.2 | loop fusion | bytes 393216
  0.9 0.9 %constant_dynamic-update-slice_fusion.panels = f32[384,256]{1,0:T(8,128)S(1)} fusion(f32[384,256]{1,0:T(8,128)S(1)} %constant_dynamic-update-slice_fusion.1, f32[192,256]{1,0:T(8,128)} %param.6), kind=kLoop, calls=%fused_computation.1 | loop fusion | bytes 393216 | tf_op jit(solution)/shard_map/concatenate | solution.py:52
  1.9 1.3 %collective-permute-start = (f32[384,256]{1,0:T(8,128)S(1)}, f32[384,256]{1,0:T(8,128)S(1)}, u32[]{:S(2)}, u32[]{:S(2)}) collective-permute-start(f32[384,256]{1,0:T(8,128)S(1)} %constant_dynamic-update-slice_fusion.panels), channel_id=1, source_target_pairs={{0,8},{4,12},{8,0},{12,4},{16,24},{20,28},{24,16},{28,20},{1,9},{5... | collective-permute-start | bytes 1179656 | tf_op jit(solution)/shard_map/ppermute | solution.py:40
  3.2 1.2 %collective-permute-start.1 = (f32[384,256]{1,0:T(8,128)S(1)}, f32[384,256]{1,0:T(8,128)S(1)}, u32[]{:S(2)}, u32[]{:S(2)}) collective-permute-start(f32[384,256]{1,0:T(8,128)S(1)} %constant_dynamic-update-slice_fusion.panels), channel_id=1, source_target_pairs={{0,16},{4,20},{8,24},{12,28},{16,0},{20,4},{24,8},{28,12},{1,17},{... | collective-permute-start | bytes 1179656 | tf_op jit(solution)/shard_map/ppermute | solution.py:40
  4.4 0.9 %copy.6 = f32[192,64]{1,0:T(8,128)S(1)} copy(f32[192,64]{0,1:T(8,128)} %param.7) | data formatting | bytes 98304 | tf_op args[3]
  5.3 1.4 %collective-permute-start.2 = (f32[192,64]{1,0:T(8,128)S(1)}, f32[192,64]{1,0:T(8,128)S(1)}, u32[]{:S(2)}, u32[]{:S(2)}) collective-permute-start(f32[192,64]{1,0:T(8,128)S(1)} %copy.6), channel_id=1, source_target_pairs={{0,1},{1,0},{2,3},{3,2},{4,5},{5,4},{6,7},{7,6},{8,9},{9,8},{10,11... | collective-permute-start | bytes 147464 | tf_op jit(solution)/shard_map/ppermute | solution.py:40
  6.7 2.5 %collective-permute-done.2 = f32[192,64]{1,0:T(8,128)S(1)} collective-permute-done((f32[192,64]{1,0:T(8,128)S(1)}, f32[192,64]{1,0:T(8,128)S(1)}, u32[]{:S(2)}, u32[]{:S(2)}) %collective-permute-start.2) | collective-permute-done | bytes 49184 | tf_op jit(solution)/shard_map/ppermute | solution.py:40
  9.2 0.1 pad_maximum_fusion.refs_0_
  9.3 0.1 collective-permute-start.3
  9.4 4.4 %collective-permute-done.3.refs_1_ = f32[192,128]{1,0:T(8,128)S(1)} collective-permute-done((f32[192,128]{1,0:T(8,128)S(1)}, f32[192,128]{1,0:T(8,128)S(1)}, u32[]{:S(2)}, u32[]{:S(2)}) %collective-permute-start.3) | collective-permute-done | bytes 98336 | tf_op jit(solution)/shard_map/ppermute | solution.py:40
  13.8 0.0 collective-permute-done.near_x
  13.8 0.0 collective-permute-done.1.near_y
  13.8 0.1 shard_map.46
  13.9 0.0 copy-start
  14.0 0.3 collective-permute-start.5
  14.3 0.3 collective-permute-start.6
  14.6 3.7 %collective-permute-start.4 = (f32[1344,256]{1,0:T(8,128)S(1)}, f32[1344,256]{1,0:T(8,128)S(1)}, u32[]{:S(2)}, u32[]{:S(2)}) collective-permute-start(f32[1344,256]{1,0:T(8,128)S(1)} %get-tuple-element.18.refs_0_.near.refs_4_), channel_id=1, source_target_pairs={{0,4},{4,0},{8,12},{12,8},{16,20},{20,16},{24,28},{28,24},{1,5},{5... | collective-permute-start | bytes 4128776 | tf_op jit(solution)/shard_map/ppermute | solution.py:40
  18.3 2.2 %collective-permute-start.7 = (f32[192,256]{1,0:T(8,128)S(1)}, f32[192,256]{1,0:T(8,128)S(1)}, u32[]{:S(2)}, u32[]{:S(2)}) collective-permute-start(f32[192,256]{1,0:T(8,128)S(1)} %slice.9), channel_id=1, source_target_pairs={{0,24},{4,28},{8,16},{12,20},{16,8},{20,12},{24,0},{28,4},{1,25},{... | collective-permute-start | bytes 589832 | tf_op jit(solution)/shard_map/ppermute | solution.py:40
  20.6 0.8 %collective-permute-done.5 = f32[384,256]{1,0:T(8,128)S(1)} collective-permute-done((f32[384,256]{1,0:T(8,128)S(1)}, f32[384,256]{1,0:T(8,128)S(1)}, u32[]{:S(2)}, u32[]{:S(2)}) %collective-permute-start.5) | collective-permute-done | bytes 393248 | tf_op jit(solution)/shard_map/ppermute | solution.py:40
  21.4 0.0 collective-permute-done.6
  21.5 4.5 %collective-permute-done.7 = f32[192,256]{1,0:T(8,128)S(1)} collective-permute-done((f32[192,256]{1,0:T(8,128)S(1)}, f32[192,256]{1,0:T(8,128)S(1)}, u32[]{:S(2)}, u32[]{:S(2)}) %collective-permute-start.7) | collective-permute-done | bytes 196640 | tf_op jit(solution)/shard_map/ppermute | solution.py:40
  26.0 4.2 %collective-permute-start.8 = (f32[960,256]{1,0:T(8,128)S(1)}, f32[960,256]{1,0:T(8,128)S(1)}, u32[]{:S(2)}, u32[]{:S(2)}) collective-permute-start(f32[960,256]{1,0:T(8,128)S(1)} %constant_dynamic-update-slice_fusion.2.refs_2_), channel_id=1, source_target_pairs={{0,4},{4,0},{8,12},{12,8},{16,20},{20,16},{24,28},{28,24},{1,5},{5... | collective-permute-start | bytes 2949128 | tf_op jit(solution)/shard_map/ppermute | solution.py:40
  30.2 0.0 copy-done
  30.2 0.4 shard_map.50
  30.6 0.1 collective-permute-start.12
  30.6 2.3 %collective-permute-done.12 = f32[256,384]{1,0:T(8,128)S(1)} collective-permute-done((f32[256,384]{1,0:T(8,128)S(1)}, f32[256,384]{1,0:T(8,128)S(1)}, u32[]{:S(2)}, u32[]{:S(2)}) %collective-permute-start.12) | collective-permute-done | bytes 393248 | tf_op jit(solution)/shard_map/ppermute | solution.py:40
  33.0 1.3 %collective-permute-start.13 = (f32[256,384]{1,0:T(8,128)S(1)}, f32[256,384]{1,0:T(8,128)S(1)}, u32[]{:S(2)}, u32[]{:S(2)}) collective-permute-start(f32[256,384]{1,0:T(8,128)S(1)} %add.6), channel_id=1, source_target_pairs={{0,8},{4,12},{8,0},{12,4},{16,24},{20,28},{24,16},{28,20},{1,9},{5... | collective-permute-start | bytes 1179656 | tf_op jit(solution)/shard_map/ppermute | solution.py:40
  34.2 0.0 collective-permute-done.4.refs_1_
  34.2 0.0 collective-permute-done.8.refs_3_
  34.2 4.4 %shard_map.47 = (f32[192,768]{1,0:T(8,128)S(1)}, f32[192,384]{1,0:T(8,128)S(1)}, f32[192,384]{1,0:T(8,128)S(1)}, f32[192,384]{1,0:T(8,128)S(1)}) custom-call(f32[1344,256]{1,0:T(8,128)S(1)} %get-tuple-element.18.refs_0_.near.refs_4_, f32[1344,256]{1,0:T(8,128)S(1)} %collective-permute-done.4.refs_1_, ...), custom_call_target="tpu_custom_call" | custom-call | flops 2566914048 | bytes 4718592 | tf_op jit(solution)/shard_map/pallas_call | solution.py:235
  38.7 0.1 collective-permute-start.9
  38.8 3.3 %collective-permute-start.10 = (f32[192,384]{1,0:T(8,128)S(1)}, f32[192,384]{1,0:T(8,128)S(1)}, u32[]{:S(2)}, u32[]{:S(2)}) collective-permute-start(f32[192,384]{1,0:T(8,128)S(1)} %get-tuple-element.22), channel_id=1, source_target_pairs={{0,3},{1,2},{2,1},{3,0},{4,7},{5,6},{6,5},{7,4},{8,11},{9,10},{10,... | collective-permute-start | bytes 884744 | tf_op jit(solution)/shard_map/ppermute | solution.py:40
  42.1 0.2 collective-permute-start.11
  42.3 1.1 %collective-permute-done.13 = f32[256,384]{1,0:T(8,128)S(1)} collective-permute-done((f32[256,384]{1,0:T(8,128)S(1)}, f32[256,384]{1,0:T(8,128)S(1)}, u32[]{:S(2)}, u32[]{:S(2)}) %collective-permute-start.13) | collective-permute-done | bytes 393248 | tf_op jit(solution)/shard_map/ppermute | solution.py:40
  43.4 0.9 %collective-permute-start.14 = (f32[128,384]{1,0:T(8,128)S(1)}, f32[128,384]{1,0:T(8,128)S(1)}, u32[]{:S(2)}, u32[]{:S(2)}) collective-permute-start(f32[128,384]{1,0:T(8,128)S(1)} %get-tuple-element.32), channel_id=1, source_target_pairs={{0,16},{4,20},{8,24},{12,28},{16,0},{20,4},{24,8},{28,12},{1,17},{... | collective-permute-start | bytes 589832 | tf_op jit(solution)/shard_map/ppermute | solution.py:40
  44.4 0.6 collective-permute-start.15
  45.0 1.8 %shard_map.48.refs_3_ = f32[192,384]{1,0:T(8,128)S(1)} custom-call(f32[1344,256]{1,0:T(8,128)S(1)} %get-tuple-element.18.refs_0_.near.refs_4_, f32[1344,256]{1,0:T(8,128)S(1)} %collective-permute-done.4.refs_1_, f32[960,256]{1,0:T(8,128)S(1)} %constant_dynamic-update-slice_fusion.2.refs_2_, f32[960,256]{1,0:T(8,128)S(1)} %collective-permute-done.8.refs_3_, ...), custom_call_target="tpu_custom_call" | custom-call | flops 339738624 | bytes 4718592 | tf_op jit(solution)/shard_map/pallas_call | solution.py:235
  46.7 10.4 %collective-permute-done.9.refs_0_ = f32[192,384]{1,0:T(8,128)S(1)} collective-permute-done((f32[192,384]{1,0:T(8,128)S(1)}, f32[192,384]{1,0:T(8,128)S(1)}, u32[]{:S(2)}, u32[]{:S(2)}) %collective-permute-start.9) | collective-permute-done | bytes 294944 | tf_op jit(solution)/shard_map/ppermute | solution.py:40
  57.2 10.4 %collective-permute-done.10.refs_1_ = f32[192,384]{1,0:T(8,128)S(1)} collective-permute-done((f32[192,384]{1,0:T(8,128)S(1)}, f32[192,384]{1,0:T(8,128)S(1)}, u32[]{:S(2)}, u32[]{:S(2)}) %collective-permute-start.10) | collective-permute-done | bytes 294944 | tf_op jit(solution)/shard_map/ppermute | solution.py:40
  67.6 0.0 collective-permute-done.11.refs_2_
  67.6 0.2 shard_map.49.refs_0_
  67.8 0.0 collective-permute-done.14.refs_2_
  67.8 0.0 collective-permute-done.15.refs_3_
  67.8 1.0 %shard_map.51 = f32[192,384]{1,0:T(8,128)} custom-call(f32[192,384]{1,0:T(8,128)S(1)} %shard_map.49.refs_0_, f32[256,384]{1,0:T(8,128)S(1)} %add.7.refs_1_, f32[128,384]{1,0:T(8,128)S(1)} %collective-permute-done.14.refs_2_, f32[128,384]{1,0:T(8,128)S(1)} %collective-permute-done.15.refs_3_, f32[1344,256]{1,0:T(8,128)S(1)} %get-tuple-element.18.refs_0_.near.refs_4_), custom_call_target="tpu_custom_call" | custom-call | flops 113246208 | bytes 786432 | tf_op jit(solution)/shard_map/pallas_call | solution.py:235
  (7 shorter events, 0.2 us)
Async XLA Ops:
  1.9 11.9 %collective-permute-start = (f32[384,256]{1,0:T(8,128)S(1)}, f32[384,256]{1,0:T(8,128)S(1)}, u32[]{:S(2)}, u32[]{:S(2)}) collective-permute-start(f32[384,256]{1,0:T(8,128)S(1)} %constant_dynamic-update-slice_fusion.panels), channel_id=1, source_target_pairs={{0,8},{4,12},{8,0},{12,4},{16,24},{20,28},{24,16},{28,20},{1,9},{5... | collective-permute-start | bytes 1179656 | tf_op jit(solution)/shard_map/ppermute | solution.py:40
  3.2 10.6 %collective-permute-start.1 = (f32[384,256]{1,0:T(8,128)S(1)}, f32[384,256]{1,0:T(8,128)S(1)}, u32[]{:S(2)}, u32[]{:S(2)}) collective-permute-start(f32[384,256]{1,0:T(8,128)S(1)} %constant_dynamic-update-slice_fusion.panels), channel_id=1, source_target_pairs={{0,16},{4,20},{8,24},{12,28},{16,0},{20,4},{24,8},{28,12},{1,17},{... | collective-permute-start | bytes 1179656 | tf_op jit(solution)/shard_map/ppermute | solution.py:40
  5.3 3.8 %collective-permute-start.2 = (f32[192,64]{1,0:T(8,128)S(1)}, f32[192,64]{1,0:T(8,128)S(1)}, u32[]{:S(2)}, u32[]{:S(2)}) collective-permute-start(f32[192,64]{1,0:T(8,128)S(1)} %copy.6), channel_id=1, source_target_pairs={{0,1},{1,0},{2,3},{3,2},{4,5},{5,4},{6,7},{7,6},{8,9},{9,8},{10,11... | collective-permute-start | bytes 147464 | tf_op jit(solution)/shard_map/ppermute | solution.py:40
  9.3 4.5 %collective-permute-start.3 = (f32[192,128]{1,0:T(8,128)S(1)}, f32[192,128]{1,0:T(8,128)S(1)}, u32[]{:S(2)}, u32[]{:S(2)}) collective-permute-start(f32[192,128]{1,0:T(8,128)S(1)} %pad_maximum_fusion.refs_0_), channel_id=1, source_target_pairs={{0,2},{1,3},{2,0},{3,1},{4,6},{5,7},{6,4},{7,5},{8,10},{9,11},{10,... | collective-permute-start | bytes 294920 | tf_op jit(solution)/shard_map/ppermute | solution.py:40
  13.9 16.2 %copy-start = (f32[192,384]{1,0:T(8,128)S(1)}, f32[192,384]{1,0:T(8,128)}, u32[]{:S(2)}) copy-start(f32[192,384]{1,0:T(8,128)} %matrix.1) | copy-start | bytes 884740
  14.0 7.4 %collective-permute-start.5 = (f32[384,256]{1,0:T(8,128)S(1)}, f32[384,256]{1,0:T(8,128)S(1)}, u32[]{:S(2)}, u32[]{:S(2)}) collective-permute-start(f32[384,256]{1,0:T(8,128)S(1)} %get-tuple-element.19), channel_id=1, source_target_pairs={{0,8},{4,12},{8,0},{12,4},{16,24},{20,28},{24,16},{28,20},{1,9},{5... | collective-permute-start | bytes 1179656 | tf_op jit(solution)/shard_map/ppermute | solution.py:40
  14.3 7.1 %collective-permute-start.6 = (f32[384,256]{1,0:T(8,128)S(1)}, f32[384,256]{1,0:T(8,128)S(1)}, u32[]{:S(2)}, u32[]{:S(2)}) collective-permute-start(f32[384,256]{1,0:T(8,128)S(1)} %get-tuple-element.20), channel_id=1, source_target_pairs={{0,16},{4,20},{8,24},{12,28},{16,0},{20,4},{24,8},{28,12},{1,17},{... | collective-permute-start | bytes 1179656 | tf_op jit(solution)/shard_map/ppermute | solution.py:40
  14.6 19.6 %collective-permute-start.4 = (f32[1344,256]{1,0:T(8,128)S(1)}, f32[1344,256]{1,0:T(8,128)S(1)}, u32[]{:S(2)}, u32[]{:S(2)}) collective-permute-start(f32[1344,256]{1,0:T(8,128)S(1)} %get-tuple-element.18.refs_0_.near.refs_4_), channel_id=1, source_target_pairs={{0,4},{4,0},{8,12},{12,8},{16,20},{20,16},{24,28},{28,24},{1,5},{5... | collective-permute-start | bytes 4128776 | tf_op jit(solution)/shard_map/ppermute | solution.py:40
  18.3 7.7 %collective-permute-start.7 = (f32[192,256]{1,0:T(8,128)S(1)}, f32[192,256]{1,0:T(8,128)S(1)}, u32[]{:S(2)}, u32[]{:S(2)}) collective-permute-start(f32[192,256]{1,0:T(8,128)S(1)} %slice.9), channel_id=1, source_target_pairs={{0,24},{4,28},{8,16},{12,20},{16,8},{20,12},{24,0},{28,4},{1,25},{... | collective-permute-start | bytes 589832 | tf_op jit(solution)/shard_map/ppermute | solution.py:40
  26.0 8.2 %collective-permute-start.8 = (f32[960,256]{1,0:T(8,128)S(1)}, f32[960,256]{1,0:T(8,128)S(1)}, u32[]{:S(2)}, u32[]{:S(2)}) collective-permute-start(f32[960,256]{1,0:T(8,128)S(1)} %constant_dynamic-update-slice_fusion.2.refs_2_), channel_id=1, source_target_pairs={{0,4},{4,0},{8,12},{12,8},{16,20},{20,16},{24,28},{28,24},{1,5},{5... | collective-permute-start | bytes 2949128 | tf_op jit(solution)/shard_map/ppermute | solution.py:40
  30.6 2.4 %collective-permute-start.12 = (f32[256,384]{1,0:T(8,128)S(1)}, f32[256,384]{1,0:T(8,128)S(1)}, u32[]{:S(2)}, u32[]{:S(2)}) collective-permute-start(f32[256,384]{1,0:T(8,128)S(1)} %shard_map.50), channel_id=1, source_target_pairs={{0,4},{4,0},{8,12},{12,8},{16,20},{20,16},{24,28},{28,24},{1,5},{5... | collective-permute-start | bytes 1179656 | tf_op jit(solution)/shard_map/ppermute | solution.py:40
  33.0 10.4 %collective-permute-start.13 = (f32[256,384]{1,0:T(8,128)S(1)}, f32[256,384]{1,0:T(8,128)S(1)}, u32[]{:S(2)}, u32[]{:S(2)}) collective-permute-start(f32[256,384]{1,0:T(8,128)S(1)} %add.6), channel_id=1, source_target_pairs={{0,8},{4,12},{8,0},{12,4},{16,24},{20,28},{24,16},{28,20},{1,9},{5... | collective-permute-start | bytes 1179656 | tf_op jit(solution)/shard_map/ppermute | solution.py:40
  38.7 18.5 %collective-permute-start.9 = (f32[192,384]{1,0:T(8,128)S(1)}, f32[192,384]{1,0:T(8,128)S(1)}, u32[]{:S(2)}, u32[]{:S(2)}) collective-permute-start(f32[192,384]{1,0:T(8,128)S(1)} %get-tuple-element.21), channel_id=1, source_target_pairs={{0,2},{1,3},{2,0},{3,1},{4,6},{5,7},{6,4},{7,5},{8,10},{9,11},{10,... | collective-permute-start | bytes 884744 | tf_op jit(solution)/shard_map/ppermute | solution.py:40
  38.8 28.8 %collective-permute-start.10 = (f32[192,384]{1,0:T(8,128)S(1)}, f32[192,384]{1,0:T(8,128)S(1)}, u32[]{:S(2)}, u32[]{:S(2)}) collective-permute-start(f32[192,384]{1,0:T(8,128)S(1)} %get-tuple-element.22), channel_id=1, source_target_pairs={{0,3},{1,2},{2,1},{3,0},{4,7},{5,6},{6,5},{7,4},{8,11},{9,10},{10,... | collective-permute-start | bytes 884744 | tf_op jit(solution)/shard_map/ppermute | solution.py:40
  42.1 25.5 %collective-permute-start.11 = (f32[192,384]{1,0:T(8,128)S(1)}, f32[192,384]{1,0:T(8,128)S(1)}, u32[]{:S(2)}, u32[]{:S(2)}) collective-permute-start(f32[192,384]{1,0:T(8,128)S(1)} %get-tuple-element.23), channel_id=1, source_target_pairs={{0,1},{1,0},{2,3},{3,2},{4,5},{5,4},{6,7},{7,6},{8,9},{9,8},{10,11... | collective-permute-start | bytes 884744 | tf_op jit(solution)/shard_map/ppermute | solution.py:40
  43.4 24.4 %collective-permute-start.14 = (f32[128,384]{1,0:T(8,128)S(1)}, f32[128,384]{1,0:T(8,128)S(1)}, u32[]{:S(2)}, u32[]{:S(2)}) collective-permute-start(f32[128,384]{1,0:T(8,128)S(1)} %get-tuple-element.32), channel_id=1, source_target_pairs={{0,16},{4,20},{8,24},{12,28},{16,0},{20,4},{24,8},{28,12},{1,17},{... | collective-permute-start | bytes 589832 | tf_op jit(solution)/shard_map/ppermute | solution.py:40
  44.4 23.4 %collective-permute-start.15 = (f32[128,384]{1,0:T(8,128)S(1)}, f32[128,384]{1,0:T(8,128)S(1)}, u32[]{:S(2)}, u32[]{:S(2)}) collective-permute-start(f32[128,384]{1,0:T(8,128)S(1)} %get-tuple-element.31), channel_id=1, source_target_pairs={{0,16},{4,20},{8,24},{12,28},{16,0},{20,4},{24,8},{28,12},{1,17},{... | collective-permute-start | bytes 589832 | tf_op jit(solution)/shard_map/ppermute | solution.py:40

commit v4 on v3

--- a/solution.py
+++ b/solution.py
@@ -52,45 +52,55 @@
     return jnp.concatenate(parts, axis=0)
 
 
-def pack_kernel(panels, near_x, near_y, *refs):
+def pack_kernel(left_x, right_x, left_y, right_y, *refs):
     *parts, by_x, by_y, near = refs
-    height = panels.shape[0] // 2
-    at = 0
-    for part in parts:
-        near[:height, at : at + part.shape[1]] = part[...]
-        at += part.shape[1]
-    for n, value in enumerate((panels, near_x, near_y)):
-        near[(2 * n + 1) * height : (2 * n + 3) * height, :] = value[...]
-    by_x[:height, :] = near_y[:height, :]
+    height = left_x.shape[0]
+    near[:height, :] = jnp.concatenate([part[...] for part in parts], axis=0).T
+    for n, value in enumerate((left_x, right_x, left_y, right_y)):
+        near[(n + 1) * height : (n + 2) * height, :] = value[...]
+    by_x[:height, :] = left_y[...]
     by_x[height:, :] = near[:height, :]
-    by_y[:height, :] = near_x[height:, :]
+    by_y[:height, :] = right_x[...]
     by_y[height:, :] = near[:height, :]
 
 
-def gather_square(panels, refl_parts, height):
-    near_x, near_y = swap(panels, "row", 2), swap(panels, "row", 4)
-    width = panels.shape[1]
+def gather_square(left_panel, right_panel, refl_parts, matrix):
+    height, width = left_panel.shape
+    wide = matrix.shape[1]
+    near = [swap(panel, "row", bits) for bits in (2, 4) for panel in (left_panel, right_panel)]
     by_x, by_y, near = run_kernel(
         pack_kernel,
-        [(2 * height, width)] * 2 + [(7 * height, width)],
-        [panels, near_x, near_y, *refl_parts],
+        [(2 * height, width)] * 2 + [(5 * height, width)],
+        [*near, *refl_parts],
         (),
         0,
         72 * height * width,
     )
     far = swap(near[:height], "row", 6)
     by_x, by_y = swap(by_x, "row", 2), swap(by_y, "row", 4)
-    last = stack(by_x, by_y, far)
-    near_at = ((0, 2), (0, 0), (0, 1), (2, 0), (2, 1), (4, 0), (4, 1))
+    (sides,) = run_kernel(
+        sides_kernel,
+        [(width, wide)],
+        [near, matrix],
+        (),
+        6 * height * width * wide,
+        4 * height * (width + wide),
+    )
+    sides = sides + swap(sides, "row", 1)
+    panels = stack(left_panel, right_panel)
+    across_own = swap(panels, "row", 1)
+    last, across_own = lax.optimization_barrier((stack(by_x, by_y, far), across_own))
+    own_at = ((0, 0), (0, 1))
+    near_at = ((0, 2), (2, 0), (2, 1), (4, 0), (4, 1))
     last_at = ((6, 0), (2, 2), (6, 1), (4, 2), (6, 2))
 
     def across(places):
         return tuple((index + 1, kind) for index, kind in places)
 
-    found = []
+    found = [(panels, own_at), (across_own, across(own_at))]
     for value, places in ((near, near_at), (last, last_at)):
         found += [(value, places), (swap(value, "row", 1), across(places))]
-    return found, near, by_x
+    return found, near, sides, by_x
 
 
 def core_sum(value):
@@ -162,7 +172,7 @@
     panels = (high[:, : 2 * share], low[:, : 2 * share])
     refl = (high[:, 2 * share :], low[:, 2 * share :])
     mixed_pair = halves(pair_dot(refl, panels, DOWN))
-    left_panel, right_panel = (in_refs[0][n * height : (n + 1) * height, :] for n in (1, 2))
+    left_panel, right_panel = in_refs[0][:height, :], in_refs[0][height:, :]
     own_refl = (high[:height, 2 * share :], low[:height, 2 * share :])
     spread = pair_dot(own_refl, mixed_pair, OVER)
     turned = halves(jnp.concatenate([right_panel, -left_panel], axis=1))
@@ -286,22 +296,13 @@
     per = rows // cols
     height, share = left_panel.shape
     wide = per * height
-    refl_parts, bit = [reflectors], 1
+    refl_parts, bit = [reflectors.T], 1
     while bit < cols:
-        known = jnp.concatenate(refl_parts, axis=1)
+        known = jnp.concatenate(refl_parts, axis=0)
         refl_parts = [known, swap(known, "col", bit)]
         bit *= 2
-    found, near, by_x = gather_square(stack(left_panel, right_panel), refl_parts, height)
+    found, near, sides, by_x = gather_square(left_panel, right_panel, refl_parts, matrix)
     width = share
-    (sides,) = run_kernel(
-        sides_kernel,
-        [(width, wide)],
-        [near, matrix],
-        (),
-        6 * height * width * wide,
-        4 * height * (width + wide),
-    )
-    sides = sides + swap(sides, "row", 1)
     sides, _ = lax.optimization_barrier((sides, by_x))
     beside = swap(sides, "row", 2)
 
@@ -337,7 +338,7 @@
         [*received, base],
         [block],
         height * wide * cols,
-        4 * height * wide * (cols + 1),
+        16 * height * wide * (cols + 1),
     )
     summed, parts = lax.optimization_barrier((summed, parts))
     (updated,) = run_kernel(

time: 69.1 us -> 67.3 us (0.974)
  starting transfers between devices: 21.2 us -> 18.9 us
  local copies, waits for them, and re-layouts: 2.93 us -> 0.68 us
  waiting for transfers between devices: 36.4 us -> 38.4 us
  other arithmetic: 0.17 us -> 1 us
    ppermute x16 -> x19, starting transfers between devices: 21.2 us -> 18.9 us  [swap(): return lax.ppermute(value, axis, [(i, i ^ offset) for i in range(size)])]
    ppermute x16 -> x19, waiting for transfers between devices: 36.4 us -> 38.4 us  [swap(): return lax.ppermute(value, axis, [(i, i ^ offset) for i in range(size)])]
    unnamed x6 -> x7, local copies, waits for them, and re-layouts: 1.93 us -> 0.63 us
    concatenate x2 -> x1, local copies, waits for them, and re-layouts: 0.96 us -> 0.01 us  [stack(): return jnp.concatenate(parts, axis=0)]
    concatenate x1 -> x2, other arithmetic: 0.09 us -> 0.91 us  [the longest x1 0.85 us: local_square(): known = jnp.concatenate(refl_parts, axis=0)]
  transfers between devices with their start and end apart: 16 -> 19, of which waited for: 8 -> 8; matrix products, arithmetic and copies ran while one was open for 2% -> 2% of each run, Pallas kernels for 10% -> 10%
where the time goes in v4:
time: 67.3 us; the launch traced here: 67.2 us
  waiting for transfers between devices  38.4 us (57%)
  starting transfers between devices  18.9 us (28%)
  Pallas kernels  7.98 us (12%)
  other arithmetic  1 us (1%)
  local copies, waits for them, and re-layouts  0.68 us (1%)
    ppermute x19, waiting for transfers between devices, swap(): return lax.ppermute(value, axis, [(i, i ^ offset) for i in range(size)])  38.4 us
    ppermute x19, starting transfers between devices, swap(): return lax.ppermute(value, axis, [(i, i ^ offset) for i in range(size)])  18.9 us
    pallas_call x6, Pallas kernels, run_kernel(): pl.pallas_call(body, out_shape=[jax.ShapeDtypeStruct(shape, jnp.float32)...  7.98 us
  transfers between devices with their start and end apart: 19, of which 8 were waited for; matrix products, arithmetic and copies ran while one was open for 2% of the time, Pallas kernels for 10%

profile of v4, /device:TPU:17, one launch (start us, length us, event | category | flops | bytes accessed | tf_op | source)
XLA Modules:
  0.0 67.2 jit_solution(5441548872774865457)
XLA Ops:
  0.0 1.3 %collective-permute-start.4 = (f32[64,192]{1,0:T(8,128)}, f32[64,192]{1,0:T(8,128)S(1)}, u32[]{:S(2)}, u32[]{:S(2)}) collective-permute-start(f32[64,192]{1,0:T(8,128)} %bitcast.1), channel_id=1, source_target_pairs={{0,1},{1,0},{2,3},{3,2},{4,5},{5,4},{6,7},{7,6},{8,9},{9,8},{10,11... | collective-permute-start | bytes 147464 | tf_op jit(solution)/shard_map/ppermute | solution.py:40
  1.3 1.2 %collective-permute-start = (f32[192,256]{1,0:T(8,128)}, f32[192,256]{1,0:T(8,128)S(1)}, u32[]{:S(2)}, u32[]{:S(2)}) collective-permute-start(f32[192,256]{1,0:T(8,128)} %param.5), channel_id=1, source_target_pairs={{0,8},{4,12},{8,0},{12,4},{16,24},{20,28},{24,16},{28,20},{1,9},{5... | collective-permute-start | bytes 589832 | tf_op jit(solution)/shard_map/ppermute | solution.py:40
  2.5 1.2 %collective-permute-start.2 = (f32[192,256]{1,0:T(8,128)}, f32[192,256]{1,0:T(8,128)S(1)}, u32[]{:S(2)}, u32[]{:S(2)}) collective-permute-start(f32[192,256]{1,0:T(8,128)} %param.5), channel_id=1, source_target_pairs={{0,16},{4,20},{8,24},{12,28},{16,0},{20,4},{24,8},{28,12},{1,17},{... | collective-permute-start | bytes 589832 | tf_op jit(solution)/shard_map/ppermute | solution.py:40
  3.7 0.3 collective-permute-start.1
  4.0 0.2 collective-permute-start.3
  4.2 0.0 collective-permute-done.4
  4.2 0.8 %pad_maximum_fusion.1.refs_0_ = f32[128,192]{1,0:T(8,128)S(1)} fusion(f32[64,192]{1,0:T(8,128)S(1)} %collective-permute-done.4, f32[64,192]{1,0:T(8,128)} %bitcast.2), kind=kLoop, calls=%fused_computation.1 | loop fusion | flops 24576 | bytes 196608 | tf_op jit(solution)/shard_map/concatenate | solution.py:301
  5.1 0.0 copy-start.1
  5.1 0.1 collective-permute-start.5
  5.2 4.8 %collective-permute-done.5.refs_1_ = f32[128,192]{1,0:T(8,128)S(1)} collective-permute-done((f32[128,192]{1,0:T(8,128)S(1)}, f32[128,192]{1,0:T(8,128)S(1)}, u32[]{:S(2)}, u32[]{:S(2)}) %collective-permute-start.5) | collective-permute-done | bytes 98336 | tf_op jit(solution)/shard_map/ppermute | solution.py:40
  10.1 0.0 collective-permute-done.left_x
  10.1 1.1 %collective-permute-done.1.right_x = f32[192,256]{1,0:T(8,128)S(1)} collective-permute-done((f32[192,256]{1,0:T(8,128)}, f32[192,256]{1,0:T(8,128)S(1)}, u32[]{:S(2)}, u32[]{:S(2)}) %collective-permute-start.1) | collective-permute-done | bytes 196640 | tf_op jit(solution)/shard_map/ppermute | solution.py:40
  11.2 0.0 collective-permute-done.2.left_y
  11.2 0.9 %collective-permute-done.3.right_y = f32[192,256]{1,0:T(8,128)S(1)} collective-permute-done((f32[192,256]{1,0:T(8,128)}, f32[192,256]{1,0:T(8,128)S(1)}, u32[]{:S(2)}, u32[]{:S(2)}) %collective-permute-start.3) | collective-permute-done | bytes 196640 | tf_op jit(solution)/shard_map/ppermute | solution.py:40
  12.1 0.1 shard_map.46
  12.2 1.3 %collective-permute-start.7 = (f32[384,256]{1,0:T(8,128)S(1)}, f32[384,256]{1,0:T(8,128)S(1)}, u32[]{:S(2)}, u32[]{:S(2)}) collective-permute-start(f32[384,256]{1,0:T(8,128)S(1)} %get-tuple-element.21), channel_id=1, source_target_pairs={{0,16},{4,20},{8,24},{12,28},{16,0},{20,4},{24,8},{28,12},{1,17},{... | collective-permute-start | bytes 1179656 | tf_op jit(solution)/shard_map/ppermute | solution.py:40
  13.5 0.3 collective-permute-start.6
  13.9 0.6 copy-done.2
  14.5 2.5 %collective-permute-start.9 = (f32[384,256]{1,0:T(8,128)S(1)}, f32[384,256]{1,0:T(8,128)S(1)}, u32[]{:S(2)}, u32[]{:S(2)}) collective-permute-start(f32[384,256]{1,0:T(8,128)S(1)} %constant_dynamic-update-slice_fusion.refs_0_), channel_id=1, source_target_pairs={{0,4},{4,0},{8,12},{12,8},{16,20},{20,16},{24,28},{28,24},{1,5},{5... | collective-permute-start | bytes 1179656 | tf_op jit(solution)/shard_map/ppermute | solution.py:40
  17.0 0.0 copy-start
  17.0 0.9 %collective-permute-start.8 = (f32[192,256]{1,0:T(8,128)S(1)}, f32[192,256]{1,0:T(8,128)S(1)}, u32[]{:S(2)}, u32[]{:S(2)}) collective-permute-start(f32[192,256]{1,0:T(8,128)S(1)} %slice.9), channel_id=1, source_target_pairs={{0,24},{4,28},{8,16},{12,20},{16,8},{20,12},{24,0},{28,4},{1,25},{... | collective-permute-start | bytes 589832 | tf_op jit(solution)/shard_map/ppermute | solution.py:40
  17.9 0.3 collective-permute-start.10
  18.2 7.4 %collective-permute-done.8 = f32[192,256]{1,0:T(8,128)S(1)} collective-permute-done((f32[192,256]{1,0:T(8,128)S(1)}, f32[192,256]{1,0:T(8,128)S(1)}, u32[]{:S(2)}, u32[]{:S(2)}) %collective-permute-start.8) | collective-permute-done | bytes 196640 | tf_op jit(solution)/shard_map/ppermute | solution.py:40
  25.6 0.0 collective-permute-done.7
  25.6 0.0 collective-permute-done.6
  25.6 0.1 pad_maximum_fusion.refs_4_
  25.6 0.0 collective-permute-done.9.refs_1_
  25.7 3.7 %collective-permute-start.11 = (f32[960,256]{1,0:T(8,128)S(1)}, f32[960,256]{1,0:T(8,128)S(1)}, u32[]{:S(2)}, u32[]{:S(2)}) collective-permute-start(f32[960,256]{1,0:T(8,128)S(1)} %pad_maximum_fusion.refs_4_), channel_id=1, source_target_pairs={{0,4},{4,0},{8,12},{12,8},{16,20},{20,16},{24,28},{28,24},{1,5},{5... | collective-permute-start | bytes 2949128 | tf_op jit(solution)/shard_map/ppermute | solution.py:40
  29.4 0.4 shard_map.50
  29.8 0.1 collective-permute-start.15
  29.9 2.3 %collective-permute-done.15 = f32[256,384]{1,0:T(8,128)S(1)} collective-permute-done((f32[256,384]{1,0:T(8,128)S(1)}, f32[256,384]{1,0:T(8,128)S(1)}, u32[]{:S(2)}, u32[]{:S(2)}) %collective-permute-start.15) | collective-permute-done | bytes 393248 | tf_op jit(solution)/shard_map/ppermute | solution.py:40
  32.2 0.4 collective-permute-start.16
  32.6 0.0 collective-permute-done.10.refs_3_
  32.6 0.0 collective-permute-done.11.refs_5_
  32.6 4.4 %shard_map.47 = (f32[192,768]{1,0:T(8,128)S(1)}, f32[192,384]{1,0:T(8,128)S(1)}, f32[192,384]{1,0:T(8,128)S(1)}, f32[192,384]{1,0:T(8,128)S(1)}) custom-call(f32[384,256]{1,0:T(8,128)S(1)} %constant_dynamic-update-slice_fusion.refs_0_, f32[384,256]{1,0:T(8,128)S(1)} %collective-permute-done.9.refs_1_, f32[960,256]{1,0:T(8,128)S(1)} %get-tuple-element.22.refs_2_.near.refs_4_, ...), custom_call_target="tpu_custom_call" | custom-call | flops 2566914048 | bytes 4718592 | tf_op jit(solution)/shard_map/pallas_call | solution.py:245
  37.0 2.2 %collective-permute-start.12 = (f32[192,384]{1,0:T(8,128)S(1)}, f32[192,384]{1,0:T(8,128)S(1)}, u32[]{:S(2)}, u32[]{:S(2)}) collective-permute-start(f32[192,384]{1,0:T(8,128)S(1)} %get-tuple-element.25), channel_id=1, source_target_pairs={{0,2},{1,3},{2,0},{3,1},{4,6},{5,7},{6,4},{7,5},{8,10},{9,11},{10,... | collective-permute-start | bytes 884744 | tf_op jit(solution)/shard_map/ppermute | solution.py:40
  39.2 0.3 collective-permute-start.13
  39.5 1.1 %collective-permute-start.14 = (f32[192,384]{1,0:T(8,128)S(1)}, f32[192,384]{1,0:T(8,128)S(1)}, u32[]{:S(2)}, u32[]{:S(2)}) collective-permute-start(f32[192,384]{1,0:T(8,128)S(1)} %get-tuple-element.27), channel_id=1, source_target_pairs={{0,1},{1,0},{2,3},{3,2},{4,5},{5,4},{6,7},{7,6},{8,9},{9,8},{10,11... | collective-permute-start | bytes 884744 | tf_op jit(solution)/shard_map/ppermute | solution.py:40
  40.6 2.0 %collective-permute-done.16 = f32[256,384]{1,0:T(8,128)S(1)} collective-permute-done((f32[256,384]{1,0:T(8,128)S(1)}, f32[256,384]{1,0:T(8,128)S(1)}, u32[]{:S(2)}, u32[]{:S(2)}) %collective-permute-start.16) | collective-permute-done | bytes 393248 | tf_op jit(solution)/shard_map/ppermute | solution.py:40
  42.7 1.3 %collective-permute-start.17 = (f32[128,384]{1,0:T(8,128)S(1)}, f32[128,384]{1,0:T(8,128)S(1)}, u32[]{:S(2)}, u32[]{:S(2)}) collective-permute-start(f32[128,384]{1,0:T(8,128)S(1)} %get-tuple-element.36), channel_id=1, source_target_pairs={{0,16},{4,20},{8,24},{12,28},{16,0},{20,4},{24,8},{28,12},{1,17},{... | collective-permute-start | bytes 589832 | tf_op jit(solution)/shard_map/ppermute | solution.py:40
  44.0 0.2 collective-permute-start.18
  44.2 1.8 %shard_map.48.refs_3_ = f32[192,384]{1,0:T(8,128)S(1)} custom-call(f32[384,256]{1,0:T(8,128)S(1)} %constant_dynamic-update-slice_fusion.refs_0_, f32[384,256]{1,0:T(8,128)S(1)} %collective-permute-done.9.refs_1_, f32[960,256]{1,0:T(8,128)S(1)} %get-tuple-element.22.refs_2_.near.refs_4_, f32[960,256]{1,0:T(8,128)S(1)} %collective-permute-done.10.refs_3_, ...), custom_call_target="tpu_custom_call" | custom-call | flops 339738624 | bytes 4718592 | tf_op jit(solution)/shard_map/pallas_call | solution.py:245
  46.0 11.5 %collective-permute-done.12.refs_0_ = f32[192,384]{1,0:T(8,128)S(1)} collective-permute-done((f32[192,384]{1,0:T(8,128)S(1)}, f32[192,384]{1,0:T(8,128)S(1)}, u32[]{:S(2)}, u32[]{:S(2)}) %collective-permute-start.12) | collective-permute-done | bytes 294944 | tf_op jit(solution)/shard_map/ppermute | solution.py:40
  57.4 8.5 %collective-permute-done.13.refs_1_ = f32[192,384]{1,0:T(8,128)S(1)} collective-permute-done((f32[192,384]{1,0:T(8,128)S(1)}, f32[192,384]{1,0:T(8,128)S(1)}, u32[]{:S(2)}, u32[]{:S(2)}) %collective-permute-start.13) | collective-permute-done | bytes 294944 | tf_op jit(solution)/shard_map/ppermute | solution.py:40
  65.9 0.0 collective-permute-done.14.refs_2_
  65.9 0.2 shard_map.49.refs_0_
  66.1 0.0 collective-permute-done.17.refs_2_
  66.1 1.0 %shard_map.51 = f32[192,384]{1,0:T(8,128)} custom-call(f32[192,384]{1,0:T(8,128)S(1)} %shard_map.49.refs_0_, f32[256,384]{1,0:T(8,128)S(1)} %add.7.refs_1_, f32[128,384]{1,0:T(8,128)S(1)} %collective-permute-done.17.refs_2_, f32[128,384]{1,0:T(8,128)S(1)} %collective-permute-done.18.refs_3_, f32[960,256]{1,0:T(8,128)S(1)} %get-tuple-element.22.refs_2_.near.refs_4_), custom_call_target="tpu_custom_call" | custom-call | flops 113246208 | bytes 786432 | tf_op jit(solution)/shard_map/pallas_call | solution.py:245
  (10 shorter events, 0.2 us)
Async XLA Ops:
  0.0 4.2 %collective-permute-start.4 = (f32[64,192]{1,0:T(8,128)}, f32[64,192]{1,0:T(8,128)S(1)}, u32[]{:S(2)}, u32[]{:S(2)}) collective-permute-start(f32[64,192]{1,0:T(8,128)} %bitcast.1), channel_id=1, source_target_pairs={{0,1},{1,0},{2,3},{3,2},{4,5},{5,4},{6,7},{7,6},{8,9},{9,8},{10,11... | collective-permute-start | bytes 147464 | tf_op jit(solution)/shard_map/ppermute | solution.py:40
  1.3 8.8 %collective-permute-start = (f32[192,256]{1,0:T(8,128)}, f32[192,256]{1,0:T(8,128)S(1)}, u32[]{:S(2)}, u32[]{:S(2)}) collective-permute-start(f32[192,256]{1,0:T(8,128)} %param.5), channel_id=1, source_target_pairs={{0,8},{4,12},{8,0},{12,4},{16,24},{20,28},{24,16},{28,20},{1,9},{5... | collective-permute-start | bytes 589832 | tf_op jit(solution)/shard_map/ppermute | solution.py:40
  2.5 8.7 %collective-permute-start.2 = (f32[192,256]{1,0:T(8,128)}, f32[192,256]{1,0:T(8,128)S(1)}, u32[]{:S(2)}, u32[]{:S(2)}) collective-permute-start(f32[192,256]{1,0:T(8,128)} %param.5), channel_id=1, source_target_pairs={{0,16},{4,20},{8,24},{12,28},{16,0},{20,4},{24,8},{28,12},{1,17},{... | collective-permute-start | bytes 589832 | tf_op jit(solution)/shard_map/ppermute | solution.py:40
  3.7 7.4 %collective-permute-start.1 = (f32[192,256]{1,0:T(8,128)}, f32[192,256]{1,0:T(8,128)S(1)}, u32[]{:S(2)}, u32[]{:S(2)}) collective-permute-start(f32[192,256]{1,0:T(8,128)} %param.6), channel_id=1, source_target_pairs={{0,8},{4,12},{8,0},{12,4},{16,24},{20,28},{24,16},{28,20},{1,9},{5... | collective-permute-start | bytes 589832 | tf_op jit(solution)/shard_map/ppermute | solution.py:40
  4.0 8.1 %collective-permute-start.3 = (f32[192,256]{1,0:T(8,128)}, f32[192,256]{1,0:T(8,128)S(1)}, u32[]{:S(2)}, u32[]{:S(2)}) collective-permute-start(f32[192,256]{1,0:T(8,128)} %param.6), channel_id=1, source_target_pairs={{0,16},{4,20},{8,24},{12,28},{16,0},{20,4},{24,8},{28,12},{1,17},{... | collective-permute-start | bytes 589832 | tf_op jit(solution)/shard_map/ppermute | solution.py:40
  5.1 8.8 %copy-start.1 = (f32[192,256]{1,0:T(8,128)S(1)}, f32[192,256]{1,0:T(8,128)}, u32[]{:S(2)}) copy-start(f32[192,256]{1,0:T(8,128)} %param.5) | copy-start | bytes 589828
  5.1 5.0 %collective-permute-start.5 = (f32[128,192]{1,0:T(8,128)S(1)}, f32[128,192]{1,0:T(8,128)S(1)}, u32[]{:S(2)}, u32[]{:S(2)}) collective-permute-start(f32[128,192]{1,0:T(8,128)S(1)} %pad_maximum_fusion.1.refs_0_), channel_id=1, source_target_pairs={{0,2},{1,3},{2,0},{3,1},{4,6},{5,7},{6,4},{7,5},{8,10},{9,11},{10,... | collective-permute-start | bytes 294920 | tf_op jit(solution)/shard_map/ppermute | solution.py:40
  12.2 13.3 %collective-permute-start.7 = (f32[384,256]{1,0:T(8,128)S(1)}, f32[384,256]{1,0:T(8,128)S(1)}, u32[]{:S(2)}, u32[]{:S(2)}) collective-permute-start(f32[384,256]{1,0:T(8,128)S(1)} %get-tuple-element.21), channel_id=1, source_target_pairs={{0,16},{4,20},{8,24},{12,28},{16,0},{20,4},{24,8},{28,12},{1,17},{... | collective-permute-start | bytes 1179656 | tf_op jit(solution)/shard_map/ppermute | solution.py:40
  13.5 0.9 %copy-start.2 = (f32[192,256]{1,0:T(8,128)S(1)}, f32[192,256]{1,0:T(8,128)}, u32[]{:S(2)}) copy-start(f32[192,256]{1,0:T(8,128)} %param.6) | copy-start | bytes 589828
  13.5 12.0 %collective-permute-start.6 = (f32[384,256]{1,0:T(8,128)S(1)}, f32[384,256]{1,0:T(8,128)S(1)}, u32[]{:S(2)}, u32[]{:S(2)}) collective-permute-start(f32[384,256]{1,0:T(8,128)S(1)} %get-tuple-element.20), channel_id=1, source_target_pairs={{0,8},{4,12},{8,0},{12,4},{16,24},{20,28},{24,16},{28,20},{1,9},{5... | collective-permute-start | bytes 1179656 | tf_op jit(solution)/shard_map/ppermute | solution.py:40
  14.5 11.2 %collective-permute-start.9 = (f32[384,256]{1,0:T(8,128)S(1)}, f32[384,256]{1,0:T(8,128)S(1)}, u32[]{:S(2)}, u32[]{:S(2)}) collective-permute-start(f32[384,256]{1,0:T(8,128)S(1)} %constant_dynamic-update-slice_fusion.refs_0_), channel_id=1, source_target_pairs={{0,4},{4,0},{8,12},{12,8},{16,20},{20,16},{24,28},{28,24},{1,5},{5... | collective-permute-start | bytes 1179656 | tf_op jit(solution)/shard_map/ppermute | solution.py:40
  17.0 12.4 %copy-start = (f32[192,384]{1,0:T(8,128)S(1)}, f32[192,384]{1,0:T(8,128)}, u32[]{:S(2)}) copy-start(f32[192,384]{1,0:T(8,128)} %matrix.1) | copy-start | bytes 884740
  17.0 8.6 %collective-permute-start.8 = (f32[192,256]{1,0:T(8,128)S(1)}, f32[192,256]{1,0:T(8,128)S(1)}, u32[]{:S(2)}, u32[]{:S(2)}) collective-permute-start(f32[192,256]{1,0:T(8,128)S(1)} %slice.9), channel_id=1, source_target_pairs={{0,24},{4,28},{8,16},{12,20},{16,8},{20,12},{24,0},{28,4},{1,25},{... | collective-permute-start | bytes 589832 | tf_op jit(solution)/shard_map/ppermute | solution.py:40
  17.9 14.7 %collective-permute-start.10 = (f32[960,256]{1,0:T(8,128)S(1)}, f32[960,256]{1,0:T(8,128)S(1)}, u32[]{:S(2)}, u32[]{:S(2)}) collective-permute-start(f32[960,256]{1,0:T(8,128)S(1)} %get-tuple-element.22.refs_2_.near.refs_4_), channel_id=1, source_target_pairs={{0,4},{4,0},{8,12},{12,8},{16,20},{20,16},{24,28},{28,24},{1,5},{5... | collective-permute-start | bytes 2949128 | tf_op jit(solution)/shard_map/ppermute | solution.py:40
  25.7 6.9 %collective-permute-start.11 = (f32[960,256]{1,0:T(8,128)S(1)}, f32[960,256]{1,0:T(8,128)S(1)}, u32[]{:S(2)}, u32[]{:S(2)}) collective-permute-start(f32[960,256]{1,0:T(8,128)S(1)} %pad_maximum_fusion.refs_4_), channel_id=1, source_target_pairs={{0,4},{4,0},{8,12},{12,8},{16,20},{20,16},{24,28},{28,24},{1,5},{5... | collective-permute-start | bytes 2949128 | tf_op jit(solution)/shard_map/ppermute | solution.py:40
  29.8 2.4 %collective-permute-start.15 = (f32[256,384]{1,0:T(8,128)S(1)}, f32[256,384]{1,0:T(8,128)S(1)}, u32[]{:S(2)}, u32[]{:S(2)}) collective-permute-start(f32[256,384]{1,0:T(8,128)S(1)} %shard_map.50), channel_id=1, source_target_pairs={{0,4},{4,0},{8,12},{12,8},{16,20},{20,16},{24,28},{28,24},{1,5},{5... | collective-permute-start | bytes 1179656 | tf_op jit(solution)/shard_map/ppermute | solution.py:40
  32.2 10.4 %collective-permute-start.16 = (f32[256,384]{1,0:T(8,128)S(1)}, f32[256,384]{1,0:T(8,128)S(1)}, u32[]{:S(2)}, u32[]{:S(2)}) collective-permute-start(f32[256,384]{1,0:T(8,128)S(1)} %add.6), channel_id=1, source_target_pairs={{0,8},{4,12},{8,0},{12,4},{16,24},{20,28},{24,16},{28,20},{1,9},{5... | collective-permute-start | bytes 1179656 | tf_op jit(solution)/shard_map/ppermute | solution.py:40
  37.0 20.4 %collective-permute-start.12 = (f32[192,384]{1,0:T(8,128)S(1)}, f32[192,384]{1,0:T(8,128)S(1)}, u32[]{:S(2)}, u32[]{:S(2)}) collective-permute-start(f32[192,384]{1,0:T(8,128)S(1)} %get-tuple-element.25), channel_id=1, source_target_pairs={{0,2},{1,3},{2,0},{3,1},{4,6},{5,7},{6,4},{7,5},{8,10},{9,11},{10,... | collective-permute-start | bytes 884744 | tf_op jit(solution)/shard_map/ppermute | solution.py:40
  39.2 26.7 %collective-permute-start.13 = (f32[192,384]{1,0:T(8,128)S(1)}, f32[192,384]{1,0:T(8,128)S(1)}, u32[]{:S(2)}, u32[]{:S(2)}) collective-permute-start(f32[192,384]{1,0:T(8,128)S(1)} %get-tuple-element.26), channel_id=1, source_target_pairs={{0,3},{1,2},{2,1},{3,0},{4,7},{5,6},{6,5},{7,4},{8,11},{9,10},{10,... | collective-permute-start | bytes 884744 | tf_op jit(solution)/shard_map/ppermute | solution.py:40
  39.5 26.4 %collective-permute-start.14 = (f32[192,384]{1,0:T(8,128)S(1)}, f32[192,384]{1,0:T(8,128)S(1)}, u32[]{:S(2)}, u32[]{:S(2)}) collective-permute-start(f32[192,384]{1,0:T(8,128)S(1)} %get-tuple-element.27), channel_id=1, source_target_pairs={{0,1},{1,0},{2,3},{3,2},{4,5},{5,4},{6,7},{7,6},{8,9},{9,8},{10,11... | collective-permute-start | bytes 884744 | tf_op jit(solution)/shard_map/ppermute | solution.py:40
  42.7 23.5 %collective-permute-start.17 = (f32[128,384]{1,0:T(8,128)S(1)}, f32[128,384]{1,0:T(8,128)S(1)}, u32[]{:S(2)}, u32[]{:S(2)}) collective-permute-start(f32[128,384]{1,0:T(8,128)S(1)} %get-tuple-element.36), channel_id=1, source_target_pairs={{0,16},{4,20},{8,24},{12,28},{16,0},{20,4},{24,8},{28,12},{1,17},{... | collective-permute-start | bytes 589832 | tf_op jit(solution)/shard_map/ppermute | solution.py:40
  44.0 22.2 %collective-permute-start.18 = (f32[128,384]{1,0:T(8,128)S(1)}, f32[128,384]{1,0:T(8,128)S(1)}, u32[]{:S(2)}, u32[]{:S(2)}) collective-permute-start(f32[128,384]{1,0:T(8,128)S(1)} %get-tuple-element.35), channel_id=1, source_target_pairs={{0,16},{4,20},{8,24},{12,28},{16,0},{20,4},{24,8},{28,12},{1,17},{... | collective-permute-start | bytes 589832 | tf_op jit(solution)/shard_map/ppermute | solution.py:40

commit v5 on v4

--- a/solution.py
+++ b/solution.py
@@ -139,6 +139,11 @@
     return (row // per) ^ col, row % per
 
 
+def at_end():
+    col = lax.axis_index("col")
+    return (col == 0) | (col == lax.axis_size("col") - 1)
+
+
 def split_pieces(pieces, in_refs, high, low, height, share):
     for ref, places in zip(in_refs, pieces):
         for n, (index, kind) in enumerate(places):
@@ -160,11 +165,10 @@
     return both[:height] + (both[height:] + one(factors[:height], low[rows, :]))
 
 
-def send_kernel(pieces, per, share, offsets, *refs):
+def send_kernel(pieces, per, share, *refs):
     count = len(pieces)
     in_refs, matrix, factors_ref = refs[:count], refs[count], refs[count + 1]
-    outs = refs[count + 2 : count + 2 + len(offsets)]
-    high, low = refs[count + 2 + len(offsets) :]
+    outs, (high, low) = refs[count + 2 : -2], refs[-2:]
     height = matrix.shape[0]
     wide = per * height
     base, first = place_in_kernel(per)
@@ -190,7 +194,8 @@
     )
     factors_ref[...] = factors
     stacked = jnp.concatenate(halves(factors), axis=0)
-    for k, out in zip(offsets, outs):
+    onward = jnp.where(at_end(), 3, 1)
+    for k, out in zip((onward, 2, 4 - onward), outs):
         out[...] = block_of(stacked, high, low, (base ^ k) * wide, wide)
 
 
@@ -233,11 +238,31 @@
     put_in_order(out, base, made, first, per)
 
 
-def last_kernel(*refs):
-    summed, sides, *parts, near, out = refs
+def late_kernel(passed, across, other, sides, beside, out, added):
+    added[...] = sides[...] + beside[...]
+
+    @pl.when(at_end())
+    def _():
+        out[...] = other[...]
+
+    @pl.when(jnp.logical_not(at_end()))
+    def _():
+        out[...] = passed[...] + across[...]
+
+
+def last_kernel(per, *refs):
+    summed, late, passed, sides, *parts, near, out, made = refs
+    _, first = place_in_kernel(per)
+    made[...] = late[...]
+
+    @pl.when(at_end())
+    def _():
+        made[...] = made[...] + passed[...]
+
+    put_in_order(out, summed, made, first, per)
     refl = near[: out.shape[0], :]
     whole = sides[...] + jnp.concatenate([part[...] for part in parts], axis=0)
-    out[...] = summed[...] - pair_dot(halves(refl), halves(whole), OVER)
+    out[...] = out[...] - pair_dot(halves(refl), halves(whole), OVER)
 
 
 def run_kernel(body, outs, args, scratch=(), flops=0, moved=0):
@@ -311,16 +336,23 @@
     total, depth = rows * height, 2 * share + width
     halved = pltpu.VMEM((total, depth), jnp.bfloat16)
     block = pltpu.VMEM((height, wide), jnp.float32)
-    offsets = sorted(range(1, cols), key=lambda k: (k == 1, k))
     factors, *blocks = run_kernel(
-        functools.partial(send_kernel, pieces, per, share, offsets),
-        [(height, depth)] + [(height, wide)] * len(offsets),
+        functools.partial(send_kernel, pieces, per, share),
+        [(height, depth)] + [(height, wide)] * (cols - 1),
         arrays + [matrix],
         [halved, halved],
         12 * total * share * width + 6 * total * height * depth,
         4 * total * depth,
     )
-    received = [swap(b, "col", k) for k, b in zip(offsets, blocks)]
+    received = [lax.ppermute(blocks[2], "col", [(1, 2), (2, 1)])]
+    passed = swap(blocks[0], "col", 1)
+    received += [lax.ppermute(blocks[1], "col", [(0, 2), (3, 1)])]
+    late, sides = run_kernel(
+        late_kernel,
+        [(height, wide), (width, wide)],
+        [passed, blocks[1], blocks[2], sides, beside],
+    )
+    late = lax.ppermute(late, "col", [(0, 1), (3, 2), (1, 3), (2, 0)])
     (base,) = run_kernel(
         functools.partial(keep_kernel, pieces, per, share),
         [(height, wide)],
@@ -329,8 +361,6 @@
         6 * wide * height * depth,
         4 * total * depth,
     )
-    sides, beside, _ = lax.optimization_barrier((sides, beside, factors))
-    sides = sides + beside
     parts = [swap(sides[n : n + width // 2], "row", 4) for n in (0, width // 2)]
     (summed,) = run_kernel(
         functools.partial(sum_kernel, per),
@@ -340,12 +370,12 @@
         height * wide * cols,
         16 * height * wide * (cols + 1),
     )
-    summed, parts = lax.optimization_barrier((summed, parts))
+    summed, parts, late = lax.optimization_barrier((summed, parts, late))
     (updated,) = run_kernel(
-        last_kernel,
+        functools.partial(last_kernel, per),
         [(height, wide)],
-        [summed, sides, *parts, near],
-        (),
+        [summed, late, passed, sides, *parts, near],
+        [block],
         6 * height * width * wide,
         4 * width * wide * 2,
     )
@@ -373,7 +403,7 @@
     height, share = left_panel.shape
     width = reflectors.shape[1] * cols
     need = rows * height * (2 * share + width) * 8 + rows * height * height * 8
-    if rows == 8 and share == width and need <= VMEM_BYTES:
+    if rows == 8 and cols == 4 and share == width and need <= VMEM_BYTES:
         return local_square(matrix, left_panel, right_panel, reflectors)
     return local_general(matrix, left_panel, right_panel, reflectors)
 

time: 67.3 us -> 66.1 us (0.982)
  the two profiles are of different devices: /device:TPU:17 before, /device:TPU:0 now
where the time goes in v5:
time: 66.1 us; the launch traced here: 65.9 us
  waiting for transfers between devices  31.1 us (47%)
  starting transfers between devices  25.7 us (39%)
  Pallas kernels  7.84 us (12%)
  other arithmetic  0.96 us (1%)
    ppermute x17, waiting for transfers between devices, swap(): return lax.ppermute(value, axis, [(i, i ^ offset) for i in range(size)])  24.1 us
    ppermute x17, starting transfers between devices, swap(): return lax.ppermute(value, axis, [(i, i ^ offset) for i in range(size)])  18.1 us
    pallas_call x7, Pallas kernels, run_kernel(): pl.pallas_call(body, out_shape=[jax.ShapeDtypeStruct(shape, jnp.float32)...  7.84 us
    ppermute x1, starting transfers between devices, local_square(): received += [lax.ppermute(blocks[1], 'col', [(0, 2), (3, 1)])]  6.61 us
    ppermute x1, waiting for transfers between devices, local_square(): late = lax.ppermute(late, 'col', [(0, 1), (3, 2), (1, 3), (2, 0)])  5.15 us
    ppermute x1, waiting for transfers between devices, local_square(): received += [lax.ppermute(blocks[1], 'col', [(0, 2), (3, 1)])]  1.81 us
  transfers between devices with their start and end apart: 20, of which 9 were waited for; matrix products, arithmetic and copies ran while one was open for 2% of the time, Pallas kernels for 10%

profile of v5, /device:TPU:0, one launch (start us, length us, event | category | flops | bytes accessed | tf_op | source)
XLA Modules:
  0.0 65.9 jit_solution(13598790823682646776)
XLA Ops:
  0.0 3.0 %collective-permute-start.4 = (f32[64,192]{1,0:T(8,128)}, f32[64,192]{1,0:T(8,128)S(1)}, u32[]{:S(2)}, u32[]{:S(2)}) collective-permute-start(f32[64,192]{1,0:T(8,128)} %bitcast.1), channel_id=1, source_target_pairs={{0,1},{1,0},{2,3},{3,2},{4,5},{5,4},{6,7},{7,6},{8,9},{9,8},{10,11... | collective-permute-start | bytes 147464 | tf_op jit(solution)/shard_map/ppermute | solution.py:40
  3.0 1.5 %collective-permute-start.2 = (f32[192,256]{1,0:T(8,128)}, f32[192,256]{1,0:T(8,128)S(1)}, u32[]{:S(2)}, u32[]{:S(2)}) collective-permute-start(f32[192,256]{1,0:T(8,128)} %param.5), channel_id=1, source_target_pairs={{0,16},{4,20},{8,24},{12,28},{16,0},{20,4},{24,8},{28,12},{1,17},{... | collective-permute-start | bytes 589832 | tf_op jit(solution)/shard_map/ppermute | solution.py:40
  4.5 1.5 %collective-permute-start = (f32[192,256]{1,0:T(8,128)}, f32[192,256]{1,0:T(8,128)S(1)}, u32[]{:S(2)}, u32[]{:S(2)}) collective-permute-start(f32[192,256]{1,0:T(8,128)} %param.5), channel_id=1, source_target_pairs={{0,8},{4,12},{8,0},{12,4},{16,24},{20,28},{24,16},{28,20},{1,9},{5... | collective-permute-start | bytes 589832 | tf_op jit(solution)/shard_map/ppermute | solution.py:40
  6.0 0.5 collective-permute-start.3
  6.5 0.5 collective-permute-start.1
  7.1 0.0 collective-permute-done.4
  7.1 0.8 %pad_maximum_fusion.1.refs_0_ = f32[128,192]{1,0:T(8,128)S(1)} fusion(f32[64,192]{1,0:T(8,128)S(1)} %collective-permute-done.4, f32[64,192]{1,0:T(8,128)} %bitcast.2), kind=kLoop, calls=%fused_computation.1 | loop fusion | flops 24576 | bytes 196608 | tf_op jit(solution)/shard_map/concatenate | solution.py:326
  7.9 0.0 copy-start.1
  7.9 2.7 %collective-permute-start.5 = (f32[128,192]{1,0:T(8,128)S(1)}, f32[128,192]{1,0:T(8,128)S(1)}, u32[]{:S(2)}, u32[]{:S(2)}) collective-permute-start(f32[128,192]{1,0:T(8,128)S(1)} %pad_maximum_fusion.1.refs_0_), channel_id=1, source_target_pairs={{0,2},{1,3},{2,0},{3,1},{4,6},{5,7},{6,4},{7,5},{8,10},{9,11},{10,... | collective-permute-start | bytes 294920 | tf_op jit(solution)/shard_map/ppermute | solution.py:40
  10.6 5.0 %collective-permute-done.5.refs_1_ = f32[128,192]{1,0:T(8,128)S(1)} collective-permute-done((f32[128,192]{1,0:T(8,128)S(1)}, f32[128,192]{1,0:T(8,128)S(1)}, u32[]{:S(2)}, u32[]{:S(2)}) %collective-permute-start.5) | collective-permute-done | bytes 98336 | tf_op jit(solution)/shard_map/ppermute | solution.py:40
  15.6 0.0 collective-permute-done.2.left_y
  15.6 0.0 collective-permute-done.left_x
  15.6 0.0 collective-permute-done.3.right_y
  15.6 0.0 collective-permute-done.1.right_x
  15.6 0.1 shard_map.46
  15.7 1.6 %collective-permute-start.6 = (f32[384,256]{1,0:T(8,128)S(1)}, f32[384,256]{1,0:T(8,128)S(1)}, u32[]{:S(2)}, u32[]{:S(2)}) collective-permute-start(f32[384,256]{1,0:T(8,128)S(1)} %get-tuple-element.21), channel_id=1, source_target_pairs={{0,8},{4,12},{8,0},{12,4},{16,24},{20,28},{24,16},{28,20},{1,9},{5... | collective-permute-start | bytes 1179656 | tf_op jit(solution)/shard_map/ppermute | solution.py:40
  17.3 1.5 %collective-permute-start.7 = (f32[384,256]{1,0:T(8,128)S(1)}, f32[384,256]{1,0:T(8,128)S(1)}, u32[]{:S(2)}, u32[]{:S(2)}) collective-permute-start(f32[384,256]{1,0:T(8,128)S(1)} %get-tuple-element.22), channel_id=1, source_target_pairs={{0,16},{4,20},{8,24},{12,28},{16,0},{20,4},{24,8},{28,12},{1,17},{... | collective-permute-start | bytes 1179656 | tf_op jit(solution)/shard_map/ppermute | solution.py:40
  18.9 0.1 collective-permute-start.9
  19.0 0.0 copy-start
  19.0 0.9 %collective-permute-start.8 = (f32[192,256]{1,0:T(8,128)S(1)}, f32[192,256]{1,0:T(8,128)S(1)}, u32[]{:S(2)}, u32[]{:S(2)}) collective-permute-start(f32[192,256]{1,0:T(8,128)S(1)} %slice.9), channel_id=1, source_target_pairs={{0,24},{4,28},{8,16},{12,20},{16,8},{20,12},{24,0},{28,4},{1,25},{... | collective-permute-start | bytes 589832 | tf_op jit(solution)/shard_map/ppermute | solution.py:40
  19.9 0.2 collective-permute-start.10
  20.1 10.9 %collective-permute-done.8 = f32[192,256]{1,0:T(8,128)S(1)} collective-permute-done((f32[192,256]{1,0:T(8,128)S(1)}, f32[192,256]{1,0:T(8,128)S(1)}, u32[]{:S(2)}, u32[]{:S(2)}) %collective-permute-start.8) | collective-permute-done | bytes 196640 | tf_op jit(solution)/shard_map/ppermute | solution.py:40
  31.0 0.0 collective-permute-done.6
  31.0 0.1 collective-permute-done.7
  31.2 0.1 pad_maximum_fusion.refs_4_
  31.2 0.0 collective-permute-done.9.refs_1_
  31.3 0.1 collective-permute-start.11
  31.3 0.4 shard_map.50
  31.7 0.6 collective-permute-start.15
  32.3 2.1 %collective-permute-done.15 = f32[256,384]{1,0:T(8,128)S(1)} collective-permute-done((f32[256,384]{1,0:T(8,128)S(1)}, f32[256,384]{1,0:T(8,128)S(1)}, u32[]{:S(2)}, u32[]{:S(2)}) %collective-permute-start.15) | collective-permute-done | bytes 393248 | tf_op jit(solution)/shard_map/ppermute | solution.py:40
  34.5 1.3 %collective-permute-start.16 = (f32[256,384]{1,0:T(8,128)S(1)}, f32[256,384]{1,0:T(8,128)S(1)}, u32[]{:S(2)}, u32[]{:S(2)}) collective-permute-start(f32[256,384]{1,0:T(8,128)S(1)} %add.3.sides), channel_id=1, source_target_pairs={{0,8},{4,12},{8,0},{12,4},{16,24},{20,28},{24,16},{28,20},{1,9},{5... | collective-permute-start | bytes 1179656 | tf_op jit(solution)/shard_map/ppermute | solution.py:40
  35.8 4.4 %shard_map.47 = (f32[192,768]{1,0:T(8,128)S(1)}, f32[192,384]{1,0:T(8,128)S(1)}, f32[192,384]{1,0:T(8,128)S(1)}, f32[192,384]{1,0:T(8,128)S(1)}) custom-call(f32[384,256]{1,0:T(8,128)S(1)} %constant_dynamic-update-slice_fusion.refs_0_, f32[384,256]{1,0:T(8,128)S(1)} %collective-permute-done.9.refs_1_, f32[960,256]{1,0:T(8,128)S(1)} %get-tuple-element.23.refs_2_.near.refs_6_, ...), custom_call_target="tpu_custom_call" | custom-call | flops 2566914048 | bytes 4718592 | tf_op jit(solution)/shard_map/pallas_call | solution.py:270
  40.2 0.1 collective-permute-start.14
  40.3 0.7 %collective-permute-start.12 = (f32[192,384]{1,0:T(8,128)S(1)}, f32[192,384]{1,0:T(8,128)S(1)}, u32[]{:S(2)}, u32[]{:S(2)}) collective-permute-start(f32[192,384]{1,0:T(8,128)S(1)} %get-tuple-element.26.other), channel_id=1, source_target_pairs={{1,2},{2,1},{5,6},{6,5},{9,10},{10,9},{13,14},{14,13},{17,18},{18,... | collective-permute-start | bytes 884744 | tf_op jit(solution)/shard_map/ppermute | solution.py:347
  41.0 6.6 %collective-permute-start.13 = (f32[192,384]{1,0:T(8,128)S(1)}, f32[192,384]{1,0:T(8,128)S(1)}, u32[]{:S(2)}, u32[]{:S(2)}) collective-permute-start(f32[192,384]{1,0:T(8,128)S(1)} %get-tuple-element.27.across), channel_id=1, source_target_pairs={{0,2},{3,1},{4,6},{7,5},{8,10},{11,9},{12,14},{15,13},{16,18},{19,... | collective-permute-start | bytes 884744 | tf_op jit(solution)/shard_map/ppermute | solution.py:349
  47.6 0.0 collective-permute-done.16.beside
  47.6 1.4 %collective-permute-done.14.passed.refs_2_ = f32[192,384]{1,0:T(8,128)S(1)} collective-permute-done((f32[192,384]{1,0:T(8,128)S(1)}, f32[192,384]{1,0:T(8,128)S(1)}, u32[]{:S(2)}, u32[]{:S(2)}) %collective-permute-start.14) | collective-permute-done | bytes 294944 | tf_op jit(solution)/shard_map/ppermute | solution.py:40
  49.1 0.1 shard_map.51
  49.1 0.3 collective-permute-start.19
  49.5 0.9 %collective-permute-start.18 = (f32[128,384]{1,0:T(8,128)S(1)}, f32[128,384]{1,0:T(8,128)S(1)}, u32[]{:S(2)}, u32[]{:S(2)}) collective-permute-start(f32[128,384]{1,0:T(8,128)S(1)} %get-tuple-element.37), channel_id=1, source_target_pairs={{0,16},{4,20},{8,24},{12,28},{16,0},{20,4},{24,8},{28,12},{1,17},{... | collective-permute-start | bytes 589832 | tf_op jit(solution)/shard_map/ppermute | solution.py:40
  50.4 1.2 %collective-permute-start.17 = (f32[128,384]{1,0:T(8,128)S(1)}, f32[128,384]{1,0:T(8,128)S(1)}, u32[]{:S(2)}, u32[]{:S(2)}) collective-permute-start(f32[128,384]{1,0:T(8,128)S(1)} %get-tuple-element.38), channel_id=1, source_target_pairs={{0,16},{4,20},{8,24},{12,28},{16,0},{20,4},{24,8},{28,12},{1,17},{... | collective-permute-start | bytes 589832 | tf_op jit(solution)/shard_map/ppermute | solution.py:40
  51.6 1.6 %shard_map.48.refs_2_ = f32[192,384]{1,0:T(8,128)S(1)} custom-call(f32[384,256]{1,0:T(8,128)S(1)} %constant_dynamic-update-slice_fusion.refs_0_, f32[384,256]{1,0:T(8,128)S(1)} %collective-permute-done.9.refs_1_, f32[960,256]{1,0:T(8,128)S(1)} %get-tuple-element.23.refs_2_.near.refs_6_, f32[960,256]{1,0:T(8,128)S(1)} %collective-permute-done.10.refs_3_, ...), custom_call_target="tpu_custom_call" | custom-call | flops 339738624 | bytes 4718592 | tf_op jit(solution)/shard_map/pallas_call | solution.py:270
  53.3 1.8 %collective-permute-done.13.refs_1_ = f32[192,384]{1,0:T(8,128)S(1)} collective-permute-done((f32[192,384]{1,0:T(8,128)S(1)}, f32[192,384]{1,0:T(8,128)S(1)}, u32[]{:S(2)}, u32[]{:S(2)}) %collective-permute-start.13) | collective-permute-done | bytes 294944 | tf_op jit(solution)/shard_map/ppermute | solution.py:349
  55.1 0.1 shard_map.49.refs_0_
  55.1 2.3 %collective-permute-done.18.refs_5_ = f32[128,384]{1,0:T(8,128)S(1)} collective-permute-done((f32[128,384]{1,0:T(8,128)S(1)}, f32[128,384]{1,0:T(8,128)S(1)}, u32[]{:S(2)}, u32[]{:S(2)}) %collective-permute-start.18) | collective-permute-done | bytes 196640 | tf_op jit(solution)/shard_map/ppermute | solution.py:40
  57.4 2.2 %collective-permute-done.17.refs_4_ = f32[128,384]{1,0:T(8,128)S(1)} collective-permute-done((f32[128,384]{1,0:T(8,128)S(1)}, f32[128,384]{1,0:T(8,128)S(1)}, u32[]{:S(2)}, u32[]{:S(2)}) %collective-permute-start.17) | collective-permute-done | bytes 196640 | tf_op jit(solution)/shard_map/ppermute | solution.py:40
  59.6 5.1 %collective-permute-done.19.refs_1_ = f32[192,384]{1,0:T(8,128)S(1)} collective-permute-done((f32[192,384]{1,0:T(8,128)S(1)}, f32[192,384]{1,0:T(8,128)S(1)}, u32[]{:S(2)}, u32[]{:S(2)}) %collective-permute-start.19) | collective-permute-done | bytes 294944 | tf_op jit(solution)/shard_map/ppermute | solution.py:355
  64.8 1.1 %shard_map.52 = f32[192,384]{1,0:T(8,128)} custom-call(f32[192,384]{1,0:T(8,128)S(1)} %shard_map.49.refs_0_, f32[192,384]{1,0:T(8,128)S(1)} %collective-permute-done.19.refs_1_, f32[192,384]{1,0:T(8,128)S(1)} %collective-permute-done.14.passed.refs_2_, f32[256,384]{1,0:T(8,128)S(1)} %get-tuple-element.31.refs_3_, ...), custom_call_target="tpu_custom_call" | custom-call | flops 113246208 | bytes 786432 | tf_op jit(solution)/shard_map/pallas_call | solution.py:270
  (12 shorter events, 0.1 us)
Async XLA Ops:
  0.0 7.1 %collective-permute-start.4 = (f32[64,192]{1,0:T(8,128)}, f32[64,192]{1,0:T(8,128)S(1)}, u32[]{:S(2)}, u32[]{:S(2)}) collective-permute-start(f32[64,192]{1,0:T(8,128)} %bitcast.1), channel_id=1, source_target_pairs={{0,1},{1,0},{2,3},{3,2},{4,5},{5,4},{6,7},{7,6},{8,9},{9,8},{10,11... | collective-permute-start | bytes 147464 | tf_op jit(solution)/shard_map/ppermute | solution.py:40
  3.0 12.5 %collective-permute-start.2 = (f32[192,256]{1,0:T(8,128)}, f32[192,256]{1,0:T(8,128)S(1)}, u32[]{:S(2)}, u32[]{:S(2)}) collective-permute-start(f32[192,256]{1,0:T(8,128)} %param.5), channel_id=1, source_target_pairs={{0,16},{4,20},{8,24},{12,28},{16,0},{20,4},{24,8},{28,12},{1,17},{... | collective-permute-start | bytes 589832 | tf_op jit(solution)/shard_map/ppermute | solution.py:40
  4.5 11.0 %collective-permute-start = (f32[192,256]{1,0:T(8,128)}, f32[192,256]{1,0:T(8,128)S(1)}, u32[]{:S(2)}, u32[]{:S(2)}) collective-permute-start(f32[192,256]{1,0:T(8,128)} %param.5), channel_id=1, source_target_pairs={{0,8},{4,12},{8,0},{12,4},{16,24},{20,28},{24,16},{28,20},{1,9},{5... | collective-permute-start | bytes 589832 | tf_op jit(solution)/shard_map/ppermute | solution.py:40
  6.0 9.5 %collective-permute-start.3 = (f32[192,256]{1,0:T(8,128)}, f32[192,256]{1,0:T(8,128)S(1)}, u32[]{:S(2)}, u32[]{:S(2)}) collective-permute-start(f32[192,256]{1,0:T(8,128)} %param.6), channel_id=1, source_target_pairs={{0,16},{4,20},{8,24},{12,28},{16,0},{20,4},{24,8},{28,12},{1,17},{... | collective-permute-start | bytes 589832 | tf_op jit(solution)/shard_map/ppermute | solution.py:40
  6.5 9.0 %collective-permute-start.1 = (f32[192,256]{1,0:T(8,128)}, f32[192,256]{1,0:T(8,128)S(1)}, u32[]{:S(2)}, u32[]{:S(2)}) collective-permute-start(f32[192,256]{1,0:T(8,128)} %param.6), channel_id=1, source_target_pairs={{0,8},{4,12},{8,0},{12,4},{16,24},{20,28},{24,16},{28,20},{1,9},{5... | collective-permute-start | bytes 589832 | tf_op jit(solution)/shard_map/ppermute | solution.py:40
  7.9 10.9 %copy-start.1 = (f32[192,256]{1,0:T(8,128)S(1)}, f32[192,256]{1,0:T(8,128)}, u32[]{:S(2)}) copy-start(f32[192,256]{1,0:T(8,128)} %param.5) | copy-start | bytes 589828
  7.9 7.6 %collective-permute-start.5 = (f32[128,192]{1,0:T(8,128)S(1)}, f32[128,192]{1,0:T(8,128)S(1)}, u32[]{:S(2)}, u32[]{:S(2)}) collective-permute-start(f32[128,192]{1,0:T(8,128)S(1)} %pad_maximum_fusion.1.refs_0_), channel_id=1, source_target_pairs={{0,2},{1,3},{2,0},{3,1},{4,6},{5,7},{6,4},{7,5},{8,10},{9,11},{10,... | collective-permute-start | bytes 294920 | tf_op jit(solution)/shard_map/ppermute | solution.py:40
  15.7 15.3 %collective-permute-start.6 = (f32[384,256]{1,0:T(8,128)S(1)}, f32[384,256]{1,0:T(8,128)S(1)}, u32[]{:S(2)}, u32[]{:S(2)}) collective-permute-start(f32[384,256]{1,0:T(8,128)S(1)} %get-tuple-element.21), channel_id=1, source_target_pairs={{0,8},{4,12},{8,0},{12,4},{16,24},{20,28},{24,16},{28,20},{1,9},{5... | collective-permute-start | bytes 1179656 | tf_op jit(solution)/shard_map/ppermute | solution.py:40
  17.3 1.5 %copy-start.2 = (f32[192,256]{1,0:T(8,128)S(1)}, f32[192,256]{1,0:T(8,128)}, u32[]{:S(2)}) copy-start(f32[192,256]{1,0:T(8,128)} %param.6) | copy-start | bytes 589828
  17.3 13.9 %collective-permute-start.7 = (f32[384,256]{1,0:T(8,128)S(1)}, f32[384,256]{1,0:T(8,128)S(1)}, u32[]{:S(2)}, u32[]{:S(2)}) collective-permute-start(f32[384,256]{1,0:T(8,128)S(1)} %get-tuple-element.22), channel_id=1, source_target_pairs={{0,16},{4,20},{8,24},{12,28},{16,0},{20,4},{24,8},{28,12},{1,17},{... | collective-permute-start | bytes 1179656 | tf_op jit(solution)/shard_map/ppermute | solution.py:40
  18.9 12.4 %collective-permute-start.9 = (f32[384,256]{1,0:T(8,128)S(1)}, f32[384,256]{1,0:T(8,128)S(1)}, u32[]{:S(2)}, u32[]{:S(2)}) collective-permute-start(f32[384,256]{1,0:T(8,128)S(1)} %constant_dynamic-update-slice_fusion.refs_0_), channel_id=1, source_target_pairs={{0,4},{4,0},{8,12},{12,8},{16,20},{20,16},{24,28},{28,24},{1,5},{5... | collective-permute-start | bytes 1179656 | tf_op jit(solution)/shard_map/ppermute | solution.py:40
  19.0 12.4 %copy-start = (f32[192,384]{1,0:T(8,128)S(1)}, f32[192,384]{1,0:T(8,128)}, u32[]{:S(2)}) copy-start(f32[192,384]{1,0:T(8,128)} %matrix.1) | copy-start | bytes 884740
  19.0 12.0 %collective-permute-start.8 = (f32[192,256]{1,0:T(8,128)S(1)}, f32[192,256]{1,0:T(8,128)S(1)}, u32[]{:S(2)}, u32[]{:S(2)}) collective-permute-start(f32[192,256]{1,0:T(8,128)S(1)} %slice.9), channel_id=1, source_target_pairs={{0,24},{4,28},{8,16},{12,20},{16,8},{20,12},{24,0},{28,4},{1,25},{... | collective-permute-start | bytes 589832 | tf_op jit(solution)/shard_map/ppermute | solution.py:40
  19.9 15.9 %collective-permute-start.10 = (f32[960,256]{1,0:T(8,128)S(1)}, f32[960,256]{1,0:T(8,128)S(1)}, u32[]{:S(2)}, u32[]{:S(2)}) collective-permute-start(f32[960,256]{1,0:T(8,128)S(1)} %get-tuple-element.23.refs_2_.near.refs_6_), channel_id=1, source_target_pairs={{0,4},{4,0},{8,12},{12,8},{16,20},{20,16},{24,28},{28,24},{1,5},{5... | collective-permute-start | bytes 2949128 | tf_op jit(solution)/shard_map/ppermute | solution.py:40
  31.3 4.6 %collective-permute-start.11 = (f32[960,256]{1,0:T(8,128)S(1)}, f32[960,256]{1,0:T(8,128)S(1)}, u32[]{:S(2)}, u32[]{:S(2)}) collective-permute-start(f32[960,256]{1,0:T(8,128)S(1)} %pad_maximum_fusion.refs_4_), channel_id=1, source_target_pairs={{0,4},{4,0},{8,12},{12,8},{16,20},{20,16},{24,28},{28,24},{1,5},{5... | collective-permute-start | bytes 2949128 | tf_op jit(solution)/shard_map/ppermute | solution.py:40
  31.7 2.7 %collective-permute-start.15 = (f32[256,384]{1,0:T(8,128)S(1)}, f32[256,384]{1,0:T(8,128)S(1)}, u32[]{:S(2)}, u32[]{:S(2)}) collective-permute-start(f32[256,384]{1,0:T(8,128)S(1)} %shard_map.50), channel_id=1, source_target_pairs={{0,4},{4,0},{8,12},{12,8},{16,20},{20,16},{24,28},{28,24},{1,5},{5... | collective-permute-start | bytes 1179656 | tf_op jit(solution)/shard_map/ppermute | solution.py:40
  34.5 13.1 %collective-permute-start.16 = (f32[256,384]{1,0:T(8,128)S(1)}, f32[256,384]{1,0:T(8,128)S(1)}, u32[]{:S(2)}, u32[]{:S(2)}) collective-permute-start(f32[256,384]{1,0:T(8,128)S(1)} %add.3.sides), channel_id=1, source_target_pairs={{0,8},{4,12},{8,0},{12,4},{16,24},{20,28},{24,16},{28,20},{1,9},{5... | collective-permute-start | bytes 1179656 | tf_op jit(solution)/shard_map/ppermute | solution.py:40
  40.2 8.8 %collective-permute-start.14 = (f32[192,384]{1,0:T(8,128)S(1)}, f32[192,384]{1,0:T(8,128)S(1)}, u32[]{:S(2)}, u32[]{:S(2)}) collective-permute-start(f32[192,384]{1,0:T(8,128)S(1)} %get-tuple-element.29), channel_id=1, source_target_pairs={{0,1},{1,0},{2,3},{3,2},{4,5},{5,4},{6,7},{7,6},{8,9},{9,8},{10,11... | collective-permute-start | bytes 884744 | tf_op jit(solution)/shard_map/ppermute | solution.py:40
  40.3 12.9 %collective-permute-start.12 = (f32[192,384]{1,0:T(8,128)S(1)}, f32[192,384]{1,0:T(8,128)S(1)}, u32[]{:S(2)}, u32[]{:S(2)}) collective-permute-start(f32[192,384]{1,0:T(8,128)S(1)} %get-tuple-element.26.other), channel_id=1, source_target_pairs={{1,2},{2,1},{5,6},{6,5},{9,10},{10,9},{13,14},{14,13},{17,18},{18,... | collective-permute-start | bytes 884744 | tf_op jit(solution)/shard_map/ppermute | solution.py:347
  41.0 14.1 %collective-permute-start.13 = (f32[192,384]{1,0:T(8,128)S(1)}, f32[192,384]{1,0:T(8,128)S(1)}, u32[]{:S(2)}, u32[]{:S(2)}) collective-permute-start(f32[192,384]{1,0:T(8,128)S(1)} %get-tuple-element.27.across), channel_id=1, source_target_pairs={{0,2},{3,1},{4,6},{7,5},{8,10},{11,9},{12,14},{15,13},{16,18},{19,... | collective-permute-start | bytes 884744 | tf_op jit(solution)/shard_map/ppermute | solution.py:349
  49.1 15.6 %collective-permute-start.19 = (f32[192,384]{1,0:T(8,128)S(1)}, f32[192,384]{1,0:T(8,128)S(1)}, u32[]{:S(2)}, u32[]{:S(2)}) collective-permute-start(f32[192,384]{1,0:T(8,128)S(1)} %get-tuple-element.32), channel_id=1, source_target_pairs={{0,1},{3,2},{1,3},{2,0},{4,5},{7,6},{5,7},{6,4},{8,9},{11,10},{9,1... | collective-permute-start | bytes 884744 | tf_op jit(solution)/shard_map/ppermute | solution.py:355
  49.5 7.9 %collective-permute-start.18 = (f32[128,384]{1,0:T(8,128)S(1)}, f32[128,384]{1,0:T(8,128)S(1)}, u32[]{:S(2)}, u32[]{:S(2)}) collective-permute-start(f32[128,384]{1,0:T(8,128)S(1)} %get-tuple-element.37), channel_id=1, source_target_pairs={{0,16},{4,20},{8,24},{12,28},{16,0},{20,4},{24,8},{28,12},{1,17},{... | collective-permute-start | bytes 589832 | tf_op jit(solution)/shard_map/ppermute | solution.py:40
  50.4 9.2 %collective-permute-start.17 = (f32[128,384]{1,0:T(8,128)S(1)}, f32[128,384]{1,0:T(8,128)S(1)}, u32[]{:S(2)}, u32[]{:S(2)}) collective-permute-start(f32[128,384]{1,0:T(8,128)S(1)} %get-tuple-element.38), channel_id=1, source_target_pairs={{0,16},{4,20},{8,24},{12,28},{16,0},{20,4},{24,8},{28,12},{1,17},{... | collective-permute-start | bytes 589832 | tf_op jit(solution)/shard_map/ppermute | solution.py:40

commit v6 on v5

--- a/solution.py
+++ b/solution.py
@@ -86,10 +86,13 @@
         6 * height * width * wide,
         4 * height * (width + wide),
     )
-    sides = sides + swap(sides, "row", 1)
+    across_sides = swap(sides, "row", 1)
     panels = stack(left_panel, right_panel)
     across_own = swap(panels, "row", 1)
-    last, across_own = lax.optimization_barrier((stack(by_x, by_y, far), across_own))
+    last, across_own, _ = lax.optimization_barrier(
+        (stack(by_x, by_y, far), across_own, across_sides)
+    )
+    sides = sides + across_sides
     own_at = ((0, 0), (0, 1))
     near_at = ((0, 2), (2, 0), (2, 1), (4, 0), (4, 1))
     last_at = ((6, 0), (2, 2), (6, 1), (4, 2), (6, 2))
@@ -165,30 +168,59 @@
     return both[:height] + (both[height:] + one(factors[:height], low[rows, :]))
 
 
-def send_kernel(pieces, per, share, *refs):
+def of_core(matrix, first, same):
+    height = matrix.shape[0]
+    return jnp.where((first == 0) == same, matrix[:, :height], matrix[:, height:])
+
+
+def mix_kernel(pieces, order, per, share, *refs):
     count = len(pieces)
-    in_refs, matrix, factors_ref = refs[:count], refs[count], refs[count + 1]
-    outs, (high, low) = refs[count + 2 : -2], refs[-2:]
+    in_refs, (matrix, mixed, image, high, low) = refs[:count], refs[count:]
+    height = matrix.shape[0]
+    for ref, places in zip(in_refs, pieces):
+        for n, (index, kind) in enumerate(places):
+            upper, lower = halves(ref[n * height : (n + 1) * height, :])
+            rows = slice(order.index(index) * height, (order.index(index) + 1) * height)
+            columns = slice(kind * share, (kind + 1) * share)
+            high[rows, columns] = upper
+            low[rows, columns] = lower
+    panels = (high[:, : 2 * share], low[:, : 2 * share])
+    refl = (high[:, 2 * share :], low[:, 2 * share :])
+    mixed[...] = pair_dot(refl, panels, DOWN)
+    base, first = place_in_kernel(per)
+    rows = pl.ds(pl.multiple_of(base * height, 16), height)
+    image[...] = pair_dot(
+        halves(of_core(matrix, first, True)), (high[rows, 2 * share :], low[rows, 2 * share :]), OVER
+    )
+
+
+def send_kernel(pieces, order, per, share, *refs):
+    count = len(pieces)
+    in_refs, (mixed_ref, image_ref, matrix, factors_ref) = refs[:count], refs[count : count + 4]
+    outs, (high, low) = refs[count + 4 : -2], refs[-2:]
     height = matrix.shape[0]
     wide = per * height
     base, first = place_in_kernel(per)
     split_pieces(pieces, in_refs, high, low, height, share)
-    panels = (high[:, : 2 * share], low[:, : 2 * share])
-    refl = (high[:, 2 * share :], low[:, 2 * share :])
-    mixed_pair = halves(pair_dot(refl, panels, DOWN))
+    mixed = mixed_ref[...]
+    for index in range(high.shape[0] // height):
+        if index not in order:
+            rows = slice(index * height, (index + 1) * height)
+            panels = (high[rows, : 2 * share], low[rows, : 2 * share])
+            refl = (high[rows, 2 * share :], low[rows, 2 * share :])
+            mixed = mixed + pair_dot(refl, panels, DOWN)
+    mixed_pair = halves(mixed)
     left_panel, right_panel = in_refs[0][:height, :], in_refs[0][height:, :]
     own_refl = (high[:height, 2 * share :], low[:height, 2 * share :])
+    rows = pl.ds(pl.multiple_of((base * per + 1) * height, 16), height)
+    image = image_ref[...] + pair_dot(
+        halves(of_core(matrix, first, False)),
+        (high[rows, 2 * share :], low[rows, 2 * share :]),
+        OVER,
+    )
     spread = pair_dot(own_refl, mixed_pair, OVER)
     turned = halves(jnp.concatenate([right_panel, -left_panel], axis=1))
-    image = pair_dot(turned, mixed_pair, ALONG)
-    for t in range(per):
-        begin = pl.multiple_of((base * per + (t ^ first)) * height, 16)
-        rows = pl.ds(begin, height)
-        image = image + pair_dot(
-            halves(matrix[:, t * height : (t + 1) * height]),
-            (high[rows, 2 * share :], low[rows, 2 * share :]),
-            OVER,
-        )
+    image = image + pair_dot(turned, mixed_pair, ALONG)
     factors = jnp.concatenate(
         [right_panel - spread[:, share:], spread[:, :share] - left_panel, -image], axis=1
     )
@@ -336,12 +368,23 @@
     total, depth = rows * height, 2 * share + width
     halved = pltpu.VMEM((total, depth), jnp.bfloat16)
     block = pltpu.VMEM((height, wide), jnp.float32)
+    order = tuple(range(0, rows, 2))
+    mine = [n for n, places in enumerate(pieces) if all(i in order for i, _ in places)]
+    known = pltpu.VMEM((len(order) * height, depth), jnp.bfloat16)
+    mixed, image = run_kernel(
+        functools.partial(mix_kernel, tuple(pieces[n] for n in mine), order, per, share),
+        [(width, 2 * share), (height, width)],
+        [arrays[n] for n in mine] + [matrix],
+        [known, known],
+        12 * len(order) * height * share * width,
+        4 * len(order) * height * depth,
+    )
     factors, *blocks = run_kernel(
-        functools.partial(send_kernel, pieces, per, share),
+        functools.partial(send_kernel, pieces, order, per, share),
         [(height, depth)] + [(height, wide)] * (cols - 1),
-        arrays + [matrix],
+        arrays + [mixed, image, matrix],
         [halved, halved],
-        12 * total * share * width + 6 * total * height * depth,
+        12 * (total - len(order) * height) * share * width + 6 * total * height * depth,
         4 * total * depth,
     )
     received = [lax.ppermute(blocks[2], "col", [(1, 2), (2, 1)])]

time: 66.1 us -> 64.6 us (0.977)
  waiting for transfers between devices: 31.1 us -> 28.8 us
  local copies, waits for them, and re-layouts: 0.09 us -> 0.93 us
    ppermute x17, waiting for transfers between devices: 24.1 us -> 22.5 us  [swap(): return lax.ppermute(value, axis, [(i, i ^ offset) for i in range(size)])]
    unnamed x7, local copies, waits for them, and re-layouts: 0.03 us -> 0.88 us
    pallas_call x7 -> x8, Pallas kernels: 7.84 us -> 7.89 us  [run_kernel(): pl.pallas_call(body, out_shape=[jax.ShapeDtypeStruct(shape, jnp.float32)...]
where the time goes in v6:
time: 64.6 us; the launch traced here: 64.4 us
  waiting for transfers between devices  28.8 us (45%)
  starting transfers between devices  25.6 us (40%)
  Pallas kernels  7.89 us (12%)
  other arithmetic  0.96 us (1%)
  local copies, waits for them, and re-layouts  0.93 us (1%)
    ppermute x17, waiting for transfers between devices, swap(): return lax.ppermute(value, axis, [(i, i ^ offset) for i in range(size)])  22.5 us
    ppermute x17, starting transfers between devices, swap(): return lax.ppermute(value, axis, [(i, i ^ offset) for i in range(size)])  17.9 us
    pallas_call x8, Pallas kernels, run_kernel(): pl.pallas_call(body, out_shape=[jax.ShapeDtypeStruct(shape, jnp.float32)...  7.89 us
    ppermute x1, starting transfers between devices, local_square(): received += [lax.ppermute(blocks[1], 'col', [(0, 2), (3, 1)])]  6.61 us
    ppermute x1, waiting for transfers between devices, local_square(): late = lax.ppermute(late, 'col', [(0, 1), (3, 2), (1, 3), (2, 0)])  4.83 us
    ppermute x1, waiting for transfers between devices, local_square(): received += [lax.ppermute(blocks[1], 'col', [(0, 2), (3, 1)])]  1.51 us
  transfers between devices with their start and end apart: 20, of which 9 were waited for; matrix products, arithmetic and copies ran while one was open for 2% of the time, Pallas kernels for 10%

profile of v6, /device:TPU:0, one launch (start us, length us, event | category | flops | bytes accessed | tf_op | source)
XLA Modules:
  0.0 64.4 jit_solution(2236139573940007637)
XLA Ops:
  0.0 3.0 %collective-permute-start.4 = (f32[64,192]{1,0:T(8,128)}, f32[64,192]{1,0:T(8,128)S(1)}, u32[]{:S(2)}, u32[]{:S(2)}) collective-permute-start(f32[64,192]{1,0:T(8,128)} %bitcast.1), channel_id=1, source_target_pairs={{0,1},{1,0},{2,3},{3,2},{4,5},{5,4},{6,7},{7,6},{8,9},{9,8},{10,11... | collective-permute-start | bytes 147464 | tf_op jit(solution)/shard_map/ppermute | solution.py:40
  3.0 1.5 %collective-permute-start.2 = (f32[192,256]{1,0:T(8,128)}, f32[192,256]{1,0:T(8,128)S(1)}, u32[]{:S(2)}, u32[]{:S(2)}) collective-permute-start(f32[192,256]{1,0:T(8,128)} %param.5), channel_id=1, source_target_pairs={{0,16},{4,20},{8,24},{12,28},{16,0},{20,4},{24,8},{28,12},{1,17},{... | collective-permute-start | bytes 589832 | tf_op jit(solution)/shard_map/ppermute | solution.py:40
  4.5 1.5 %collective-permute-start = (f32[192,256]{1,0:T(8,128)}, f32[192,256]{1,0:T(8,128)S(1)}, u32[]{:S(2)}, u32[]{:S(2)}) collective-permute-start(f32[192,256]{1,0:T(8,128)} %param.5), channel_id=1, source_target_pairs={{0,8},{4,12},{8,0},{12,4},{16,24},{20,28},{24,16},{28,20},{1,9},{5... | collective-permute-start | bytes 589832 | tf_op jit(solution)/shard_map/ppermute | solution.py:40
  6.0 0.5 collective-permute-start.3
  6.5 0.5 collective-permute-start.1
  7.1 0.0 collective-permute-done.4
  7.1 0.8 %pad_maximum_fusion.1.refs_0_ = f32[128,192]{1,0:T(8,128)S(1)} fusion(f32[64,192]{1,0:T(8,128)S(1)} %collective-permute-done.4, f32[64,192]{1,0:T(8,128)} %bitcast.2), kind=kLoop, calls=%fused_computation.1 | loop fusion | flops 24576 | bytes 196608 | tf_op jit(solution)/shard_map/concatenate | solution.py:358
  7.9 0.0 copy-start.1
  7.9 2.7 %collective-permute-start.5 = (f32[128,192]{1,0:T(8,128)S(1)}, f32[128,192]{1,0:T(8,128)S(1)}, u32[]{:S(2)}, u32[]{:S(2)}) collective-permute-start(f32[128,192]{1,0:T(8,128)S(1)} %pad_maximum_fusion.1.refs_0_), channel_id=1, source_target_pairs={{0,2},{1,3},{2,0},{3,1},{4,6},{5,7},{6,4},{7,5},{8,10},{9,11},{10,... | collective-permute-start | bytes 294920 | tf_op jit(solution)/shard_map/ppermute | solution.py:40
  10.6 5.0 %collective-permute-done.5.refs_1_ = f32[128,192]{1,0:T(8,128)S(1)} collective-permute-done((f32[128,192]{1,0:T(8,128)S(1)}, f32[128,192]{1,0:T(8,128)S(1)}, u32[]{:S(2)}, u32[]{:S(2)}) %collective-permute-start.5) | collective-permute-done | bytes 98336 | tf_op jit(solution)/shard_map/ppermute | solution.py:40
  15.6 0.0 collective-permute-done.2.left_y
  15.6 0.0 collective-permute-done.left_x
  15.6 0.0 collective-permute-done.3.right_y
  15.6 0.1 shard_map.46
  15.7 1.6 %collective-permute-start.6 = (f32[384,256]{1,0:T(8,128)S(1)}, f32[384,256]{1,0:T(8,128)S(1)}, u32[]{:S(2)}, u32[]{:S(2)}) collective-permute-start(f32[384,256]{1,0:T(8,128)S(1)} %get-tuple-element.23), channel_id=1, source_target_pairs={{0,8},{4,12},{8,0},{12,4},{16,24},{20,28},{24,16},{28,20},{1,9},{5... | collective-permute-start | bytes 1179656 | tf_op jit(solution)/shard_map/ppermute | solution.py:40
  17.3 1.5 %collective-permute-start.7 = (f32[384,256]{1,0:T(8,128)S(1)}, f32[384,256]{1,0:T(8,128)S(1)}, u32[]{:S(2)}, u32[]{:S(2)}) collective-permute-start(f32[384,256]{1,0:T(8,128)S(1)} %get-tuple-element.24), channel_id=1, source_target_pairs={{0,16},{4,20},{8,24},{12,28},{16,0},{20,4},{24,8},{28,12},{1,17},{... | collective-permute-start | bytes 1179656 | tf_op jit(solution)/shard_map/ppermute | solution.py:40
  18.8 0.0 copy-start
  18.9 0.1 collective-permute-start.9
  19.0 0.8 %copy-done = f32[192,384]{1,0:T(8,128)S(1)} copy-done((f32[192,384]{1,0:T(8,128)S(1)}, f32[192,384]{1,0:T(8,128)}, u32[]{:S(2)}) %copy-start) | copy-done | bytes 294936
  19.8 0.4 shard_map.47
  20.2 0.1 collective-permute-start.10
  20.3 0.9 %collective-permute-start.8 = (f32[192,256]{1,0:T(8,128)S(1)}, f32[192,256]{1,0:T(8,128)S(1)}, u32[]{:S(2)}, u32[]{:S(2)}) collective-permute-start(f32[192,256]{1,0:T(8,128)S(1)} %slice.9), channel_id=1, source_target_pairs={{0,24},{4,28},{8,16},{12,20},{16,8},{20,12},{24,0},{28,4},{1,25},{... | collective-permute-start | bytes 589832 | tf_op jit(solution)/shard_map/ppermute | solution.py:40
  21.2 9.8 %collective-permute-done.8 = f32[192,256]{1,0:T(8,128)S(1)} collective-permute-done((f32[192,256]{1,0:T(8,128)S(1)}, f32[192,256]{1,0:T(8,128)S(1)}, u32[]{:S(2)}, u32[]{:S(2)}) %collective-permute-start.8) | collective-permute-done | bytes 196640 | tf_op jit(solution)/shard_map/ppermute | solution.py:40
  31.0 0.0 collective-permute-start.11
  31.0 0.0 collective-permute-done.6
  31.0 0.1 collective-permute-done.7
  31.2 0.1 pad_maximum_fusion.refs_2_.refs_4_
  31.2 0.0 collective-permute-done.9.refs_1_
  31.3 0.4 collective-permute-start.12
  31.7 1.5 %collective-permute-start.16 = (f32[256,384]{1,0:T(8,128)S(1)}, f32[256,384]{1,0:T(8,128)S(1)}, u32[]{:S(2)}, u32[]{:S(2)}) collective-permute-start(f32[256,384]{1,0:T(8,128)S(1)} %add.3.sides), channel_id=1, source_target_pairs={{0,8},{4,12},{8,0},{12,4},{16,24},{20,28},{24,16},{28,20},{1,9},{5... | collective-permute-start | bytes 1179656 | tf_op jit(solution)/shard_map/ppermute | solution.py:40
  33.2 1.0 %shard_map.48 = (f32[256,512]{1,0:T(8,128)S(1)}, f32[192,256]{1,0:T(8,128)S(1)}) custom-call(f32[384,256]{1,0:T(8,128)S(1)} %constant_dynamic-update-slice_fusion.refs_0_, f32[960,256]{1,0:T(8,128)S(1)} %get-tuple-element.25.near.refs_1_.refs_2_.refs_6_, f32[960,256]{1,0:T(8,128)S(1)} %pad_maximum_fusion.refs_2_.refs_4_, f32[192,384]{1,0:T(8,128)S(1)} %copy-done), custom_call_target="tpu_custom_call" | custom-call | flops 603979776 | bytes 2359296 | tf_op jit(solution)/shard_map/pallas_call | solution.py:302
  34.2 0.8 %collective-permute-done.12.refs_5_ = f32[960,256]{1,0:T(8,128)S(1)} collective-permute-done((f32[960,256]{1,0:T(8,128)S(1)}, f32[960,256]{1,0:T(8,128)S(1)}, u32[]{:S(2)}, u32[]{:S(2)}) %collective-permute-start.12) | collective-permute-done | bytes 983072 | tf_op jit(solution)/shard_map/ppermute | solution.py:40
  35.0 3.5 %shard_map.49 = (f32[192,768]{1,0:T(8,128)S(1)}, f32[192,384]{1,0:T(8,128)S(1)}, f32[192,384]{1,0:T(8,128)S(1)}, f32[192,384]{1,0:T(8,128)S(1)}) custom-call(f32[384,256]{1,0:T(8,128)S(1)} %constant_dynamic-update-slice_fusion.refs_0_, f32[384,256]{1,0:T(8,128)S(1)} %collective-permute-done.9.refs_1_, ...), custom_call_target="tpu_custom_call" | custom-call | flops 1962934272 | bytes 4718592 | tf_op jit(solution)/shard_map/pallas_call | solution.py:302
  38.5 0.1 collective-permute-start.15
  38.5 0.7 %collective-permute-start.13 = (f32[192,384]{1,0:T(8,128)S(1)}, f32[192,384]{1,0:T(8,128)S(1)}, u32[]{:S(2)}, u32[]{:S(2)}) collective-permute-start(f32[192,384]{1,0:T(8,128)S(1)} %get-tuple-element.30.other), channel_id=1, source_target_pairs={{1,2},{2,1},{5,6},{6,5},{9,10},{10,9},{13,14},{14,13},{17,18},{18,... | collective-permute-start | bytes 884744 | tf_op jit(solution)/shard_map/ppermute | solution.py:390
  39.2 6.6 %collective-permute-start.14 = (f32[192,384]{1,0:T(8,128)S(1)}, f32[192,384]{1,0:T(8,128)S(1)}, u32[]{:S(2)}, u32[]{:S(2)}) collective-permute-start(f32[192,384]{1,0:T(8,128)S(1)} %get-tuple-element.31.across), channel_id=1, source_target_pairs={{0,2},{3,1},{4,6},{7,5},{8,10},{11,9},{12,14},{15,13},{16,18},{19,... | collective-permute-start | bytes 884744 | tf_op jit(solution)/shard_map/ppermute | solution.py:392
  45.9 1.7 %collective-permute-done.15.passed.refs_2_ = f32[192,384]{1,0:T(8,128)S(1)} collective-permute-done((f32[192,384]{1,0:T(8,128)S(1)}, f32[192,384]{1,0:T(8,128)S(1)}, u32[]{:S(2)}, u32[]{:S(2)}) %collective-permute-start.15) | collective-permute-done | bytes 294944 | tf_op jit(solution)/shard_map/ppermute | solution.py:40
  47.6 0.1 shard_map.52
  47.6 0.3 collective-permute-start.19
  48.0 0.6 collective-permute-start.18
  48.6 1.5 %collective-permute-start.17 = (f32[128,384]{1,0:T(8,128)S(1)}, f32[128,384]{1,0:T(8,128)S(1)}, u32[]{:S(2)}, u32[]{:S(2)}) collective-permute-start(f32[128,384]{1,0:T(8,128)S(1)} %get-tuple-element.42), channel_id=1, source_target_pairs={{0,16},{4,20},{8,24},{12,28},{16,0},{20,4},{24,8},{28,12},{1,17},{... | collective-permute-start | bytes 589832 | tf_op jit(solution)/shard_map/ppermute | solution.py:40
  50.1 1.6 %shard_map.50.refs_2_ = f32[192,384]{1,0:T(8,128)S(1)} custom-call(f32[384,256]{1,0:T(8,128)S(1)} %constant_dynamic-update-slice_fusion.refs_0_, f32[384,256]{1,0:T(8,128)S(1)} %collective-permute-done.9.refs_1_, f32[960,256]{1,0:T(8,128)S(1)} %get-tuple-element.25.near.refs_1_.refs_2_.refs_6_, f32[960,256]{1,0:T(8,128)S(1)} %collective-permute-done.11.refs_3_, ...), custom_call_target="tpu_custom_call" | custom-call | flops 339738624 | bytes 4718592 | tf_op jit(solution)/shard_map/pallas_call | solution.py:302
  51.7 1.5 %collective-permute-done.14.refs_1_ = f32[192,384]{1,0:T(8,128)S(1)} collective-permute-done((f32[192,384]{1,0:T(8,128)S(1)}, f32[192,384]{1,0:T(8,128)S(1)}, u32[]{:S(2)}, u32[]{:S(2)}) %collective-permute-start.14) | collective-permute-done | bytes 294944 | tf_op jit(solution)/shard_map/ppermute | solution.py:392
  53.3 0.1 shard_map.51.refs_0_
  53.3 2.6 %collective-permute-done.18.refs_5_ = f32[128,384]{1,0:T(8,128)S(1)} collective-permute-done((f32[128,384]{1,0:T(8,128)S(1)}, f32[128,384]{1,0:T(8,128)S(1)}, u32[]{:S(2)}, u32[]{:S(2)}) %collective-permute-start.18) | collective-permute-done | bytes 196640 | tf_op jit(solution)/shard_map/ppermute | solution.py:40
  55.9 2.5 %collective-permute-done.17.refs_4_ = f32[128,384]{1,0:T(8,128)S(1)} collective-permute-done((f32[128,384]{1,0:T(8,128)S(1)}, f32[128,384]{1,0:T(8,128)S(1)}, u32[]{:S(2)}, u32[]{:S(2)}) %collective-permute-start.17) | collective-permute-done | bytes 196640 | tf_op jit(solution)/shard_map/ppermute | solution.py:40
  58.5 4.8 %collective-permute-done.19.refs_1_ = f32[192,384]{1,0:T(8,128)S(1)} collective-permute-done((f32[192,384]{1,0:T(8,128)S(1)}, f32[192,384]{1,0:T(8,128)S(1)}, u32[]{:S(2)}, u32[]{:S(2)}) %collective-permute-start.19) | collective-permute-done | bytes 294944 | tf_op jit(solution)/shard_map/ppermute | solution.py:398
  63.3 1.1 %shard_map.53 = f32[192,384]{1,0:T(8,128)} custom-call(f32[192,384]{1,0:T(8,128)S(1)} %shard_map.51.refs_0_, f32[192,384]{1,0:T(8,128)S(1)} %collective-permute-done.19.refs_1_, f32[192,384]{1,0:T(8,128)S(1)} %collective-permute-done.15.passed.refs_2_, f32[256,384]{1,0:T(8,128)S(1)} %get-tuple-element.35.refs_3_, ...), custom_call_target="tpu_custom_call" | custom-call | flops 113246208 | bytes 786432 | tf_op jit(solution)/shard_map/pallas_call | solution.py:302
  (13 shorter events, 0.1 us)
Async XLA Ops:
  0.0 7.1 %collective-permute-start.4 = (f32[64,192]{1,0:T(8,128)}, f32[64,192]{1,0:T(8,128)S(1)}, u32[]{:S(2)}, u32[]{:S(2)}) collective-permute-start(f32[64,192]{1,0:T(8,128)} %bitcast.1), channel_id=1, source_target_pairs={{0,1},{1,0},{2,3},{3,2},{4,5},{5,4},{6,7},{7,6},{8,9},{9,8},{10,11... | collective-permute-start | bytes 147464 | tf_op jit(solution)/shard_map/ppermute | solution.py:40
  3.0 12.5 %collective-permute-start.2 = (f32[192,256]{1,0:T(8,128)}, f32[192,256]{1,0:T(8,128)S(1)}, u32[]{:S(2)}, u32[]{:S(2)}) collective-permute-start(f32[192,256]{1,0:T(8,128)} %param.5), channel_id=1, source_target_pairs={{0,16},{4,20},{8,24},{12,28},{16,0},{20,4},{24,8},{28,12},{1,17},{... | collective-permute-start | bytes 589832 | tf_op jit(solution)/shard_map/ppermute | solution.py:40
  4.5 11.0 %collective-permute-start = (f32[192,256]{1,0:T(8,128)}, f32[192,256]{1,0:T(8,128)S(1)}, u32[]{:S(2)}, u32[]{:S(2)}) collective-permute-start(f32[192,256]{1,0:T(8,128)} %param.5), channel_id=1, source_target_pairs={{0,8},{4,12},{8,0},{12,4},{16,24},{20,28},{24,16},{28,20},{1,9},{5... | collective-permute-start | bytes 589832 | tf_op jit(solution)/shard_map/ppermute | solution.py:40
  6.0 9.5 %collective-permute-start.3 = (f32[192,256]{1,0:T(8,128)}, f32[192,256]{1,0:T(8,128)S(1)}, u32[]{:S(2)}, u32[]{:S(2)}) collective-permute-start(f32[192,256]{1,0:T(8,128)} %param.6), channel_id=1, source_target_pairs={{0,16},{4,20},{8,24},{12,28},{16,0},{20,4},{24,8},{28,12},{1,17},{... | collective-permute-start | bytes 589832 | tf_op jit(solution)/shard_map/ppermute | solution.py:40
  6.5 9.0 %collective-permute-start.1 = (f32[192,256]{1,0:T(8,128)}, f32[192,256]{1,0:T(8,128)S(1)}, u32[]{:S(2)}, u32[]{:S(2)}) collective-permute-start(f32[192,256]{1,0:T(8,128)} %param.6), channel_id=1, source_target_pairs={{0,8},{4,12},{8,0},{12,4},{16,24},{20,28},{24,16},{28,20},{1,9},{5... | collective-permute-start | bytes 589832 | tf_op jit(solution)/shard_map/ppermute | solution.py:40
  7.9 10.9 %copy-start.1 = (f32[192,256]{1,0:T(8,128)S(1)}, f32[192,256]{1,0:T(8,128)}, u32[]{:S(2)}) copy-start(f32[192,256]{1,0:T(8,128)} %param.5) | copy-start | bytes 589828
  7.9 7.6 %collective-permute-start.5 = (f32[128,192]{1,0:T(8,128)S(1)}, f32[128,192]{1,0:T(8,128)S(1)}, u32[]{:S(2)}, u32[]{:S(2)}) collective-permute-start(f32[128,192]{1,0:T(8,128)S(1)} %pad_maximum_fusion.1.refs_0_), channel_id=1, source_target_pairs={{0,2},{1,3},{2,0},{3,1},{4,6},{5,7},{6,4},{7,5},{8,10},{9,11},{10,... | collective-permute-start | bytes 294920 | tf_op jit(solution)/shard_map/ppermute | solution.py:40
  15.7 15.3 %collective-permute-start.6 = (f32[384,256]{1,0:T(8,128)S(1)}, f32[384,256]{1,0:T(8,128)S(1)}, u32[]{:S(2)}, u32[]{:S(2)}) collective-permute-start(f32[384,256]{1,0:T(8,128)S(1)} %get-tuple-element.23), channel_id=1, source_target_pairs={{0,8},{4,12},{8,0},{12,4},{16,24},{20,28},{24,16},{28,20},{1,9},{5... | collective-permute-start | bytes 1179656 | tf_op jit(solution)/shard_map/ppermute | solution.py:40
  17.3 1.5 %copy-start.2 = (f32[192,256]{1,0:T(8,128)S(1)}, f32[192,256]{1,0:T(8,128)}, u32[]{:S(2)}) copy-start(f32[192,256]{1,0:T(8,128)} %param.6) | copy-start | bytes 589828
  17.3 13.9 %collective-permute-start.7 = (f32[384,256]{1,0:T(8,128)S(1)}, f32[384,256]{1,0:T(8,128)S(1)}, u32[]{:S(2)}, u32[]{:S(2)}) collective-permute-start(f32[384,256]{1,0:T(8,128)S(1)} %get-tuple-element.24), channel_id=1, source_target_pairs={{0,16},{4,20},{8,24},{12,28},{16,0},{20,4},{24,8},{28,12},{1,17},{... | collective-permute-start | bytes 1179656 | tf_op jit(solution)/shard_map/ppermute | solution.py:40
  18.8 1.0 %copy-start = (f32[192,384]{1,0:T(8,128)S(1)}, f32[192,384]{1,0:T(8,128)}, u32[]{:S(2)}) copy-start(f32[192,384]{1,0:T(8,128)} %refs_7_.1) | copy-start | bytes 884740
  18.9 12.4 %collective-permute-start.9 = (f32[384,256]{1,0:T(8,128)S(1)}, f32[384,256]{1,0:T(8,128)S(1)}, u32[]{:S(2)}, u32[]{:S(2)}) collective-permute-start(f32[384,256]{1,0:T(8,128)S(1)} %constant_dynamic-update-slice_fusion.refs_0_), channel_id=1, source_target_pairs={{0,4},{4,0},{8,12},{12,8},{16,20},{20,16},{24,28},{28,24},{1,5},{5... | collective-permute-start | bytes 1179656 | tf_op jit(solution)/shard_map/ppermute | solution.py:40
  20.2 11.1 %collective-permute-start.10 = (f32[256,384]{1,0:T(8,128)S(1)}, f32[256,384]{1,0:T(8,128)S(1)}, u32[]{:S(2)}, u32[]{:S(2)}) collective-permute-start(f32[256,384]{1,0:T(8,128)S(1)} %shard_map.47), channel_id=1, source_target_pairs={{0,4},{4,0},{8,12},{12,8},{16,20},{20,16},{24,28},{28,24},{1,5},{5... | collective-permute-start | bytes 1179656 | tf_op jit(solution)/shard_map/ppermute | solution.py:40
  20.3 10.7 %collective-permute-start.8 = (f32[192,256]{1,0:T(8,128)S(1)}, f32[192,256]{1,0:T(8,128)S(1)}, u32[]{:S(2)}, u32[]{:S(2)}) collective-permute-start(f32[192,256]{1,0:T(8,128)S(1)} %slice.9), channel_id=1, source_target_pairs={{0,24},{4,28},{8,16},{12,20},{16,8},{20,12},{24,0},{28,4},{1,25},{... | collective-permute-start | bytes 589832 | tf_op jit(solution)/shard_map/ppermute | solution.py:40
  31.0 3.2 %collective-permute-start.11 = (f32[960,256]{1,0:T(8,128)S(1)}, f32[960,256]{1,0:T(8,128)S(1)}, u32[]{:S(2)}, u32[]{:S(2)}) collective-permute-start(f32[960,256]{1,0:T(8,128)S(1)} %get-tuple-element.25.near.refs_1_.refs_2_.refs_6_), channel_id=1, source_target_pairs={{0,4},{4,0},{8,12},{12,8},{16,20},{20,16},{24,28},{28,24},{1,5},{5... | collective-permute-start | bytes 2949128 | tf_op jit(solution)/shard_map/ppermute | solution.py:40
  31.3 3.7 %collective-permute-start.12 = (f32[960,256]{1,0:T(8,128)S(1)}, f32[960,256]{1,0:T(8,128)S(1)}, u32[]{:S(2)}, u32[]{:S(2)}) collective-permute-start(f32[960,256]{1,0:T(8,128)S(1)} %pad_maximum_fusion.refs_2_.refs_4_), channel_id=1, source_target_pairs={{0,4},{4,0},{8,12},{12,8},{16,20},{20,16},{24,28},{28,24},{1,5},{5... | collective-permute-start | bytes 2949128 | tf_op jit(solution)/shard_map/ppermute | solution.py:40
  31.7 14.1 %collective-permute-start.16 = (f32[256,384]{1,0:T(8,128)S(1)}, f32[256,384]{1,0:T(8,128)S(1)}, u32[]{:S(2)}, u32[]{:S(2)}) collective-permute-start(f32[256,384]{1,0:T(8,128)S(1)} %add.3.sides), channel_id=1, source_target_pairs={{0,8},{4,12},{8,0},{12,4},{16,24},{20,28},{24,16},{28,20},{1,9},{5... | collective-permute-start | bytes 1179656 | tf_op jit(solution)/shard_map/ppermute | solution.py:40
  38.5 9.1 %collective-permute-start.15 = (f32[192,384]{1,0:T(8,128)S(1)}, f32[192,384]{1,0:T(8,128)S(1)}, u32[]{:S(2)}, u32[]{:S(2)}) collective-permute-start(f32[192,384]{1,0:T(8,128)S(1)} %get-tuple-element.33), channel_id=1, source_target_pairs={{0,1},{1,0},{2,3},{3,2},{4,5},{5,4},{6,7},{7,6},{8,9},{9,8},{10,11... | collective-permute-start | bytes 884744 | tf_op jit(solution)/shard_map/ppermute | solution.py:40
  38.5 13.2 %collective-permute-start.13 = (f32[192,384]{1,0:T(8,128)S(1)}, f32[192,384]{1,0:T(8,128)S(1)}, u32[]{:S(2)}, u32[]{:S(2)}) collective-permute-start(f32[192,384]{1,0:T(8,128)S(1)} %get-tuple-element.30.other), channel_id=1, source_target_pairs={{1,2},{2,1},{5,6},{6,5},{9,10},{10,9},{13,14},{14,13},{17,18},{18,... | collective-permute-start | bytes 884744 | tf_op jit(solution)/shard_map/ppermute | solution.py:390
  39.2 14.0 %collective-permute-start.14 = (f32[192,384]{1,0:T(8,128)S(1)}, f32[192,384]{1,0:T(8,128)S(1)}, u32[]{:S(2)}, u32[]{:S(2)}) collective-permute-start(f32[192,384]{1,0:T(8,128)S(1)} %get-tuple-element.31.across), channel_id=1, source_target_pairs={{0,2},{3,1},{4,6},{7,5},{8,10},{11,9},{12,14},{15,13},{16,18},{19,... | collective-permute-start | bytes 884744 | tf_op jit(solution)/shard_map/ppermute | solution.py:392
  47.6 15.6 %collective-permute-start.19 = (f32[192,384]{1,0:T(8,128)S(1)}, f32[192,384]{1,0:T(8,128)S(1)}, u32[]{:S(2)}, u32[]{:S(2)}) collective-permute-start(f32[192,384]{1,0:T(8,128)S(1)} %get-tuple-element.36), channel_id=1, source_target_pairs={{0,1},{3,2},{1,3},{2,0},{4,5},{7,6},{5,7},{6,4},{8,9},{11,10},{9,1... | collective-permute-start | bytes 884744 | tf_op jit(solution)/shard_map/ppermute | solution.py:398
  48.0 7.9 %collective-permute-start.18 = (f32[128,384]{1,0:T(8,128)S(1)}, f32[128,384]{1,0:T(8,128)S(1)}, u32[]{:S(2)}, u32[]{:S(2)}) collective-permute-start(f32[128,384]{1,0:T(8,128)S(1)} %get-tuple-element.41), channel_id=1, source_target_pairs={{0,16},{4,20},{8,24},{12,28},{16,0},{20,4},{24,8},{28,12},{1,17},{... | collective-permute-start | bytes 589832 | tf_op jit(solution)/shard_map/ppermute | solution.py:40
  48.6 9.8 %collective-permute-start.17 = (f32[128,384]{1,0:T(8,128)S(1)}, f32[128,384]{1,0:T(8,128)S(1)}, u32[]{:S(2)}, u32[]{:S(2)}) collective-permute-start(f32[128,384]{1,0:T(8,128)S(1)} %get-tuple-element.42), channel_id=1, source_target_pairs={{0,16},{4,20},{8,24},{12,28},{16,0},{20,4},{24,8},{28,12},{1,17},{... | collective-permute-start | bytes 589832 | tf_op jit(solution)/shard_map/ppermute | solution.py:40

commit v7 on v6

--- a/solution.py
+++ b/solution.py
@@ -282,8 +282,14 @@
         out[...] = passed[...] + across[...]
 
 
-def last_kernel(per, *refs):
-    summed, late, passed, sides, *parts, near, out, made = refs
+def image_kernel(summed, sides, *refs):
+    *parts, near, out = refs
+    refl = near[: out.shape[0], :]
+    whole = sides[...] + jnp.concatenate([part[...] for part in parts], axis=0)
+    out[...] = summed[...] - pair_dot(halves(refl), halves(whole), OVER)
+
+
+def last_kernel(per, summed, late, passed, out, made):
     _, first = place_in_kernel(per)
     made[...] = late[...]
 
@@ -292,9 +298,6 @@
         made[...] = made[...] + passed[...]
 
     put_in_order(out, summed, made, first, per)
-    refl = near[: out.shape[0], :]
-    whole = sides[...] + jnp.concatenate([part[...] for part in parts], axis=0)
-    out[...] = out[...] - pair_dot(halves(refl), halves(whole), OVER)
 
 
 def run_kernel(body, outs, args, scratch=(), flops=0, moved=0):
@@ -413,14 +416,22 @@
         height * wide * cols,
         16 * height * wide * (cols + 1),
     )
-    summed, parts, late = lax.optimization_barrier((summed, parts, late))
+    summed, parts = lax.optimization_barrier((summed, parts))
+    (summed,) = run_kernel(
+        image_kernel,
+        [(height, wide)],
+        [summed, sides, *parts, near],
+        (),
+        6 * height * width * wide,
+        4 * width * wide * 2,
+    )
     (updated,) = run_kernel(
         functools.partial(last_kernel, per),
         [(height, wide)],
-        [summed, late, passed, sides, *parts, near],
+        [summed, late, passed],
         [block],
-        6 * height * width * wide,
-        4 * width * wide * 2,
+        2 * height * wide,
+        16 * height * wide,
     )
     return updated
 

time: 64.6 us -> 64.3 us (level)
    pallas_call x8 -> x9, Pallas kernels: 7.89 us -> 7.88 us  [run_kernel(): pl.pallas_call(body, out_shape=[jax.ShapeDtypeStruct(shape, jnp.float32)...]
  transfers between devices with their start and end apart: 20 -> 20, of which waited for: 9 -> 9; matrix products, arithmetic and copies ran while one was open for 2% -> 2% of each run, Pallas kernels for 10% -> 11%
where the time goes in v7:
time: 64.3 us; the launch traced here: 64.1 us
  waiting for transfers between devices  28.5 us (44%)
  starting transfers between devices  25.6 us (40%)
  Pallas kernels  7.88 us (12%)
  other arithmetic  0.96 us (1%)
  local copies, waits for them, and re-layouts  0.93 us (1%)
    ppermute x17, waiting for transfers between devices, swap(): return lax.ppermute(value, axis, [(i, i ^ offset) for i in range(size)])  22.5 us
    ppermute x17, starting transfers between devices, swap(): return lax.ppermute(value, axis, [(i, i ^ offset) for i in range(size)])  17.9 us
    pallas_call x9, Pallas kernels, run_kernel(): pl.pallas_call(body, out_shape=[jax.ShapeDtypeStruct(shape, jnp.float32)...  7.88 us
    ppermute x1, starting transfers between devices, local_square(): received += [lax.ppermute(blocks[1], 'col', [(0, 2), (3, 1)])]  6.61 us
    ppermute x1, waiting for transfers between devices, local_square(): late = lax.ppermute(late, 'col', [(0, 1), (3, 2), (1, 3), (2, 0)])  4.49 us
    ppermute x1, waiting for transfers between devices, local_square(): received += [lax.ppermute(blocks[1], 'col', [(0, 2), (3, 1)])]  1.51 us
  transfers between devices with their start and end apart: 20, of which 9 were waited for; matrix products, arithmetic and copies ran while one was open for 2% of the time, Pallas kernels for 11%

profile of v7, /device:TPU:0, one launch (start us, length us, event | category | flops | bytes accessed | tf_op | source)
XLA Modules:
  0.0 64.1 jit_solution(14375592524500063375)
XLA Ops:
  0.0 3.0 %collective-permute-start.4 = (f32[64,192]{1,0:T(8,128)}, f32[64,192]{1,0:T(8,128)S(1)}, u32[]{:S(2)}, u32[]{:S(2)}) collective-permute-start(f32[64,192]{1,0:T(8,128)} %bitcast.1), channel_id=1, source_target_pairs={{0,1},{1,0},{2,3},{3,2},{4,5},{5,4},{6,7},{7,6},{8,9},{9,8},{10,11... | collective-permute-start | bytes 147464 | tf_op jit(solution)/shard_map/ppermute | solution.py:40
  3.0 1.5 %collective-permute-start.2 = (f32[192,256]{1,0:T(8,128)}, f32[192,256]{1,0:T(8,128)S(1)}, u32[]{:S(2)}, u32[]{:S(2)}) collective-permute-start(f32[192,256]{1,0:T(8,128)} %param.5), channel_id=1, source_target_pairs={{0,16},{4,20},{8,24},{12,28},{16,0},{20,4},{24,8},{28,12},{1,17},{... | collective-permute-start | bytes 589832 | tf_op jit(solution)/shard_map/ppermute | solution.py:40
  4.5 1.5 %collective-permute-start = (f32[192,256]{1,0:T(8,128)}, f32[192,256]{1,0:T(8,128)S(1)}, u32[]{:S(2)}, u32[]{:S(2)}) collective-permute-start(f32[192,256]{1,0:T(8,128)} %param.5), channel_id=1, source_target_pairs={{0,8},{4,12},{8,0},{12,4},{16,24},{20,28},{24,16},{28,20},{1,9},{5... | collective-permute-start | bytes 589832 | tf_op jit(solution)/shard_map/ppermute | solution.py:40
  6.0 0.5 collective-permute-start.3
  6.5 0.5 collective-permute-start.1
  7.1 0.0 collective-permute-done.4
  7.1 0.8 %pad_maximum_fusion.1.refs_0_ = f32[128,192]{1,0:T(8,128)S(1)} fusion(f32[64,192]{1,0:T(8,128)S(1)} %collective-permute-done.4, f32[64,192]{1,0:T(8,128)} %bitcast.2), kind=kLoop, calls=%fused_computation.1 | loop fusion | flops 24576 | bytes 196608 | tf_op jit(solution)/shard_map/concatenate | solution.py:361
  7.9 0.0 copy-start.1
  7.9 2.7 %collective-permute-start.5 = (f32[128,192]{1,0:T(8,128)S(1)}, f32[128,192]{1,0:T(8,128)S(1)}, u32[]{:S(2)}, u32[]{:S(2)}) collective-permute-start(f32[128,192]{1,0:T(8,128)S(1)} %pad_maximum_fusion.1.refs_0_), channel_id=1, source_target_pairs={{0,2},{1,3},{2,0},{3,1},{4,6},{5,7},{6,4},{7,5},{8,10},{9,11},{10,... | collective-permute-start | bytes 294920 | tf_op jit(solution)/shard_map/ppermute | solution.py:40
  10.6 5.0 %collective-permute-done.5.refs_1_ = f32[128,192]{1,0:T(8,128)S(1)} collective-permute-done((f32[128,192]{1,0:T(8,128)S(1)}, f32[128,192]{1,0:T(8,128)S(1)}, u32[]{:S(2)}, u32[]{:S(2)}) %collective-permute-start.5) | collective-permute-done | bytes 98336 | tf_op jit(solution)/shard_map/ppermute | solution.py:40
  15.6 0.0 collective-permute-done.2.left_y
  15.6 0.0 collective-permute-done.left_x
  15.6 0.0 collective-permute-done.3.right_y
  15.6 0.1 shard_map.46
  15.7 1.6 %collective-permute-start.6 = (f32[384,256]{1,0:T(8,128)S(1)}, f32[384,256]{1,0:T(8,128)S(1)}, u32[]{:S(2)}, u32[]{:S(2)}) collective-permute-start(f32[384,256]{1,0:T(8,128)S(1)} %get-tuple-element.22), channel_id=1, source_target_pairs={{0,8},{4,12},{8,0},{12,4},{16,24},{20,28},{24,16},{28,20},{1,9},{5... | collective-permute-start | bytes 1179656 | tf_op jit(solution)/shard_map/ppermute | solution.py:40
  17.3 1.5 %collective-permute-start.7 = (f32[384,256]{1,0:T(8,128)S(1)}, f32[384,256]{1,0:T(8,128)S(1)}, u32[]{:S(2)}, u32[]{:S(2)}) collective-permute-start(f32[384,256]{1,0:T(8,128)S(1)} %get-tuple-element.23), channel_id=1, source_target_pairs={{0,16},{4,20},{8,24},{12,28},{16,0},{20,4},{24,8},{28,12},{1,17},{... | collective-permute-start | bytes 1179656 | tf_op jit(solution)/shard_map/ppermute | solution.py:40
  18.8 0.0 copy-start
  18.9 0.1 collective-permute-start.9
  19.0 0.8 %copy-done = f32[192,384]{1,0:T(8,128)S(1)} copy-done((f32[192,384]{1,0:T(8,128)S(1)}, f32[192,384]{1,0:T(8,128)}, u32[]{:S(2)}) %copy-start) | copy-done | bytes 294936
  19.8 0.4 shard_map.47
  20.2 0.1 collective-permute-start.10
  20.3 0.9 %collective-permute-start.8 = (f32[192,256]{1,0:T(8,128)S(1)}, f32[192,256]{1,0:T(8,128)S(1)}, u32[]{:S(2)}, u32[]{:S(2)}) collective-permute-start(f32[192,256]{1,0:T(8,128)S(1)} %slice.9), channel_id=1, source_target_pairs={{0,24},{4,28},{8,16},{12,20},{16,8},{20,12},{24,0},{28,4},{1,25},{... | collective-permute-start | bytes 589832 | tf_op jit(solution)/shard_map/ppermute | solution.py:40
  21.2 9.8 %collective-permute-done.8 = f32[192,256]{1,0:T(8,128)S(1)} collective-permute-done((f32[192,256]{1,0:T(8,128)S(1)}, f32[192,256]{1,0:T(8,128)S(1)}, u32[]{:S(2)}, u32[]{:S(2)}) %collective-permute-start.8) | collective-permute-done | bytes 196640 | tf_op jit(solution)/shard_map/ppermute | solution.py:40
  31.0 0.0 collective-permute-start.11
  31.0 0.0 collective-permute-done.6
  31.0 0.1 collective-permute-done.7
  31.2 0.1 pad_maximum_fusion.refs_2_.refs_4_
  31.3 0.4 collective-permute-start.12
  31.7 1.5 %collective-permute-start.16 = (f32[256,384]{1,0:T(8,128)S(1)}, f32[256,384]{1,0:T(8,128)S(1)}, u32[]{:S(2)}, u32[]{:S(2)}) collective-permute-start(f32[256,384]{1,0:T(8,128)S(1)} %add.3.sides), channel_id=1, source_target_pairs={{0,8},{4,12},{8,0},{12,4},{16,24},{20,28},{24,16},{28,20},{1,9},{5... | collective-permute-start | bytes 1179656 | tf_op jit(solution)/shard_map/ppermute | solution.py:40
  33.2 1.0 %shard_map.48 = (f32[256,512]{1,0:T(8,128)S(1)}, f32[192,256]{1,0:T(8,128)S(1)}) custom-call(f32[384,256]{1,0:T(8,128)S(1)} %constant_dynamic-update-slice_fusion.refs_0_, f32[960,256]{1,0:T(8,128)S(1)} %get-tuple-element.24.near.refs_1_.refs_2_, f32[960,256]{1,0:T(8,128)S(1)} %pad_maximum_fusion.refs_2_.refs_4_, f32[192,384]{1,0:T(8,128)S(1)} %copy-done), custom_call_target="tpu_custom_call" | custom-call | flops 603979776 | bytes 2359296 | tf_op jit(solution)/shard_map/pallas_call | solution.py:305
  34.2 0.8 %collective-permute-done.12.refs_5_ = f32[960,256]{1,0:T(8,128)S(1)} collective-permute-done((f32[960,256]{1,0:T(8,128)S(1)}, f32[960,256]{1,0:T(8,128)S(1)}, u32[]{:S(2)}, u32[]{:S(2)}) %collective-permute-start.12) | collective-permute-done | bytes 983072 | tf_op jit(solution)/shard_map/ppermute | solution.py:40
  35.0 3.5 %shard_map.49 = (f32[192,768]{1,0:T(8,128)S(1)}, f32[192,384]{1,0:T(8,128)S(1)}, f32[192,384]{1,0:T(8,128)S(1)}, f32[192,384]{1,0:T(8,128)S(1)}) custom-call(f32[384,256]{1,0:T(8,128)S(1)} %constant_dynamic-update-slice_fusion.refs_0_, f32[384,256]{1,0:T(8,128)S(1)} %collective-permute-done.9.refs_1_, f32[960,256]{1,0:T(8,128)S(1)} %get-tuple-element.24.near.refs_1_.refs_2_, ...), custom_call_target="tpu_custom_call" | custom-call | flops 1962934272 | bytes 4718592 | tf_op jit(solution)/shard_map/pallas_call | solution.py:305
  38.5 0.1 collective-permute-start.15
  38.5 0.7 %collective-permute-start.13 = (f32[192,384]{1,0:T(8,128)S(1)}, f32[192,384]{1,0:T(8,128)S(1)}, u32[]{:S(2)}, u32[]{:S(2)}) collective-permute-start(f32[192,384]{1,0:T(8,128)S(1)} %get-tuple-element.29.other), channel_id=1, source_target_pairs={{1,2},{2,1},{5,6},{6,5},{9,10},{10,9},{13,14},{14,13},{17,18},{18,... | collective-permute-start | bytes 884744 | tf_op jit(solution)/shard_map/ppermute | solution.py:393
  39.2 6.6 %collective-permute-start.14 = (f32[192,384]{1,0:T(8,128)S(1)}, f32[192,384]{1,0:T(8,128)S(1)}, u32[]{:S(2)}, u32[]{:S(2)}) collective-permute-start(f32[192,384]{1,0:T(8,128)S(1)} %get-tuple-element.30.across), channel_id=1, source_target_pairs={{0,2},{3,1},{4,6},{7,5},{8,10},{11,9},{12,14},{15,13},{16,18},{19,... | collective-permute-start | bytes 884744 | tf_op jit(solution)/shard_map/ppermute | solution.py:395
  45.9 1.7 %collective-permute-done.15.passed = f32[192,384]{1,0:T(8,128)S(1)} collective-permute-done((f32[192,384]{1,0:T(8,128)S(1)}, f32[192,384]{1,0:T(8,128)S(1)}, u32[]{:S(2)}, u32[]{:S(2)}) %collective-permute-start.15) | collective-permute-done | bytes 294944 | tf_op jit(solution)/shard_map/ppermute | solution.py:40
  47.6 0.1 shard_map.52
  47.6 0.3 collective-permute-start.19
  48.0 0.6 collective-permute-start.18
  48.6 1.5 %collective-permute-start.17 = (f32[128,384]{1,0:T(8,128)S(1)}, f32[128,384]{1,0:T(8,128)S(1)}, u32[]{:S(2)}, u32[]{:S(2)}) collective-permute-start(f32[128,384]{1,0:T(8,128)S(1)} %get-tuple-element.40), channel_id=1, source_target_pairs={{0,16},{4,20},{8,24},{12,28},{16,0},{20,4},{24,8},{28,12},{1,17},{... | collective-permute-start | bytes 589832 | tf_op jit(solution)/shard_map/ppermute | solution.py:40
  50.1 1.6 %shard_map.50.refs_2_ = f32[192,384]{1,0:T(8,128)S(1)} custom-call(f32[384,256]{1,0:T(8,128)S(1)} %constant_dynamic-update-slice_fusion.refs_0_, f32[384,256]{1,0:T(8,128)S(1)} %collective-permute-done.9.refs_1_, f32[960,256]{1,0:T(8,128)S(1)} %get-tuple-element.24.near.refs_1_.refs_2_, f32[960,256]{1,0:T(8,128)S(1)} %collective-permute-done.11.refs_3_, ...), custom_call_target="tpu_custom_call" | custom-call | flops 339738624 | bytes 4718592 | tf_op jit(solution)/shard_map/pallas_call | solution.py:305
  51.7 1.5 %collective-permute-done.14.refs_1_ = f32[192,384]{1,0:T(8,128)S(1)} collective-permute-done((f32[192,384]{1,0:T(8,128)S(1)}, f32[192,384]{1,0:T(8,128)S(1)}, u32[]{:S(2)}, u32[]{:S(2)}) %collective-permute-start.14) | collective-permute-done | bytes 294944 | tf_op jit(solution)/shard_map/ppermute | solution.py:395
  53.3 0.1 shard_map.51.summed
  53.3 2.6 %collective-permute-done.18.refs_1_ = f32[128,384]{1,0:T(8,128)S(1)} collective-permute-done((f32[128,384]{1,0:T(8,128)S(1)}, f32[128,384]{1,0:T(8,128)S(1)}, u32[]{:S(2)}, u32[]{:S(2)}) %collective-permute-start.18) | collective-permute-done | bytes 196640 | tf_op jit(solution)/shard_map/ppermute | solution.py:40
  55.9 2.5 %collective-permute-done.17.refs_0_ = f32[128,384]{1,0:T(8,128)S(1)} collective-permute-done((f32[128,384]{1,0:T(8,128)S(1)}, f32[128,384]{1,0:T(8,128)S(1)}, u32[]{:S(2)}, u32[]{:S(2)}) %collective-permute-start.17) | collective-permute-done | bytes 196640 | tf_op jit(solution)/shard_map/ppermute | solution.py:40
  58.5 0.3 shard_map.53.summed
  58.8 4.5 %collective-permute-done.19.late = f32[192,384]{1,0:T(8,128)S(1)} collective-permute-done((f32[192,384]{1,0:T(8,128)S(1)}, f32[192,384]{1,0:T(8,128)S(1)}, u32[]{:S(2)}, u32[]{:S(2)}) %collective-permute-start.19) | collective-permute-done | bytes 294944 | tf_op jit(solution)/shard_map/ppermute | solution.py:401
  63.3 0.8 %shard_map.54 = f32[192,384]{1,0:T(8,128)} custom-call(f32[192,384]{1,0:T(8,128)S(1)} %shard_map.53.summed, f32[192,384]{1,0:T(8,128)S(1)} %collective-permute-done.19.late, f32[192,384]{1,0:T(8,128)S(1)} %collective-permute-done.15.passed), custom_call_target="tpu_custom_call" | custom-call | flops 147456 | bytes 1179648 | tf_op jit(solution)/shard_map/pallas_call | solution.py:305
  (14 shorter events, 0.1 us)
Async XLA Ops:
  0.0 7.1 %collective-permute-start.4 = (f32[64,192]{1,0:T(8,128)}, f32[64,192]{1,0:T(8,128)S(1)}, u32[]{:S(2)}, u32[]{:S(2)}) collective-permute-start(f32[64,192]{1,0:T(8,128)} %bitcast.1), channel_id=1, source_target_pairs={{0,1},{1,0},{2,3},{3,2},{4,5},{5,4},{6,7},{7,6},{8,9},{9,8},{10,11... | collective-permute-start | bytes 147464 | tf_op jit(solution)/shard_map/ppermute | solution.py:40
  3.0 12.5 %collective-permute-start.2 = (f32[192,256]{1,0:T(8,128)}, f32[192,256]{1,0:T(8,128)S(1)}, u32[]{:S(2)}, u32[]{:S(2)}) collective-permute-start(f32[192,256]{1,0:T(8,128)} %param.5), channel_id=1, source_target_pairs={{0,16},{4,20},{8,24},{12,28},{16,0},{20,4},{24,8},{28,12},{1,17},{... | collective-permute-start | bytes 589832 | tf_op jit(solution)/shard_map/ppermute | solution.py:40
  4.5 11.0 %collective-permute-start = (f32[192,256]{1,0:T(8,128)}, f32[192,256]{1,0:T(8,128)S(1)}, u32[]{:S(2)}, u32[]{:S(2)}) collective-permute-start(f32[192,256]{1,0:T(8,128)} %param.5), channel_id=1, source_target_pairs={{0,8},{4,12},{8,0},{12,4},{16,24},{20,28},{24,16},{28,20},{1,9},{5... | collective-permute-start | bytes 589832 | tf_op jit(solution)/shard_map/ppermute | solution.py:40
  6.0 9.5 %collective-permute-start.3 = (f32[192,256]{1,0:T(8,128)}, f32[192,256]{1,0:T(8,128)S(1)}, u32[]{:S(2)}, u32[]{:S(2)}) collective-permute-start(f32[192,256]{1,0:T(8,128)} %param.6), channel_id=1, source_target_pairs={{0,16},{4,20},{8,24},{12,28},{16,0},{20,4},{24,8},{28,12},{1,17},{... | collective-permute-start | bytes 589832 | tf_op jit(solution)/shard_map/ppermute | solution.py:40
  6.5 9.0 %collective-permute-start.1 = (f32[192,256]{1,0:T(8,128)}, f32[192,256]{1,0:T(8,128)S(1)}, u32[]{:S(2)}, u32[]{:S(2)}) collective-permute-start(f32[192,256]{1,0:T(8,128)} %param.6), channel_id=1, source_target_pairs={{0,8},{4,12},{8,0},{12,4},{16,24},{20,28},{24,16},{28,20},{1,9},{5... | collective-permute-start | bytes 589832 | tf_op jit(solution)/shard_map/ppermute | solution.py:40
  7.9 10.9 %copy-start.1 = (f32[192,256]{1,0:T(8,128)S(1)}, f32[192,256]{1,0:T(8,128)}, u32[]{:S(2)}) copy-start(f32[192,256]{1,0:T(8,128)} %param.5) | copy-start | bytes 589828
  7.9 7.6 %collective-permute-start.5 = (f32[128,192]{1,0:T(8,128)S(1)}, f32[128,192]{1,0:T(8,128)S(1)}, u32[]{:S(2)}, u32[]{:S(2)}) collective-permute-start(f32[128,192]{1,0:T(8,128)S(1)} %pad_maximum_fusion.1.refs_0_), channel_id=1, source_target_pairs={{0,2},{1,3},{2,0},{3,1},{4,6},{5,7},{6,4},{7,5},{8,10},{9,11},{10,... | collective-permute-start | bytes 294920 | tf_op jit(solution)/shard_map/ppermute | solution.py:40
  15.7 15.3 %collective-permute-start.6 = (f32[384,256]{1,0:T(8,128)S(1)}, f32[384,256]{1,0:T(8,128)S(1)}, u32[]{:S(2)}, u32[]{:S(2)}) collective-permute-start(f32[384,256]{1,0:T(8,128)S(1)} %get-tuple-element.22), channel_id=1, source_target_pairs={{0,8},{4,12},{8,0},{12,4},{16,24},{20,28},{24,16},{28,20},{1,9},{5... | collective-permute-start | bytes 1179656 | tf_op jit(solution)/shard_map/ppermute | solution.py:40
  17.3 1.5 %copy-start.2 = (f32[192,256]{1,0:T(8,128)S(1)}, f32[192,256]{1,0:T(8,128)}, u32[]{:S(2)}) copy-start(f32[192,256]{1,0:T(8,128)} %param.6) | copy-start | bytes 589828
  17.3 13.9 %collective-permute-start.7 = (f32[384,256]{1,0:T(8,128)S(1)}, f32[384,256]{1,0:T(8,128)S(1)}, u32[]{:S(2)}, u32[]{:S(2)}) collective-permute-start(f32[384,256]{1,0:T(8,128)S(1)} %get-tuple-element.23), channel_id=1, source_target_pairs={{0,16},{4,20},{8,24},{12,28},{16,0},{20,4},{24,8},{28,12},{1,17},{... | collective-permute-start | bytes 1179656 | tf_op jit(solution)/shard_map/ppermute | solution.py:40
  18.8 1.0 %copy-start = (f32[192,384]{1,0:T(8,128)S(1)}, f32[192,384]{1,0:T(8,128)}, u32[]{:S(2)}) copy-start(f32[192,384]{1,0:T(8,128)} %refs_7_.1) | copy-start | bytes 884740
  18.9 12.4 %collective-permute-start.9 = (f32[384,256]{1,0:T(8,128)S(1)}, f32[384,256]{1,0:T(8,128)S(1)}, u32[]{:S(2)}, u32[]{:S(2)}) collective-permute-start(f32[384,256]{1,0:T(8,128)S(1)} %constant_dynamic-update-slice_fusion.refs_0_), channel_id=1, source_target_pairs={{0,4},{4,0},{8,12},{12,8},{16,20},{20,16},{24,28},{28,24},{1,5},{5... | collective-permute-start | bytes 1179656 | tf_op jit(solution)/shard_map/ppermute | solution.py:40
  20.2 11.1 %collective-permute-start.10 = (f32[256,384]{1,0:T(8,128)S(1)}, f32[256,384]{1,0:T(8,128)S(1)}, u32[]{:S(2)}, u32[]{:S(2)}) collective-permute-start(f32[256,384]{1,0:T(8,128)S(1)} %shard_map.47), channel_id=1, source_target_pairs={{0,4},{4,0},{8,12},{12,8},{16,20},{20,16},{24,28},{28,24},{1,5},{5... | collective-permute-start | bytes 1179656 | tf_op jit(solution)/shard_map/ppermute | solution.py:40
  20.3 10.7 %collective-permute-start.8 = (f32[192,256]{1,0:T(8,128)S(1)}, f32[192,256]{1,0:T(8,128)S(1)}, u32[]{:S(2)}, u32[]{:S(2)}) collective-permute-start(f32[192,256]{1,0:T(8,128)S(1)} %slice.9), channel_id=1, source_target_pairs={{0,24},{4,28},{8,16},{12,20},{16,8},{20,12},{24,0},{28,4},{1,25},{... | collective-permute-start | bytes 589832 | tf_op jit(solution)/shard_map/ppermute | solution.py:40
  31.0 3.2 %collective-permute-start.11 = (f32[960,256]{1,0:T(8,128)S(1)}, f32[960,256]{1,0:T(8,128)S(1)}, u32[]{:S(2)}, u32[]{:S(2)}) collective-permute-start(f32[960,256]{1,0:T(8,128)S(1)} %get-tuple-element.24.near.refs_1_.refs_2_), channel_id=1, source_target_pairs={{0,4},{4,0},{8,12},{12,8},{16,20},{20,16},{24,28},{28,24},{1,5},{5... | collective-permute-start | bytes 2949128 | tf_op jit(solution)/shard_map/ppermute | solution.py:40
  31.3 3.7 %collective-permute-start.12 = (f32[960,256]{1,0:T(8,128)S(1)}, f32[960,256]{1,0:T(8,128)S(1)}, u32[]{:S(2)}, u32[]{:S(2)}) collective-permute-start(f32[960,256]{1,0:T(8,128)S(1)} %pad_maximum_fusion.refs_2_.refs_4_), channel_id=1, source_target_pairs={{0,4},{4,0},{8,12},{12,8},{16,20},{20,16},{24,28},{28,24},{1,5},{5... | collective-permute-start | bytes 2949128 | tf_op jit(solution)/shard_map/ppermute | solution.py:40
  31.7 14.1 %collective-permute-start.16 = (f32[256,384]{1,0:T(8,128)S(1)}, f32[256,384]{1,0:T(8,128)S(1)}, u32[]{:S(2)}, u32[]{:S(2)}) collective-permute-start(f32[256,384]{1,0:T(8,128)S(1)} %add.3.sides), channel_id=1, source_target_pairs={{0,8},{4,12},{8,0},{12,4},{16,24},{20,28},{24,16},{28,20},{1,9},{5... | collective-permute-start | bytes 1179656 | tf_op jit(solution)/shard_map/ppermute | solution.py:40
  38.5 9.1 %collective-permute-start.15 = (f32[192,384]{1,0:T(8,128)S(1)}, f32[192,384]{1,0:T(8,128)S(1)}, u32[]{:S(2)}, u32[]{:S(2)}) collective-permute-start(f32[192,384]{1,0:T(8,128)S(1)} %get-tuple-element.32), channel_id=1, source_target_pairs={{0,1},{1,0},{2,3},{3,2},{4,5},{5,4},{6,7},{7,6},{8,9},{9,8},{10,11... | collective-permute-start | bytes 884744 | tf_op jit(solution)/shard_map/ppermute | solution.py:40
  38.5 13.2 %collective-permute-start.13 = (f32[192,384]{1,0:T(8,128)S(1)}, f32[192,384]{1,0:T(8,128)S(1)}, u32[]{:S(2)}, u32[]{:S(2)}) collective-permute-start(f32[192,384]{1,0:T(8,128)S(1)} %get-tuple-element.29.other), channel_id=1, source_target_pairs={{1,2},{2,1},{5,6},{6,5},{9,10},{10,9},{13,14},{14,13},{17,18},{18,... | collective-permute-start | bytes 884744 | tf_op jit(solution)/shard_map/ppermute | solution.py:393
  39.2 14.0 %collective-permute-start.14 = (f32[192,384]{1,0:T(8,128)S(1)}, f32[192,384]{1,0:T(8,128)S(1)}, u32[]{:S(2)}, u32[]{:S(2)}) collective-permute-start(f32[192,384]{1,0:T(8,128)S(1)} %get-tuple-element.30.across), channel_id=1, source_target_pairs={{0,2},{3,1},{4,6},{7,5},{8,10},{11,9},{12,14},{15,13},{16,18},{19,... | collective-permute-start | bytes 884744 | tf_op jit(solution)/shard_map/ppermute | solution.py:395
  47.6 15.6 %collective-permute-start.19 = (f32[192,384]{1,0:T(8,128)S(1)}, f32[192,384]{1,0:T(8,128)S(1)}, u32[]{:S(2)}, u32[]{:S(2)}) collective-permute-start(f32[192,384]{1,0:T(8,128)S(1)} %get-tuple-element.38), channel_id=1, source_target_pairs={{0,1},{3,2},{1,3},{2,0},{4,5},{7,6},{5,7},{6,4},{8,9},{11,10},{9,1... | collective-permute-start | bytes 884744 | tf_op jit(solution)/shard_map/ppermute | solution.py:401
  48.0 7.9 %collective-permute-start.18 = (f32[128,384]{1,0:T(8,128)S(1)}, f32[128,384]{1,0:T(8,128)S(1)}, u32[]{:S(2)}, u32[]{:S(2)}) collective-permute-start(f32[128,384]{1,0:T(8,128)S(1)} %get-tuple-element.39), channel_id=1, source_target_pairs={{0,16},{4,20},{8,24},{12,28},{16,0},{20,4},{24,8},{28,12},{1,17},{... | collective-permute-start | bytes 589832 | tf_op jit(solution)/shard_map/ppermute | solution.py:40
  48.6 9.8 %collective-permute-start.17 = (f32[128,384]{1,0:T(8,128)S(1)}, f32[128,384]{1,0:T(8,128)S(1)}, u32[]{:S(2)}, u32[]{:S(2)}) collective-permute-start(f32[128,384]{1,0:T(8,128)S(1)} %get-tuple-element.40), channel_id=1, source_target_pairs={{0,16},{4,20},{8,24},{12,28},{16,0},{20,4},{24,8},{28,12},{1,17},{... | collective-permute-start | bytes 589832 | tf_op jit(solution)/shard_map/ppermute | solution.py:40

commit v8 on v7

--- a/solution.py
+++ b/solution.py
@@ -202,13 +202,19 @@
     wide = per * height
     base, first = place_in_kernel(per)
     split_pieces(pieces, in_refs, high, low, height, share)
-    mixed = mixed_ref[...]
-    for index in range(high.shape[0] // height):
-        if index not in order:
-            rows = slice(index * height, (index + 1) * height)
-            panels = (high[rows, : 2 * share], low[rows, : 2 * share])
-            refl = (high[rows, 2 * share :], low[rows, 2 * share :])
-            mixed = mixed + pair_dot(refl, panels, DOWN)
+    others = [index for index in range(high.shape[0] // height) if index not in order]
+
+    def of_others(ref, columns):
+        return jnp.concatenate(
+            [ref[index * height : (index + 1) * height, columns] for index in others], axis=0
+        )
+
+    refl_at, panels_at = slice(2 * share, None), slice(0, 2 * share)
+    mixed = mixed_ref[...] + pair_dot(
+        (of_others(high, refl_at), of_others(low, refl_at)),
+        (of_others(high, panels_at), of_others(low, panels_at)),
+        DOWN,
+    )
     mixed_pair = halves(mixed)
     left_panel, right_panel = in_refs[0][:height, :], in_refs[0][height:, :]
     own_refl = (high[:height, 2 * share :], low[:height, 2 * share :])

time: 64.3 us -> 64.1 us (level)
  no operation moved by 1% of the time
where the time goes in v8:
time: 64.1 us; the launch traced here: 63.9 us
  waiting for transfers between devices  28.5 us (44%)
  starting transfers between devices  25.6 us (40%)
  Pallas kernels  7.72 us (12%)
  other arithmetic  0.96 us (1%)
  local copies, waits for them, and re-layouts  0.93 us (1%)
    ppermute x17, waiting for transfers between devices, swap(): return lax.ppermute(value, axis, [(i, i ^ offset) for i in range(size)])  22.5 us
    ppermute x17, starting transfers between devices, swap(): return lax.ppermute(value, axis, [(i, i ^ offset) for i in range(size)])  17.9 us
    pallas_call x9, Pallas kernels, run_kernel(): pl.pallas_call(body, out_shape=[jax.ShapeDtypeStruct(shape, jnp.float32)...  7.72 us
    ppermute x1, starting transfers between devices, local_square(): received += [lax.ppermute(blocks[1], 'col', [(0, 2), (3, 1)])]  6.61 us
    ppermute x1, waiting for transfers between devices, local_square(): late = lax.ppermute(late, 'col', [(0, 1), (3, 2), (1, 3), (2, 0)])  4.49 us
    ppermute x1, waiting for transfers between devices, local_square(): received += [lax.ppermute(blocks[1], 'col', [(0, 2), (3, 1)])]  1.51 us
  transfers between devices with their start and end apart: 20, of which 9 were waited for; matrix products, arithmetic and copies ran while one was open for 2% of the time, Pallas kernels for 11%

profile of v8, /device:TPU:0, one launch (start us, length us, event | category | flops | bytes accessed | tf_op | source)
XLA Modules:
  0.0 63.9 jit_solution(4431230089487273060)
XLA Ops:
  0.0 3.0 %collective-permute-start.4 = (f32[64,192]{1,0:T(8,128)}, f32[64,192]{1,0:T(8,128)S(1)}, u32[]{:S(2)}, u32[]{:S(2)}) collective-permute-start(f32[64,192]{1,0:T(8,128)} %bitcast.1), channel_id=1, source_target_pairs={{0,1},{1,0},{2,3},{3,2},{4,5},{5,4},{6,7},{7,6},{8,9},{9,8},{10,11... | collective-permute-start | bytes 147464 | tf_op jit(solution)/shard_map/ppermute | solution.py:40
  3.0 1.5 %collective-permute-start.2 = (f32[192,256]{1,0:T(8,128)}, f32[192,256]{1,0:T(8,128)S(1)}, u32[]{:S(2)}, u32[]{:S(2)}) collective-permute-start(f32[192,256]{1,0:T(8,128)} %param.5), channel_id=1, source_target_pairs={{0,16},{4,20},{8,24},{12,28},{16,0},{20,4},{24,8},{28,12},{1,17},{... | collective-permute-start | bytes 589832 | tf_op jit(solution)/shard_map/ppermute | solution.py:40
  4.5 1.5 %collective-permute-start = (f32[192,256]{1,0:T(8,128)}, f32[192,256]{1,0:T(8,128)S(1)}, u32[]{:S(2)}, u32[]{:S(2)}) collective-permute-start(f32[192,256]{1,0:T(8,128)} %param.5), channel_id=1, source_target_pairs={{0,8},{4,12},{8,0},{12,4},{16,24},{20,28},{24,16},{28,20},{1,9},{5... | collective-permute-start | bytes 589832 | tf_op jit(solution)/shard_map/ppermute | solution.py:40
  6.0 0.5 collective-permute-start.3
  6.5 0.5 collective-permute-start.1
  7.1 0.0 collective-permute-done.4
  7.1 0.8 %pad_maximum_fusion.1.refs_0_ = f32[128,192]{1,0:T(8,128)S(1)} fusion(f32[64,192]{1,0:T(8,128)S(1)} %collective-permute-done.4, f32[64,192]{1,0:T(8,128)} %bitcast.2), kind=kLoop, calls=%fused_computation.1 | loop fusion | flops 24576 | bytes 196608 | tf_op jit(solution)/shard_map/concatenate | solution.py:367
  7.9 0.0 copy-start.1
  7.9 2.7 %collective-permute-start.5 = (f32[128,192]{1,0:T(8,128)S(1)}, f32[128,192]{1,0:T(8,128)S(1)}, u32[]{:S(2)}, u32[]{:S(2)}) collective-permute-start(f32[128,192]{1,0:T(8,128)S(1)} %pad_maximum_fusion.1.refs_0_), channel_id=1, source_target_pairs={{0,2},{1,3},{2,0},{3,1},{4,6},{5,7},{6,4},{7,5},{8,10},{9,11},{10,... | collective-permute-start | bytes 294920 | tf_op jit(solution)/shard_map/ppermute | solution.py:40
  10.6 5.0 %collective-permute-done.5.refs_1_ = f32[128,192]{1,0:T(8,128)S(1)} collective-permute-done((f32[128,192]{1,0:T(8,128)S(1)}, f32[128,192]{1,0:T(8,128)S(1)}, u32[]{:S(2)}, u32[]{:S(2)}) %collective-permute-start.5) | collective-permute-done | bytes 98336 | tf_op jit(solution)/shard_map/ppermute | solution.py:40
  15.6 0.0 collective-permute-done.2.left_y
  15.6 0.0 collective-permute-done.left_x
  15.6 0.0 collective-permute-done.3.right_y
  15.6 0.1 shard_map.46
  15.7 1.6 %collective-permute-start.6 = (f32[384,256]{1,0:T(8,128)S(1)}, f32[384,256]{1,0:T(8,128)S(1)}, u32[]{:S(2)}, u32[]{:S(2)}) collective-permute-start(f32[384,256]{1,0:T(8,128)S(1)} %get-tuple-element.22), channel_id=1, source_target_pairs={{0,8},{4,12},{8,0},{12,4},{16,24},{20,28},{24,16},{28,20},{1,9},{5... | collective-permute-start | bytes 1179656 | tf_op jit(solution)/shard_map/ppermute | solution.py:40
  17.3 1.5 %collective-permute-start.7 = (f32[384,256]{1,0:T(8,128)S(1)}, f32[384,256]{1,0:T(8,128)S(1)}, u32[]{:S(2)}, u32[]{:S(2)}) collective-permute-start(f32[384,256]{1,0:T(8,128)S(1)} %get-tuple-element.23), channel_id=1, source_target_pairs={{0,16},{4,20},{8,24},{12,28},{16,0},{20,4},{24,8},{28,12},{1,17},{... | collective-permute-start | bytes 1179656 | tf_op jit(solution)/shard_map/ppermute | solution.py:40
  18.8 0.0 copy-start
  18.9 0.1 collective-permute-start.9
  19.0 0.8 %copy-done = f32[192,384]{1,0:T(8,128)S(1)} copy-done((f32[192,384]{1,0:T(8,128)S(1)}, f32[192,384]{1,0:T(8,128)}, u32[]{:S(2)}) %copy-start) | copy-done | bytes 294936
  19.8 0.4 shard_map.47
  20.2 0.1 collective-permute-start.10
  20.3 0.9 %collective-permute-start.8 = (f32[192,256]{1,0:T(8,128)S(1)}, f32[192,256]{1,0:T(8,128)S(1)}, u32[]{:S(2)}, u32[]{:S(2)}) collective-permute-start(f32[192,256]{1,0:T(8,128)S(1)} %slice.9), channel_id=1, source_target_pairs={{0,24},{4,28},{8,16},{12,20},{16,8},{20,12},{24,0},{28,4},{1,25},{... | collective-permute-start | bytes 589832 | tf_op jit(solution)/shard_map/ppermute | solution.py:40
  21.2 9.8 %collective-permute-done.8 = f32[192,256]{1,0:T(8,128)S(1)} collective-permute-done((f32[192,256]{1,0:T(8,128)S(1)}, f32[192,256]{1,0:T(8,128)S(1)}, u32[]{:S(2)}, u32[]{:S(2)}) %collective-permute-start.8) | collective-permute-done | bytes 196640 | tf_op jit(solution)/shard_map/ppermute | solution.py:40
  31.0 0.0 collective-permute-start.11
  31.0 0.0 collective-permute-done.6
  31.0 0.1 collective-permute-done.7
  31.2 0.1 pad_maximum_fusion.refs_2_.refs_4_
  31.3 0.4 collective-permute-start.12
  31.7 1.5 %collective-permute-start.16 = (f32[256,384]{1,0:T(8,128)S(1)}, f32[256,384]{1,0:T(8,128)S(1)}, u32[]{:S(2)}, u32[]{:S(2)}) collective-permute-start(f32[256,384]{1,0:T(8,128)S(1)} %add.3.sides), channel_id=1, source_target_pairs={{0,8},{4,12},{8,0},{12,4},{16,24},{20,28},{24,16},{28,20},{1,9},{5... | collective-permute-start | bytes 1179656 | tf_op jit(solution)/shard_map/ppermute | solution.py:40
  33.2 1.0 %shard_map.48 = (f32[256,512]{1,0:T(8,128)S(1)}, f32[192,256]{1,0:T(8,128)S(1)}) custom-call(f32[384,256]{1,0:T(8,128)S(1)} %constant_dynamic-update-slice_fusion.refs_0_, f32[960,256]{1,0:T(8,128)S(1)} %get-tuple-element.24.near.refs_1_.refs_2_, f32[960,256]{1,0:T(8,128)S(1)} %pad_maximum_fusion.refs_2_.refs_4_, f32[192,384]{1,0:T(8,128)S(1)} %copy-done), custom_call_target="tpu_custom_call" | custom-call | flops 603979776 | bytes 2359296 | tf_op jit(solution)/shard_map/pallas_call | solution.py:311
  34.2 0.8 %collective-permute-done.12.refs_5_ = f32[960,256]{1,0:T(8,128)S(1)} collective-permute-done((f32[960,256]{1,0:T(8,128)S(1)}, f32[960,256]{1,0:T(8,128)S(1)}, u32[]{:S(2)}, u32[]{:S(2)}) %collective-permute-start.12) | collective-permute-done | bytes 983072 | tf_op jit(solution)/shard_map/ppermute | solution.py:40
  35.0 3.3 %shard_map.49 = (f32[192,768]{1,0:T(8,128)S(1)}, f32[192,384]{1,0:T(8,128)S(1)}, f32[192,384]{1,0:T(8,128)S(1)}, f32[192,384]{1,0:T(8,128)S(1)}) custom-call(f32[384,256]{1,0:T(8,128)S(1)} %constant_dynamic-update-slice_fusion.refs_0_, f32[384,256]{1,0:T(8,128)S(1)} %collective-permute-done.9.refs_1_, f32[960,256]{1,0:T(8,128)S(1)} %get-tuple-element.24.near.refs_1_.refs_2_, ...), custom_call_target="tpu_custom_call" | custom-call | flops 1962934272 | bytes 4718592 | tf_op jit(solution)/shard_map/pallas_call | solution.py:311
  38.3 0.1 collective-permute-start.15
  38.4 0.7 %collective-permute-start.13 = (f32[192,384]{1,0:T(8,128)S(1)}, f32[192,384]{1,0:T(8,128)S(1)}, u32[]{:S(2)}, u32[]{:S(2)}) collective-permute-start(f32[192,384]{1,0:T(8,128)S(1)} %get-tuple-element.29.other), channel_id=1, source_target_pairs={{1,2},{2,1},{5,6},{6,5},{9,10},{10,9},{13,14},{14,13},{17,18},{18,... | collective-permute-start | bytes 884744 | tf_op jit(solution)/shard_map/ppermute | solution.py:399
  39.1 6.6 %collective-permute-start.14 = (f32[192,384]{1,0:T(8,128)S(1)}, f32[192,384]{1,0:T(8,128)S(1)}, u32[]{:S(2)}, u32[]{:S(2)}) collective-permute-start(f32[192,384]{1,0:T(8,128)S(1)} %get-tuple-element.30.across), channel_id=1, source_target_pairs={{0,2},{3,1},{4,6},{7,5},{8,10},{11,9},{12,14},{15,13},{16,18},{19,... | collective-permute-start | bytes 884744 | tf_op jit(solution)/shard_map/ppermute | solution.py:401
  45.7 1.7 %collective-permute-done.15.passed = f32[192,384]{1,0:T(8,128)S(1)} collective-permute-done((f32[192,384]{1,0:T(8,128)S(1)}, f32[192,384]{1,0:T(8,128)S(1)}, u32[]{:S(2)}, u32[]{:S(2)}) %collective-permute-start.15) | collective-permute-done | bytes 294944 | tf_op jit(solution)/shard_map/ppermute | solution.py:40
  47.4 0.1 shard_map.52
  47.5 0.3 collective-permute-start.19
  47.8 0.6 collective-permute-start.18
  48.5 1.5 %collective-permute-start.17 = (f32[128,384]{1,0:T(8,128)S(1)}, f32[128,384]{1,0:T(8,128)S(1)}, u32[]{:S(2)}, u32[]{:S(2)}) collective-permute-start(f32[128,384]{1,0:T(8,128)S(1)} %get-tuple-element.40), channel_id=1, source_target_pairs={{0,16},{4,20},{8,24},{12,28},{16,0},{20,4},{24,8},{28,12},{1,17},{... | collective-permute-start | bytes 589832 | tf_op jit(solution)/shard_map/ppermute | solution.py:40
  49.9 1.6 %shard_map.50.refs_2_ = f32[192,384]{1,0:T(8,128)S(1)} custom-call(f32[384,256]{1,0:T(8,128)S(1)} %constant_dynamic-update-slice_fusion.refs_0_, f32[384,256]{1,0:T(8,128)S(1)} %collective-permute-done.9.refs_1_, f32[960,256]{1,0:T(8,128)S(1)} %get-tuple-element.24.near.refs_1_.refs_2_, f32[960,256]{1,0:T(8,128)S(1)} %collective-permute-done.11.refs_3_, ...), custom_call_target="tpu_custom_call" | custom-call | flops 339738624 | bytes 4718592 | tf_op jit(solution)/shard_map/pallas_call | solution.py:311
  51.6 1.5 %collective-permute-done.14.refs_1_ = f32[192,384]{1,0:T(8,128)S(1)} collective-permute-done((f32[192,384]{1,0:T(8,128)S(1)}, f32[192,384]{1,0:T(8,128)S(1)}, u32[]{:S(2)}, u32[]{:S(2)}) %collective-permute-start.14) | collective-permute-done | bytes 294944 | tf_op jit(solution)/shard_map/ppermute | solution.py:401
  53.1 0.1 shard_map.51.summed
  53.2 2.6 %collective-permute-done.18.refs_1_ = f32[128,384]{1,0:T(8,128)S(1)} collective-permute-done((f32[128,384]{1,0:T(8,128)S(1)}, f32[128,384]{1,0:T(8,128)S(1)}, u32[]{:S(2)}, u32[]{:S(2)}) %collective-permute-start.18) | collective-permute-done | bytes 196640 | tf_op jit(solution)/shard_map/ppermute | solution.py:40
  55.8 2.5 %collective-permute-done.17.refs_0_ = f32[128,384]{1,0:T(8,128)S(1)} collective-permute-done((f32[128,384]{1,0:T(8,128)S(1)}, f32[128,384]{1,0:T(8,128)S(1)}, u32[]{:S(2)}, u32[]{:S(2)}) %collective-permute-start.17) | collective-permute-done | bytes 196640 | tf_op jit(solution)/shard_map/ppermute | solution.py:40
  58.3 0.3 shard_map.53.summed
  58.6 4.5 %collective-permute-done.19.late = f32[192,384]{1,0:T(8,128)S(1)} collective-permute-done((f32[192,384]{1,0:T(8,128)S(1)}, f32[192,384]{1,0:T(8,128)S(1)}, u32[]{:S(2)}, u32[]{:S(2)}) %collective-permute-start.19) | collective-permute-done | bytes 294944 | tf_op jit(solution)/shard_map/ppermute | solution.py:407
  63.1 0.8 %shard_map.54 = f32[192,384]{1,0:T(8,128)} custom-call(f32[192,384]{1,0:T(8,128)S(1)} %shard_map.53.summed, f32[192,384]{1,0:T(8,128)S(1)} %collective-permute-done.19.late, f32[192,384]{1,0:T(8,128)S(1)} %collective-permute-done.15.passed), custom_call_target="tpu_custom_call" | custom-call | flops 147456 | bytes 1179648 | tf_op jit(solution)/shard_map/pallas_call | solution.py:311
  (14 shorter events, 0.1 us)
Async XLA Ops:
  0.0 7.1 %collective-permute-start.4 = (f32[64,192]{1,0:T(8,128)}, f32[64,192]{1,0:T(8,128)S(1)}, u32[]{:S(2)}, u32[]{:S(2)}) collective-permute-start(f32[64,192]{1,0:T(8,128)} %bitcast.1), channel_id=1, source_target_pairs={{0,1},{1,0},{2,3},{3,2},{4,5},{5,4},{6,7},{7,6},{8,9},{9,8},{10,11... | collective-permute-start | bytes 147464 | tf_op jit(solution)/shard_map/ppermute | solution.py:40
  3.0 12.5 %collective-permute-start.2 = (f32[192,256]{1,0:T(8,128)}, f32[192,256]{1,0:T(8,128)S(1)}, u32[]{:S(2)}, u32[]{:S(2)}) collective-permute-start(f32[192,256]{1,0:T(8,128)} %param.5), channel_id=1, source_target_pairs={{0,16},{4,20},{8,24},{12,28},{16,0},{20,4},{24,8},{28,12},{1,17},{... | collective-permute-start | bytes 589832 | tf_op jit(solution)/shard_map/ppermute | solution.py:40
  4.5 11.0 %collective-permute-start = (f32[192,256]{1,0:T(8,128)}, f32[192,256]{1,0:T(8,128)S(1)}, u32[]{:S(2)}, u32[]{:S(2)}) collective-permute-start(f32[192,256]{1,0:T(8,128)} %param.5), channel_id=1, source_target_pairs={{0,8},{4,12},{8,0},{12,4},{16,24},{20,28},{24,16},{28,20},{1,9},{5... | collective-permute-start | bytes 589832 | tf_op jit(solution)/shard_map/ppermute | solution.py:40
  6.0 9.5 %collective-permute-start.3 = (f32[192,256]{1,0:T(8,128)}, f32[192,256]{1,0:T(8,128)S(1)}, u32[]{:S(2)}, u32[]{:S(2)}) collective-permute-start(f32[192,256]{1,0:T(8,128)} %param.6), channel_id=1, source_target_pairs={{0,16},{4,20},{8,24},{12,28},{16,0},{20,4},{24,8},{28,12},{1,17},{... | collective-permute-start | bytes 589832 | tf_op jit(solution)/shard_map/ppermute | solution.py:40
  6.5 9.0 %collective-permute-start.1 = (f32[192,256]{1,0:T(8,128)}, f32[192,256]{1,0:T(8,128)S(1)}, u32[]{:S(2)}, u32[]{:S(2)}) collective-permute-start(f32[192,256]{1,0:T(8,128)} %param.6), channel_id=1, source_target_pairs={{0,8},{4,12},{8,0},{12,4},{16,24},{20,28},{24,16},{28,20},{1,9},{5... | collective-permute-start | bytes 589832 | tf_op jit(solution)/shard_map/ppermute | solution.py:40
  7.9 10.9 %copy-start.1 = (f32[192,256]{1,0:T(8,128)S(1)}, f32[192,256]{1,0:T(8,128)}, u32[]{:S(2)}) copy-start(f32[192,256]{1,0:T(8,128)} %param.5) | copy-start | bytes 589828
  7.9 7.6 %collective-permute-start.5 = (f32[128,192]{1,0:T(8,128)S(1)}, f32[128,192]{1,0:T(8,128)S(1)}, u32[]{:S(2)}, u32[]{:S(2)}) collective-permute-start(f32[128,192]{1,0:T(8,128)S(1)} %pad_maximum_fusion.1.refs_0_), channel_id=1, source_target_pairs={{0,2},{1,3},{2,0},{3,1},{4,6},{5,7},{6,4},{7,5},{8,10},{9,11},{10,... | collective-permute-start | bytes 294920 | tf_op jit(solution)/shard_map/ppermute | solution.py:40
  15.7 15.3 %collective-permute-start.6 = (f32[384,256]{1,0:T(8,128)S(1)}, f32[384,256]{1,0:T(8,128)S(1)}, u32[]{:S(2)}, u32[]{:S(2)}) collective-permute-start(f32[384,256]{1,0:T(8,128)S(1)} %get-tuple-element.22), channel_id=1, source_target_pairs={{0,8},{4,12},{8,0},{12,4},{16,24},{20,28},{24,16},{28,20},{1,9},{5... | collective-permute-start | bytes 1179656 | tf_op jit(solution)/shard_map/ppermute | solution.py:40
  17.3 1.5 %copy-start.2 = (f32[192,256]{1,0:T(8,128)S(1)}, f32[192,256]{1,0:T(8,128)}, u32[]{:S(2)}) copy-start(f32[192,256]{1,0:T(8,128)} %param.6) | copy-start | bytes 589828
  17.3 13.9 %collective-permute-start.7 = (f32[384,256]{1,0:T(8,128)S(1)}, f32[384,256]{1,0:T(8,128)S(1)}, u32[]{:S(2)}, u32[]{:S(2)}) collective-permute-start(f32[384,256]{1,0:T(8,128)S(1)} %get-tuple-element.23), channel_id=1, source_target_pairs={{0,16},{4,20},{8,24},{12,28},{16,0},{20,4},{24,8},{28,12},{1,17},{... | collective-permute-start | bytes 1179656 | tf_op jit(solution)/shard_map/ppermute | solution.py:40
  18.8 1.0 %copy-start = (f32[192,384]{1,0:T(8,128)S(1)}, f32[192,384]{1,0:T(8,128)}, u32[]{:S(2)}) copy-start(f32[192,384]{1,0:T(8,128)} %refs_7_.1) | copy-start | bytes 884740
  18.9 12.4 %collective-permute-start.9 = (f32[384,256]{1,0:T(8,128)S(1)}, f32[384,256]{1,0:T(8,128)S(1)}, u32[]{:S(2)}, u32[]{:S(2)}) collective-permute-start(f32[384,256]{1,0:T(8,128)S(1)} %constant_dynamic-update-slice_fusion.refs_0_), channel_id=1, source_target_pairs={{0,4},{4,0},{8,12},{12,8},{16,20},{20,16},{24,28},{28,24},{1,5},{5... | collective-permute-start | bytes 1179656 | tf_op jit(solution)/shard_map/ppermute | solution.py:40
  20.2 11.1 %collective-permute-start.10 = (f32[256,384]{1,0:T(8,128)S(1)}, f32[256,384]{1,0:T(8,128)S(1)}, u32[]{:S(2)}, u32[]{:S(2)}) collective-permute-start(f32[256,384]{1,0:T(8,128)S(1)} %shard_map.47), channel_id=1, source_target_pairs={{0,4},{4,0},{8,12},{12,8},{16,20},{20,16},{24,28},{28,24},{1,5},{5... | collective-permute-start | bytes 1179656 | tf_op jit(solution)/shard_map/ppermute | solution.py:40
  20.3 10.7 %collective-permute-start.8 = (f32[192,256]{1,0:T(8,128)S(1)}, f32[192,256]{1,0:T(8,128)S(1)}, u32[]{:S(2)}, u32[]{:S(2)}) collective-permute-start(f32[192,256]{1,0:T(8,128)S(1)} %slice.9), channel_id=1, source_target_pairs={{0,24},{4,28},{8,16},{12,20},{16,8},{20,12},{24,0},{28,4},{1,25},{... | collective-permute-start | bytes 589832 | tf_op jit(solution)/shard_map/ppermute | solution.py:40
  31.0 3.2 %collective-permute-start.11 = (f32[960,256]{1,0:T(8,128)S(1)}, f32[960,256]{1,0:T(8,128)S(1)}, u32[]{:S(2)}, u32[]{:S(2)}) collective-permute-start(f32[960,256]{1,0:T(8,128)S(1)} %get-tuple-element.24.near.refs_1_.refs_2_), channel_id=1, source_target_pairs={{0,4},{4,0},{8,12},{12,8},{16,20},{20,16},{24,28},{28,24},{1,5},{5... | collective-permute-start | bytes 2949128 | tf_op jit(solution)/shard_map/ppermute | solution.py:40
  31.3 3.7 %collective-permute-start.12 = (f32[960,256]{1,0:T(8,128)S(1)}, f32[960,256]{1,0:T(8,128)S(1)}, u32[]{:S(2)}, u32[]{:S(2)}) collective-permute-start(f32[960,256]{1,0:T(8,128)S(1)} %pad_maximum_fusion.refs_2_.refs_4_), channel_id=1, source_target_pairs={{0,4},{4,0},{8,12},{12,8},{16,20},{20,16},{24,28},{28,24},{1,5},{5... | collective-permute-start | bytes 2949128 | tf_op jit(solution)/shard_map/ppermute | solution.py:40
  31.7 13.9 %collective-permute-start.16 = (f32[256,384]{1,0:T(8,128)S(1)}, f32[256,384]{1,0:T(8,128)S(1)}, u32[]{:S(2)}, u32[]{:S(2)}) collective-permute-start(f32[256,384]{1,0:T(8,128)S(1)} %add.3.sides), channel_id=1, source_target_pairs={{0,8},{4,12},{8,0},{12,4},{16,24},{20,28},{24,16},{28,20},{1,9},{5... | collective-permute-start | bytes 1179656 | tf_op jit(solution)/shard_map/ppermute | solution.py:40
  38.3 9.1 %collective-permute-start.15 = (f32[192,384]{1,0:T(8,128)S(1)}, f32[192,384]{1,0:T(8,128)S(1)}, u32[]{:S(2)}, u32[]{:S(2)}) collective-permute-start(f32[192,384]{1,0:T(8,128)S(1)} %get-tuple-element.32), channel_id=1, source_target_pairs={{0,1},{1,0},{2,3},{3,2},{4,5},{5,4},{6,7},{7,6},{8,9},{9,8},{10,11... | collective-permute-start | bytes 884744 | tf_op jit(solution)/shard_map/ppermute | solution.py:40
  38.4 13.2 %collective-permute-start.13 = (f32[192,384]{1,0:T(8,128)S(1)}, f32[192,384]{1,0:T(8,128)S(1)}, u32[]{:S(2)}, u32[]{:S(2)}) collective-permute-start(f32[192,384]{1,0:T(8,128)S(1)} %get-tuple-element.29.other), channel_id=1, source_target_pairs={{1,2},{2,1},{5,6},{6,5},{9,10},{10,9},{13,14},{14,13},{17,18},{18,... | collective-permute-start | bytes 884744 | tf_op jit(solution)/shard_map/ppermute | solution.py:399
  39.1 14.0 %collective-permute-start.14 = (f32[192,384]{1,0:T(8,128)S(1)}, f32[192,384]{1,0:T(8,128)S(1)}, u32[]{:S(2)}, u32[]{:S(2)}) collective-permute-start(f32[192,384]{1,0:T(8,128)S(1)} %get-tuple-element.30.across), channel_id=1, source_target_pairs={{0,2},{3,1},{4,6},{7,5},{8,10},{11,9},{12,14},{15,13},{16,18},{19,... | collective-permute-start | bytes 884744 | tf_op jit(solution)/shard_map/ppermute | solution.py:401
  47.5 15.6 %collective-permute-start.19 = (f32[192,384]{1,0:T(8,128)S(1)}, f32[192,384]{1,0:T(8,128)S(1)}, u32[]{:S(2)}, u32[]{:S(2)}) collective-permute-start(f32[192,384]{1,0:T(8,128)S(1)} %get-tuple-element.38), channel_id=1, source_target_pairs={{0,1},{3,2},{1,3},{2,0},{4,5},{7,6},{5,7},{6,4},{8,9},{11,10},{9,1... | collective-permute-start | bytes 884744 | tf_op jit(solution)/shard_map/ppermute | solution.py:407
  47.8 7.9 %collective-permute-start.18 = (f32[128,384]{1,0:T(8,128)S(1)}, f32[128,384]{1,0:T(8,128)S(1)}, u32[]{:S(2)}, u32[]{:S(2)}) collective-permute-start(f32[128,384]{1,0:T(8,128)S(1)} %get-tuple-element.39), channel_id=1, source_target_pairs={{0,16},{4,20},{8,24},{12,28},{16,0},{20,4},{24,8},{28,12},{1,17},{... | collective-permute-start | bytes 589832 | tf_op jit(solution)/shard_map/ppermute | solution.py:40
  48.5 9.8 %collective-permute-start.17 = (f32[128,384]{1,0:T(8,128)S(1)}, f32[128,384]{1,0:T(8,128)S(1)}, u32[]{:S(2)}, u32[]{:S(2)}) collective-permute-start(f32[128,384]{1,0:T(8,128)S(1)} %get-tuple-element.40), channel_id=1, source_target_pairs={{0,16},{4,20},{8,24},{12,28},{16,0},{20,4},{24,8},{28,12},{1,17},{... | collective-permute-start | bytes 589832 | tf_op jit(solution)/shard_map/ppermute | solution.py:40

commit v9 on v8

--- a/solution.py
+++ b/solution.py
@@ -396,8 +396,8 @@
         12 * (total - len(order) * height) * share * width + 6 * total * height * depth,
         4 * total * depth,
     )
+    passed = swap(blocks[0], "col", 1)
     received = [lax.ppermute(blocks[2], "col", [(1, 2), (2, 1)])]
-    passed = swap(blocks[0], "col", 1)
     received += [lax.ppermute(blocks[1], "col", [(0, 2), (3, 1)])]
     late, sides = run_kernel(
         late_kernel,

time: 64.1 us -> 64.1 us (level)
  no operation moved by 1% of the time
where the time goes in v9:
time: 64.1 us; the launch traced here: 63.9 us
  waiting for transfers between devices  28.5 us (44%)
  starting transfers between devices  25.6 us (40%)
  Pallas kernels  7.72 us (12%)
  other arithmetic  0.96 us (1%)
  local copies, waits for them, and re-layouts  0.93 us (1%)
    ppermute x17, waiting for transfers between devices, swap(): return lax.ppermute(value, axis, [(i, i ^ offset) for i in range(size)])  22.5 us
    ppermute x17, starting transfers between devices, swap(): return lax.ppermute(value, axis, [(i, i ^ offset) for i in range(size)])  17.9 us
    pallas_call x9, Pallas kernels, run_kernel(): pl.pallas_call(body, out_shape=[jax.ShapeDtypeStruct(shape, jnp.float32)...  7.72 us
    ppermute x1, starting transfers between devices, local_square(): received += [lax.ppermute(blocks[1], 'col', [(0, 2), (3, 1)])]  6.61 us
    ppermute x1, waiting for transfers between devices, local_square(): late = lax.ppermute(late, 'col', [(0, 1), (3, 2), (1, 3), (2, 0)])  4.49 us
    ppermute x1, waiting for transfers between devices, local_square(): received += [lax.ppermute(blocks[1], 'col', [(0, 2), (3, 1)])]  1.51 us
  transfers between devices with their start and end apart: 20, of which 9 were waited for; matrix products, arithmetic and copies ran while one was open for 2% of the time, Pallas kernels for 11%

profile of v9, /device:TPU:0, one launch (start us, length us, event | category | flops | bytes accessed | tf_op | source)
XLA Modules:
  0.0 63.9 jit_solution(4431230089487273060)
XLA Ops:
  0.0 3.0 %collective-permute-start.4 = (f32[64,192]{1,0:T(8,128)}, f32[64,192]{1,0:T(8,128)S(1)}, u32[]{:S(2)}, u32[]{:S(2)}) collective-permute-start(f32[64,192]{1,0:T(8,128)} %bitcast.1), channel_id=1, source_target_pairs={{0,1},{1,0},{2,3},{3,2},{4,5},{5,4},{6,7},{7,6},{8,9},{9,8},{10,11... | collective-permute-start | bytes 147464 | tf_op jit(solution)/shard_map/ppermute | solution.py:40
  3.0 1.5 %collective-permute-start.2 = (f32[192,256]{1,0:T(8,128)}, f32[192,256]{1,0:T(8,128)S(1)}, u32[]{:S(2)}, u32[]{:S(2)}) collective-permute-start(f32[192,256]{1,0:T(8,128)} %param.5), channel_id=1, source_target_pairs={{0,16},{4,20},{8,24},{12,28},{16,0},{20,4},{24,8},{28,12},{1,17},{... | collective-permute-start | bytes 589832 | tf_op jit(solution)/shard_map/ppermute | solution.py:40
  4.5 1.5 %collective-permute-start = (f32[192,256]{1,0:T(8,128)}, f32[192,256]{1,0:T(8,128)S(1)}, u32[]{:S(2)}, u32[]{:S(2)}) collective-permute-start(f32[192,256]{1,0:T(8,128)} %param.5), channel_id=1, source_target_pairs={{0,8},{4,12},{8,0},{12,4},{16,24},{20,28},{24,16},{28,20},{1,9},{5... | collective-permute-start | bytes 589832 | tf_op jit(solution)/shard_map/ppermute | solution.py:40
  6.0 0.5 collective-permute-start.3
  6.5 0.5 collective-permute-start.1
  7.1 0.0 collective-permute-done.4
  7.1 0.8 %pad_maximum_fusion.1.refs_0_ = f32[128,192]{1,0:T(8,128)S(1)} fusion(f32[64,192]{1,0:T(8,128)S(1)} %collective-permute-done.4, f32[64,192]{1,0:T(8,128)} %bitcast.2), kind=kLoop, calls=%fused_computation.1 | loop fusion | flops 24576 | bytes 196608 | tf_op jit(solution)/shard_map/concatenate | solution.py:367
  7.9 0.0 copy-start.1
  7.9 2.7 %collective-permute-start.5 = (f32[128,192]{1,0:T(8,128)S(1)}, f32[128,192]{1,0:T(8,128)S(1)}, u32[]{:S(2)}, u32[]{:S(2)}) collective-permute-start(f32[128,192]{1,0:T(8,128)S(1)} %pad_maximum_fusion.1.refs_0_), channel_id=1, source_target_pairs={{0,2},{1,3},{2,0},{3,1},{4,6},{5,7},{6,4},{7,5},{8,10},{9,11},{10,... | collective-permute-start | bytes 294920 | tf_op jit(solution)/shard_map/ppermute | solution.py:40
  10.6 5.0 %collective-permute-done.5.refs_1_ = f32[128,192]{1,0:T(8,128)S(1)} collective-permute-done((f32[128,192]{1,0:T(8,128)S(1)}, f32[128,192]{1,0:T(8,128)S(1)}, u32[]{:S(2)}, u32[]{:S(2)}) %collective-permute-start.5) | collective-permute-done | bytes 98336 | tf_op jit(solution)/shard_map/ppermute | solution.py:40
  15.6 0.0 collective-permute-done.2.left_y
  15.6 0.0 collective-permute-done.left_x
  15.6 0.0 collective-permute-done.3.right_y
  15.6 0.1 shard_map.46
  15.7 1.6 %collective-permute-start.6 = (f32[384,256]{1,0:T(8,128)S(1)}, f32[384,256]{1,0:T(8,128)S(1)}, u32[]{:S(2)}, u32[]{:S(2)}) collective-permute-start(f32[384,256]{1,0:T(8,128)S(1)} %get-tuple-element.22), channel_id=1, source_target_pairs={{0,8},{4,12},{8,0},{12,4},{16,24},{20,28},{24,16},{28,20},{1,9},{5... | collective-permute-start | bytes 1179656 | tf_op jit(solution)/shard_map/ppermute | solution.py:40
  17.3 1.5 %collective-permute-start.7 = (f32[384,256]{1,0:T(8,128)S(1)}, f32[384,256]{1,0:T(8,128)S(1)}, u32[]{:S(2)}, u32[]{:S(2)}) collective-permute-start(f32[384,256]{1,0:T(8,128)S(1)} %get-tuple-element.23), channel_id=1, source_target_pairs={{0,16},{4,20},{8,24},{12,28},{16,0},{20,4},{24,8},{28,12},{1,17},{... | collective-permute-start | bytes 1179656 | tf_op jit(solution)/shard_map/ppermute | solution.py:40
  18.8 0.0 copy-start
  18.9 0.1 collective-permute-start.9
  19.0 0.8 %copy-done = f32[192,384]{1,0:T(8,128)S(1)} copy-done((f32[192,384]{1,0:T(8,128)S(1)}, f32[192,384]{1,0:T(8,128)}, u32[]{:S(2)}) %copy-start) | copy-done | bytes 294936
  19.8 0.4 shard_map.47
  20.2 0.1 collective-permute-start.10
  20.3 0.9 %collective-permute-start.8 = (f32[192,256]{1,0:T(8,128)S(1)}, f32[192,256]{1,0:T(8,128)S(1)}, u32[]{:S(2)}, u32[]{:S(2)}) collective-permute-start(f32[192,256]{1,0:T(8,128)S(1)} %slice.9), channel_id=1, source_target_pairs={{0,24},{4,28},{8,16},{12,20},{16,8},{20,12},{24,0},{28,4},{1,25},{... | collective-permute-start | bytes 589832 | tf_op jit(solution)/shard_map/ppermute | solution.py:40
  21.2 9.8 %collective-permute-done.8 = f32[192,256]{1,0:T(8,128)S(1)} collective-permute-done((f32[192,256]{1,0:T(8,128)S(1)}, f32[192,256]{1,0:T(8,128)S(1)}, u32[]{:S(2)}, u32[]{:S(2)}) %collective-permute-start.8) | collective-permute-done | bytes 196640 | tf_op jit(solution)/shard_map/ppermute | solution.py:40
  31.0 0.0 collective-permute-start.11
  31.0 0.0 collective-permute-done.6
  31.0 0.1 collective-permute-done.7
  31.2 0.1 pad_maximum_fusion.refs_2_.refs_4_
  31.3 0.4 collective-permute-start.12
  31.7 1.5 %collective-permute-start.16 = (f32[256,384]{1,0:T(8,128)S(1)}, f32[256,384]{1,0:T(8,128)S(1)}, u32[]{:S(2)}, u32[]{:S(2)}) collective-permute-start(f32[256,384]{1,0:T(8,128)S(1)} %add.3.sides), channel_id=1, source_target_pairs={{0,8},{4,12},{8,0},{12,4},{16,24},{20,28},{24,16},{28,20},{1,9},{5... | collective-permute-start | bytes 1179656 | tf_op jit(solution)/shard_map/ppermute | solution.py:40
  33.2 1.0 %shard_map.48 = (f32[256,512]{1,0:T(8,128)S(1)}, f32[192,256]{1,0:T(8,128)S(1)}) custom-call(f32[384,256]{1,0:T(8,128)S(1)} %constant_dynamic-update-slice_fusion.refs_0_, f32[960,256]{1,0:T(8,128)S(1)} %get-tuple-element.24.near.refs_1_.refs_2_, f32[960,256]{1,0:T(8,128)S(1)} %pad_maximum_fusion.refs_2_.refs_4_, f32[192,384]{1,0:T(8,128)S(1)} %copy-done), custom_call_target="tpu_custom_call" | custom-call | flops 603979776 | bytes 2359296 | tf_op jit(solution)/shard_map/pallas_call | solution.py:311
  34.2 0.8 %collective-permute-done.12.refs_5_ = f32[960,256]{1,0:T(8,128)S(1)} collective-permute-done((f32[960,256]{1,0:T(8,128)S(1)}, f32[960,256]{1,0:T(8,128)S(1)}, u32[]{:S(2)}, u32[]{:S(2)}) %collective-permute-start.12) | collective-permute-done | bytes 983072 | tf_op jit(solution)/shard_map/ppermute | solution.py:40
  35.0 3.3 %shard_map.49 = (f32[192,768]{1,0:T(8,128)S(1)}, f32[192,384]{1,0:T(8,128)S(1)}, f32[192,384]{1,0:T(8,128)S(1)}, f32[192,384]{1,0:T(8,128)S(1)}) custom-call(f32[384,256]{1,0:T(8,128)S(1)} %constant_dynamic-update-slice_fusion.refs_0_, f32[384,256]{1,0:T(8,128)S(1)} %collective-permute-done.9.refs_1_, f32[960,256]{1,0:T(8,128)S(1)} %get-tuple-element.24.near.refs_1_.refs_2_, ...), custom_call_target="tpu_custom_call" | custom-call | flops 1962934272 | bytes 4718592 | tf_op jit(solution)/shard_map/pallas_call | solution.py:311
  38.3 0.1 collective-permute-start.15
  38.4 0.7 %collective-permute-start.13 = (f32[192,384]{1,0:T(8,128)S(1)}, f32[192,384]{1,0:T(8,128)S(1)}, u32[]{:S(2)}, u32[]{:S(2)}) collective-permute-start(f32[192,384]{1,0:T(8,128)S(1)} %get-tuple-element.29.other), channel_id=1, source_target_pairs={{1,2},{2,1},{5,6},{6,5},{9,10},{10,9},{13,14},{14,13},{17,18},{18,... | collective-permute-start | bytes 884744 | tf_op jit(solution)/shard_map/ppermute | solution.py:400
  39.1 6.6 %collective-permute-start.14 = (f32[192,384]{1,0:T(8,128)S(1)}, f32[192,384]{1,0:T(8,128)S(1)}, u32[]{:S(2)}, u32[]{:S(2)}) collective-permute-start(f32[192,384]{1,0:T(8,128)S(1)} %get-tuple-element.30.across), channel_id=1, source_target_pairs={{0,2},{3,1},{4,6},{7,5},{8,10},{11,9},{12,14},{15,13},{16,18},{19,... | collective-permute-start | bytes 884744 | tf_op jit(solution)/shard_map/ppermute | solution.py:401
  45.7 1.7 %collective-permute-done.15.passed = f32[192,384]{1,0:T(8,128)S(1)} collective-permute-done((f32[192,384]{1,0:T(8,128)S(1)}, f32[192,384]{1,0:T(8,128)S(1)}, u32[]{:S(2)}, u32[]{:S(2)}) %collective-permute-start.15) | collective-permute-done | bytes 294944 | tf_op jit(solution)/shard_map/ppermute | solution.py:40
  47.4 0.1 shard_map.52
  47.5 0.3 collective-permute-start.19
  47.8 0.6 collective-permute-start.18
  48.5 1.5 %collective-permute-start.17 = (f32[128,384]{1,0:T(8,128)S(1)}, f32[128,384]{1,0:T(8,128)S(1)}, u32[]{:S(2)}, u32[]{:S(2)}) collective-permute-start(f32[128,384]{1,0:T(8,128)S(1)} %get-tuple-element.40), channel_id=1, source_target_pairs={{0,16},{4,20},{8,24},{12,28},{16,0},{20,4},{24,8},{28,12},{1,17},{... | collective-permute-start | bytes 589832 | tf_op jit(solution)/shard_map/ppermute | solution.py:40
  49.9 1.6 %shard_map.50.refs_2_ = f32[192,384]{1,0:T(8,128)S(1)} custom-call(f32[384,256]{1,0:T(8,128)S(1)} %constant_dynamic-update-slice_fusion.refs_0_, f32[384,256]{1,0:T(8,128)S(1)} %collective-permute-done.9.refs_1_, f32[960,256]{1,0:T(8,128)S(1)} %get-tuple-element.24.near.refs_1_.refs_2_, f32[960,256]{1,0:T(8,128)S(1)} %collective-permute-done.11.refs_3_, ...), custom_call_target="tpu_custom_call" | custom-call | flops 339738624 | bytes 4718592 | tf_op jit(solution)/shard_map/pallas_call | solution.py:311
  51.6 1.5 %collective-permute-done.14.refs_1_ = f32[192,384]{1,0:T(8,128)S(1)} collective-permute-done((f32[192,384]{1,0:T(8,128)S(1)}, f32[192,384]{1,0:T(8,128)S(1)}, u32[]{:S(2)}, u32[]{:S(2)}) %collective-permute-start.14) | collective-permute-done | bytes 294944 | tf_op jit(solution)/shard_map/ppermute | solution.py:401
  53.1 0.1 shard_map.51.summed
  53.2 2.6 %collective-permute-done.18.refs_1_ = f32[128,384]{1,0:T(8,128)S(1)} collective-permute-done((f32[128,384]{1,0:T(8,128)S(1)}, f32[128,384]{1,0:T(8,128)S(1)}, u32[]{:S(2)}, u32[]{:S(2)}) %collective-permute-start.18) | collective-permute-done | bytes 196640 | tf_op jit(solution)/shard_map/ppermute | solution.py:40
  55.8 2.5 %collective-permute-done.17.refs_0_ = f32[128,384]{1,0:T(8,128)S(1)} collective-permute-done((f32[128,384]{1,0:T(8,128)S(1)}, f32[128,384]{1,0:T(8,128)S(1)}, u32[]{:S(2)}, u32[]{:S(2)}) %collective-permute-start.17) | collective-permute-done | bytes 196640 | tf_op jit(solution)/shard_map/ppermute | solution.py:40
  58.3 0.3 shard_map.53.summed
  58.6 4.5 %collective-permute-done.19.late = f32[192,384]{1,0:T(8,128)S(1)} collective-permute-done((f32[192,384]{1,0:T(8,128)S(1)}, f32[192,384]{1,0:T(8,128)S(1)}, u32[]{:S(2)}, u32[]{:S(2)}) %collective-permute-start.19) | collective-permute-done | bytes 294944 | tf_op jit(solution)/shard_map/ppermute | solution.py:407
  63.1 0.8 %shard_map.54 = f32[192,384]{1,0:T(8,128)} custom-call(f32[192,384]{1,0:T(8,128)S(1)} %shard_map.53.summed, f32[192,384]{1,0:T(8,128)S(1)} %collective-permute-done.19.late, f32[192,384]{1,0:T(8,128)S(1)} %collective-permute-done.15.passed), custom_call_target="tpu_custom_call" | custom-call | flops 147456 | bytes 1179648 | tf_op jit(solution)/shard_map/pallas_call | solution.py:311
  (14 shorter events, 0.1 us)
Async XLA Ops:
  0.0 7.1 %collective-permute-start.4 = (f32[64,192]{1,0:T(8,128)}, f32[64,192]{1,0:T(8,128)S(1)}, u32[]{:S(2)}, u32[]{:S(2)}) collective-permute-start(f32[64,192]{1,0:T(8,128)} %bitcast.1), channel_id=1, source_target_pairs={{0,1},{1,0},{2,3},{3,2},{4,5},{5,4},{6,7},{7,6},{8,9},{9,8},{10,11... | collective-permute-start | bytes 147464 | tf_op jit(solution)/shard_map/ppermute | solution.py:40
  3.0 12.5 %collective-permute-start.2 = (f32[192,256]{1,0:T(8,128)}, f32[192,256]{1,0:T(8,128)S(1)}, u32[]{:S(2)}, u32[]{:S(2)}) collective-permute-start(f32[192,256]{1,0:T(8,128)} %param.5), channel_id=1, source_target_pairs={{0,16},{4,20},{8,24},{12,28},{16,0},{20,4},{24,8},{28,12},{1,17},{... | collective-permute-start | bytes 589832 | tf_op jit(solution)/shard_map/ppermute | solution.py:40
  4.5 11.0 %collective-permute-start = (f32[192,256]{1,0:T(8,128)}, f32[192,256]{1,0:T(8,128)S(1)}, u32[]{:S(2)}, u32[]{:S(2)}) collective-permute-start(f32[192,256]{1,0:T(8,128)} %param.5), channel_id=1, source_target_pairs={{0,8},{4,12},{8,0},{12,4},{16,24},{20,28},{24,16},{28,20},{1,9},{5... | collective-permute-start | bytes 589832 | tf_op jit(solution)/shard_map/ppermute | solution.py:40
  6.0 9.5 %collective-permute-start.3 = (f32[192,256]{1,0:T(8,128)}, f32[192,256]{1,0:T(8,128)S(1)}, u32[]{:S(2)}, u32[]{:S(2)}) collective-permute-start(f32[192,256]{1,0:T(8,128)} %param.6), channel_id=1, source_target_pairs={{0,16},{4,20},{8,24},{12,28},{16,0},{20,4},{24,8},{28,12},{1,17},{... | collective-permute-start | bytes 589832 | tf_op jit(solution)/shard_map/ppermute | solution.py:40
  6.5 9.0 %collective-permute-start.1 = (f32[192,256]{1,0:T(8,128)}, f32[192,256]{1,0:T(8,128)S(1)}, u32[]{:S(2)}, u32[]{:S(2)}) collective-permute-start(f32[192,256]{1,0:T(8,128)} %param.6), channel_id=1, source_target_pairs={{0,8},{4,12},{8,0},{12,4},{16,24},{20,28},{24,16},{28,20},{1,9},{5... | collective-permute-start | bytes 589832 | tf_op jit(solution)/shard_map/ppermute | solution.py:40
  7.9 10.9 %copy-start.1 = (f32[192,256]{1,0:T(8,128)S(1)}, f32[192,256]{1,0:T(8,128)}, u32[]{:S(2)}) copy-start(f32[192,256]{1,0:T(8,128)} %param.5) | copy-start | bytes 589828
  7.9 7.6 %collective-permute-start.5 = (f32[128,192]{1,0:T(8,128)S(1)}, f32[128,192]{1,0:T(8,128)S(1)}, u32[]{:S(2)}, u32[]{:S(2)}) collective-permute-start(f32[128,192]{1,0:T(8,128)S(1)} %pad_maximum_fusion.1.refs_0_), channel_id=1, source_target_pairs={{0,2},{1,3},{2,0},{3,1},{4,6},{5,7},{6,4},{7,5},{8,10},{9,11},{10,... | collective-permute-start | bytes 294920 | tf_op jit(solution)/shard_map/ppermute | solution.py:40
  15.7 15.3 %collective-permute-start.6 = (f32[384,256]{1,0:T(8,128)S(1)}, f32[384,256]{1,0:T(8,128)S(1)}, u32[]{:S(2)}, u32[]{:S(2)}) collective-permute-start(f32[384,256]{1,0:T(8,128)S(1)} %get-tuple-element.22), channel_id=1, source_target_pairs={{0,8},{4,12},{8,0},{12,4},{16,24},{20,28},{24,16},{28,20},{1,9},{5... | collective-permute-start | bytes 1179656 | tf_op jit(solution)/shard_map/ppermute | solution.py:40
  17.3 1.5 %copy-start.2 = (f32[192,256]{1,0:T(8,128)S(1)}, f32[192,256]{1,0:T(8,128)}, u32[]{:S(2)}) copy-start(f32[192,256]{1,0:T(8,128)} %param.6) | copy-start | bytes 589828
  17.3 13.9 %collective-permute-start.7 = (f32[384,256]{1,0:T(8,128)S(1)}, f32[384,256]{1,0:T(8,128)S(1)}, u32[]{:S(2)}, u32[]{:S(2)}) collective-permute-start(f32[384,256]{1,0:T(8,128)S(1)} %get-tuple-element.23), channel_id=1, source_target_pairs={{0,16},{4,20},{8,24},{12,28},{16,0},{20,4},{24,8},{28,12},{1,17},{... | collective-permute-start | bytes 1179656 | tf_op jit(solution)/shard_map/ppermute | solution.py:40
  18.8 1.0 %copy-start = (f32[192,384]{1,0:T(8,128)S(1)}, f32[192,384]{1,0:T(8,128)}, u32[]{:S(2)}) copy-start(f32[192,384]{1,0:T(8,128)} %refs_7_.1) | copy-start | bytes 884740
  18.9 12.4 %collective-permute-start.9 = (f32[384,256]{1,0:T(8,128)S(1)}, f32[384,256]{1,0:T(8,128)S(1)}, u32[]{:S(2)}, u32[]{:S(2)}) collective-permute-start(f32[384,256]{1,0:T(8,128)S(1)} %constant_dynamic-update-slice_fusion.refs_0_), channel_id=1, source_target_pairs={{0,4},{4,0},{8,12},{12,8},{16,20},{20,16},{24,28},{28,24},{1,5},{5... | collective-permute-start | bytes 1179656 | tf_op jit(solution)/shard_map/ppermute | solution.py:40
  20.2 11.1 %collective-permute-start.10 = (f32[256,384]{1,0:T(8,128)S(1)}, f32[256,384]{1,0:T(8,128)S(1)}, u32[]{:S(2)}, u32[]{:S(2)}) collective-permute-start(f32[256,384]{1,0:T(8,128)S(1)} %shard_map.47), channel_id=1, source_target_pairs={{0,4},{4,0},{8,12},{12,8},{16,20},{20,16},{24,28},{28,24},{1,5},{5... | collective-permute-start | bytes 1179656 | tf_op jit(solution)/shard_map/ppermute | solution.py:40
  20.3 10.7 %collective-permute-start.8 = (f32[192,256]{1,0:T(8,128)S(1)}, f32[192,256]{1,0:T(8,128)S(1)}, u32[]{:S(2)}, u32[]{:S(2)}) collective-permute-start(f32[192,256]{1,0:T(8,128)S(1)} %slice.9), channel_id=1, source_target_pairs={{0,24},{4,28},{8,16},{12,20},{16,8},{20,12},{24,0},{28,4},{1,25},{... | collective-permute-start | bytes 589832 | tf_op jit(solution)/shard_map/ppermute | solution.py:40
  31.0 3.2 %collective-permute-start.11 = (f32[960,256]{1,0:T(8,128)S(1)}, f32[960,256]{1,0:T(8,128)S(1)}, u32[]{:S(2)}, u32[]{:S(2)}) collective-permute-start(f32[960,256]{1,0:T(8,128)S(1)} %get-tuple-element.24.near.refs_1_.refs_2_), channel_id=1, source_target_pairs={{0,4},{4,0},{8,12},{12,8},{16,20},{20,16},{24,28},{28,24},{1,5},{5... | collective-permute-start | bytes 2949128 | tf_op jit(solution)/shard_map/ppermute | solution.py:40
  31.3 3.7 %collective-permute-start.12 = (f32[960,256]{1,0:T(8,128)S(1)}, f32[960,256]{1,0:T(8,128)S(1)}, u32[]{:S(2)}, u32[]{:S(2)}) collective-permute-start(f32[960,256]{1,0:T(8,128)S(1)} %pad_maximum_fusion.refs_2_.refs_4_), channel_id=1, source_target_pairs={{0,4},{4,0},{8,12},{12,8},{16,20},{20,16},{24,28},{28,24},{1,5},{5... | collective-permute-start | bytes 2949128 | tf_op jit(solution)/shard_map/ppermute | solution.py:40
  31.7 13.9 %collective-permute-start.16 = (f32[256,384]{1,0:T(8,128)S(1)}, f32[256,384]{1,0:T(8,128)S(1)}, u32[]{:S(2)}, u32[]{:S(2)}) collective-permute-start(f32[256,384]{1,0:T(8,128)S(1)} %add.3.sides), channel_id=1, source_target_pairs={{0,8},{4,12},{8,0},{12,4},{16,24},{20,28},{24,16},{28,20},{1,9},{5... | collective-permute-start | bytes 1179656 | tf_op jit(solution)/shard_map/ppermute | solution.py:40
  38.3 9.1 %collective-permute-start.15 = (f32[192,384]{1,0:T(8,128)S(1)}, f32[192,384]{1,0:T(8,128)S(1)}, u32[]{:S(2)}, u32[]{:S(2)}) collective-permute-start(f32[192,384]{1,0:T(8,128)S(1)} %get-tuple-element.32), channel_id=1, source_target_pairs={{0,1},{1,0},{2,3},{3,2},{4,5},{5,4},{6,7},{7,6},{8,9},{9,8},{10,11... | collective-permute-start | bytes 884744 | tf_op jit(solution)/shard_map/ppermute | solution.py:40
  38.4 13.2 %collective-permute-start.13 = (f32[192,384]{1,0:T(8,128)S(1)}, f32[192,384]{1,0:T(8,128)S(1)}, u32[]{:S(2)}, u32[]{:S(2)}) collective-permute-start(f32[192,384]{1,0:T(8,128)S(1)} %get-tuple-element.29.other), channel_id=1, source_target_pairs={{1,2},{2,1},{5,6},{6,5},{9,10},{10,9},{13,14},{14,13},{17,18},{18,... | collective-permute-start | bytes 884744 | tf_op jit(solution)/shard_map/ppermute | solution.py:400
  39.1 14.0 %collective-permute-start.14 = (f32[192,384]{1,0:T(8,128)S(1)}, f32[192,384]{1,0:T(8,128)S(1)}, u32[]{:S(2)}, u32[]{:S(2)}) collective-permute-start(f32[192,384]{1,0:T(8,128)S(1)} %get-tuple-element.30.across), channel_id=1, source_target_pairs={{0,2},{3,1},{4,6},{7,5},{8,10},{11,9},{12,14},{15,13},{16,18},{19,... | collective-permute-start | bytes 884744 | tf_op jit(solution)/shard_map/ppermute | solution.py:401
  47.5 15.6 %collective-permute-start.19 = (f32[192,384]{1,0:T(8,128)S(1)}, f32[192,384]{1,0:T(8,128)S(1)}, u32[]{:S(2)}, u32[]{:S(2)}) collective-permute-start(f32[192,384]{1,0:T(8,128)S(1)} %get-tuple-element.38), channel_id=1, source_target_pairs={{0,1},{3,2},{1,3},{2,0},{4,5},{7,6},{5,7},{6,4},{8,9},{11,10},{9,1... | collective-permute-start | bytes 884744 | tf_op jit(solution)/shard_map/ppermute | solution.py:407
  47.8 7.9 %collective-permute-start.18 = (f32[128,384]{1,0:T(8,128)S(1)}, f32[128,384]{1,0:T(8,128)S(1)}, u32[]{:S(2)}, u32[]{:S(2)}) collective-permute-start(f32[128,384]{1,0:T(8,128)S(1)} %get-tuple-element.39), channel_id=1, source_target_pairs={{0,16},{4,20},{8,24},{12,28},{16,0},{20,4},{24,8},{28,12},{1,17},{... | collective-permute-start | bytes 589832 | tf_op jit(solution)/shard_map/ppermute | solution.py:40
  48.5 9.8 %collective-permute-start.17 = (f32[128,384]{1,0:T(8,128)S(1)}, f32[128,384]{1,0:T(8,128)S(1)}, u32[]{:S(2)}, u32[]{:S(2)}) collective-permute-start(f32[128,384]{1,0:T(8,128)S(1)} %get-tuple-element.40), channel_id=1, source_target_pairs={{0,16},{4,20},{8,24},{12,28},{16,0},{20,4},{24,8},{28,12},{1,17},{... | collective-permute-start | bytes 589832 | tf_op jit(solution)/shard_map/ppermute | solution.py:40
